TPU v7x, 128 devices: a whole 4x4x4 slice. The times are simulated.
128 devices in a mesh: chan: 8 (over y, x_lo), blk: 16 (over x_hi, z, core).
Axes of the slice: x: 4 (x_hi: 2, x_lo: 2; x = x_hi * 2 + x_lo), y: 4, z: 4, core: 2. Of those that a mesh axis runs over, the one named last changes fastest.
Arguments:
- voltages: bfloat16 [2, 16, 64, 536576], P(None, 'blk', 'chan'), may hold values from -5.5 to 5.5
- fir_taps: float32 [4, 4096], replicated, may hold values from -3 to 3
- station_flags: int32 [512], replicated, may hold values 0 or 1
- bin_offsets: int32 [256], replicated, may hold values from 0 to 3
Outputs:
- visibilities: bfloat16 [256, 2, 1024, 1024], P('chan', None, 'blk')
All inputs are finite; a program needn't handle non-finite values.
Results may differ from a plain program's by a relative error of at most 0.0034.
Values may be sent and summed in bfloat16 or wider, within the bound.
No kernel may reach another device: no remote copies, remote signals or barrier semaphores. Data moves between devices by JAX's collectives and lax.ppermute only.
A program may use at most 256 MiB of HBM per device.

v0:
```python
import math

import jax
import jax.numpy as jnp
from jax import lax
from jax.sharding import PartitionSpec as P

NFFT = 4096
KEEP = 256
TAPS = 4
FRAMES = 128


def phase_table(length, kept):
    row_index = lax.broadcasted_iota(jnp.int32, (length, kept), 0)
    column_index = lax.broadcasted_iota(jnp.int32, (length, kept), 1)
    phases = row_index * column_index % length
    angles = phases.astype(jnp.float32) * (2.0 * math.pi / length)
    cosine = jnp.cos(angles)
    sine_part = jnp.sin(angles)
    upper = jnp.stack([cosine, -sine_part], axis=1)
    lower = jnp.stack([sine_part, cosine], axis=1)
    return jnp.stack([upper, lower])


def correlate(mine, others):
    rotated = jnp.stack([-others[1], others[0]])
    real_part = jnp.einsum("pcif,pcjf->cij", mine, others, preferred_element_type=jnp.float32)
    imag_part = jnp.einsum("pcif,pcjf->cij", mine, rotated, preferred_element_type=jnp.float32)
    return jnp.stack([real_part, imag_part], axis=1)


def on_device(voltages, fir_taps, station_flags, bin_offsets):
    inputs_here = voltages.shape[2]
    chan_total = lax.axis_size("chan")
    planes = voltages.reshape(2, inputs_here, FRAMES + TAPS - 1, NFFT)
    filtered = jnp.zeros((2, inputs_here, FRAMES, NFFT), jnp.float32)
    for tap_index in range(TAPS):
        filtered = (
            filtered
            + planes[:, :, tap_index : tap_index + FRAMES, :].astype(jnp.float32)
            * fir_taps[tap_index]
        )
    first_input = (
        lax.axis_index("blk") * (inputs_here * chan_total) + lax.axis_index("chan") * inputs_here
    )
    weights = lax.dynamic_slice_in_dim(
        jnp.repeat(station_flags, 2).astype(jnp.float32), first_input, inputs_here, 0
    )
    spectrum = jnp.einsum(
        "pifn,pnqk->qkif",
        filtered,
        phase_table(NFFT, KEEP),
        precision=lax.Precision.HIGHEST,
        preferred_element_type=jnp.float32,
    )
    spectra = (spectrum / math.sqrt(2.0 * NFFT) * weights[:, None]).astype(jnp.bfloat16)
    scales = jnp.exp2(-bin_offsets.astype(jnp.float32)) / FRAMES
    local = lax.all_to_all(spectra, "chan", split_axis=1, concat_axis=2, tiled=True)
    group_channels = local.shape[1]
    sums = correlate(local, lax.all_gather(local, "blk", axis=2, tiled=True))
    first_channel = lax.axis_index("chan") * group_channels
    factor = lax.dynamic_slice_in_dim(scales, first_channel, group_channels, 0)
    return (sums * factor[:, None, None, None]).astype(jnp.bfloat16)


def solution(mesh):
    in_specs = (P(None, "blk", "chan", None), P(), P(), P())
    out_specs = P("chan", None, "blk", None)
    return jax.shard_map(
        on_device, mesh=mesh, in_specs=in_specs, out_specs=out_specs, check_vma=False
    )
```

profile of v0, /device:TPU:1, one launch (start us, length us, event | category | flops | bytes accessed | tf_op | source)
XLA Modules:
  0.0 397.2 jit_solution(11936473295137632323)
XLA Ops:
  6.5 0.0 all-gather.2.cloned.1.call-start
  6.5 16.5 %fusion.40 = f32[4096,1,256]{0,2,1:T(8,128)} fusion(), kind=kLoop, calls=%fused_computation.48 | loop fusion | flops 15728640 | bytes 4194304 | tf_op jit(solution)/shard_map/neg | solution.py:21
  23.1 17.6 %fusion.38 = (f32[4096,1,256]{0,2,1:T(8,128)}, f32[4096,1,256]{0,2,1:T(8,128)}) fusion(), kind=kLoop, calls=%fused_computation.46 | loop fusion | flops 14680064 | bytes 8388608 | tf_op jit(solution)/shard_map/sin | solution.py:20
  40.6 0.0 copy-done.2
  40.7 0.0 copy-done.1
  40.7 0.1 broadcast_in_dim.4
  40.9 0.2 convert_element_type.58
  41.0 44.0 %fusion.45 = (bf16[2,8,128,4096]{3,1,2,0:T(8,128)(2,1)}, bf16[2,8,128,4096]{3,1,2,0:T(8,128)(2,1)}, bf16[2,8,128,4096]{3,1,2,0:T(8,128)(2,1)}, bf16[2,8,128,4096]{3,1,2,0:T(8,128)(2,1)}) fusion(bf16[2,8,131,4096]{3,1,2,0:T(8,128)(2,1)} %bitcast.53), kind=kLoop, calls=%fused_computation.54 | loop fusion | bytes 134217728 | tf_op jit(solution)/shard_map/slice | solution.py:41
  85.0 0.1 dynamic-slice_multiply_fusion
  85.1 13.3 %maximum_bitcast_fusion.2 = (f32[1,4096,2,256]{1,3,0,2:T(8,128)}, f32[1,4096,2,256]{1,3,0,2:T(8,128)}) fusion(f32[4096,1,256]{0,2,1:T(8,128)} %fusion.40, f32[4096,1,256]{0,2,1:T(8,128)} %get-tuple-element.18, f32[4096,1,256]{0,2,1:T(8,128)} %get-tuple-element.17), kind=kLoop, calls=%fused_computation.31 | loop fusion | flops 4194304 | bytes 29360128 | tf_op jit(solution)/shard_map/stack | solution.py:23
  98.5 3.0 copy-done
  101.4 100.0 %fusion.37 = bf16[2,256,8,128]{3,1,2,0:T(8,128)(2,1)S(1)} fusion(bf16[2,8,128,4096]{3,1,2,0:T(8,128)(2,1)} %get-tuple-element.8, bf16[2,8,128,4096]{3,1,2,0:T(8,128)(2,1)} %get-tuple-element.6, bf16[2,8,128,4096]{3,1,2,0:T(8,128)(2,1)} %get-tuple-element.7, bf16[2,8,128,4096]{3,1,2,0:T(8,128)(2,1)S(1)} %copy-done, f32[4096]{0:T(1024)S(1)} %bitcast.60, ...), kind=kOutput, calls=%fused_computation.45 | convolution fusion | flops 51637125120 | bytes 85000224 | tf_op jit(solution)/shard_map/pifn,pnqk->qkif/dot_general | solution.py:50
  201.4 0.7 copy.24
  202.1 20.7 %all_to_all.18 = bf16[2,256,8,128]{3,2,0,1:T(8,128)(2,1)S(1)} all-to-all(bf16[2,256,8,128]{3,2,0,1:T(8,128)(2,1)S(1)} %copy.24), channel_id=1, replica_groups=mesh['chan'=8,'blk'=16] {'chan'}, dimensions={1} | all-to-all | bytes 2097152 | tf_op jit(solution)/shard_map/all_to_all | solution.py:59
  222.8 1.3 copy.74
  224.0 0.0 all-gather.2.cloned.1.call-update
  224.1 0.0 copy-done.3
  224.1 0.1 dynamic_slice.7
  224.2 111.1 %all-gather.2.cloned.1.call-done = bf16[2,32,1024,128]{3,2,0,1:T(8,128)(2,1)} async-done(((bf16[2,32,64,128]{3,2,0,1:T(8,128)(2,1)}), bf16[2,32,1024,128]{3,2,0,1:T(8,128)(2,1)}) %all-gather.2.cloned.1.call-update) | async-done | bytes 16777232 | tf_op jit(solution)/shard_map/all_gather | solution.py:61
  335.2 11.7 %slice_negate_fusion = (bf16[1,32,1024,128]{3,2,0,1:T(8,128)(2,1)}, bf16[1,32,1024,128]{3,2,0,1:T(8,128)(2,1)}) fusion(bf16[2,32,1024,128]{3,2,0,1:T(8,128)(2,1)} %all-gather.2.cloned.1.call-done), kind=kLoop, calls=%fused_computation.30 | loop fusion | flops 4194304 | bytes 33554432 | tf_op jit(solution)/shard_map/neg | solution.py:27
  346.9 10.7 %fusion.34 = f32[32,1,64,1024]{3,2,0,1:T(8,128)} fusion(bf16[1,32,1024,128]{3,2,0,1:T(8,128)(2,1)} %get-tuple-element.10, bf16[1,32,1024,128]{3,2,0,1:T(8,128)(2,1)} %get-tuple-element.9, bf16[2,8,32,8,128]{4,3,0,2,1:T(8,128)(2,1)S(1)} %bitcast.55), kind=kOutput, calls=%fused_computation.43 | convolution fusion | flops 1082130432 | bytes 26214400 | tf_op jit(solution)/shard_map/pcif,pcjf->cij/dot_general | solution.py:29
  357.6 14.3 %convolution_bitcast_fusion = f32[32,1,64,1024]{3,2,0,1:T(8,128)} fusion(bf16[2,32,1024,128]{3,2,0,1:T(8,128)(2,1)} %all-gather.2.cloned.1.call-done, bf16[2,8,32,8,128]{4,3,0,2,1:T(8,128)(2,1)S(1)} %bitcast.56), kind=kOutput, calls=%fused_computation.42 | convolution fusion | flops 1073741824 | bytes 26214400 | tf_op jit(solution)/shard_map/pcif,pcjf->cij/dot_general | solution.py:28
  371.9 9.8 %fusion.19 = bf16[32,2,64,1024]{3,2,0,1:T(8,128)(2,1)} fusion(f32[32,1,64,1024]{3,2,0,1:T(8,128)} %fusion.34, f32[32,1,64,1024]{3,2,0,1:T(8,128)} %convolution_bitcast_fusion, f32[32]{0:T(128)S(1)} %dynamic_slice.7), kind=kLoop, calls=%fused_computation.21 | loop fusion | flops 12582912 | bytes 25165952 | tf_op jit(solution)/shard_map/convert_element_type | solution.py:64
  381.8 8.6 %copy.26 = bf16[32,2,64,1024]{3,2,1,0:T(8,128)(2,1)} copy(bf16[32,2,64,1024]{3,2,0,1:T(8,128)(2,1)} %fusion.19) | data formatting | bytes 16777216 | tf_op jit(solution)/shard_map/convert_element_type | solution.py:64
  (7 shorter events, 0.1 us)
Async XLA Ops:
  6.5 34.1 %copy-start.2 = (s32[512]{0:T(512)S(1)}, s32[512]{0:T(512)}, u32[]{:S(2)}) copy-start(s32[512]{0:T(512)} %param.6) | copy-start | bytes 6148
  6.5 34.1 %copy-start.1 = (f32[4,4096]{1,0:T(4,128)S(1)}, f32[4,4096]{1,0:T(4,128)}, u32[]{:S(2)}) copy-start(f32[4,4096]{1,0:T(4,128)} %param.5) | copy-start | bytes 196612
  6.5 328.7 %all-gather.2.cloned.1.call-start = ((), (), s32[]{:S(2)}) async-start(), calls=%async_computation.1 | async-start | bytes 17825792 | tf_op jit(solution)/shard_map/all_gather | solution.py:61
  85.1 16.3 %copy-start = (bf16[2,8,128,4096]{3,1,2,0:T(8,128)(2,1)S(1)}, bf16[2,8,128,4096]{3,1,2,0:T(8,128)(2,1)}, u32[]{:S(2)}) copy-start(bf16[2,8,128,4096]{3,1,2,0:T(8,128)(2,1)} %get-tuple-element.5) | copy-start | bytes 50331652
  101.4 122.6 %copy-start.3 = (s32[256]{0:T(256)S(1)}, s32[256]{0:T(256)}, u32[]{:S(2)}) copy-start(s32[256]{0:T(256)} %param.7) | copy-start | bytes 3076
Sparse Core Ops, SparseCore 0:
  224.2 110.9 all-gather.1
where the time goes:
time: 397 us
  matrix products  125 us (31%)
  waiting for transfers between devices  111 us (28%)
  other arithmetic  69 us (17%)
  local copies, waits for them, and re-layouts  57.9 us (15%)
  blocking collectives  20.7 us (5%)
  between operations  13.5 us (3%)
    all_gather x1, waiting for transfers between devices, on_device(): sums = correlate(local, lax.all_gather(local, 'blk', axis=2, tiled=True))  111 us
    dot_general x1, matrix products, on_device(): jnp.einsum('pifn,pnqk->qkif', filtered, phase_table(NFFT, KEEP), precisio...  100 us
    slice x1, local copies, waits for them, and re-layouts, on_device(): planes[:, :, tap_index:tap_index + FRAMES, :].astype(jnp.float32)  44 us
    all_to_all x1, blocking collectives, on_device(): lax.all_to_all(spectra, 'chan', split_axis=1, concat_axis=2, tiled=True)  20.7 us
    sin x1, other arithmetic, phase_table(): sine_part = jnp.sin(angles)  17.6 us
    neg x1, other arithmetic, phase_table(): upper = jnp.stack([cosine, -sine_part], axis=1)  16.5 us
    dot_general x1, matrix products, correlate(): jnp.einsum('pcif,pcjf->cij', mine, others, preferred_element_type=jnp.flo...  14.3 us
    another operation x1, other arithmetic, phase_table(): return jnp.stack([upper, lower])  13.3 us
  transfers between devices with their start and end apart: 1, of which 1 were waited for; matrix products, arithmetic and copies ran while one was open for 0% of the time, Pallas kernels for 0%

commit v1 on v0

v1 whole, which is shorter than its diff:
```python
import functools
import math

import jax
import jax.numpy as jnp
import ml_dtypes
import numpy as np
from jax import lax
from jax.experimental import pallas as pl
from jax.experimental.pallas import tpu as pltpu
from jax.sharding import PartitionSpec as P

NFFT = 4096
HALF = NFFT // 2
TAPS = 4
FRAMES = 128
CHUNK = 64
STEP = 32


def dft_tables():
    n = np.arange(HALF)[:, None]
    tables = []
    for cls in range(2):
        channel = 2 * np.arange(128)[None, :] + cls
        angle = 2.0 * np.pi * ((n * channel) % NFFT) / NFFT
        table = np.concatenate([np.cos(angle), np.sin(angle)], axis=1)
        high = table.astype(ml_dtypes.bfloat16)
        low = (table - high.astype(np.float64)).astype(ml_dtypes.bfloat16)
        tables.append(np.stack([high, low]))
    return np.stack(tables)


def spectra_kernel(first_frame, x_hbm, taps_ref, table_ref, weight_ref, out_ref, x_vmem, fold, sums, turned, sems):
    lanes = STEP * NFFT
    halo = (TAPS - 1) * NFFT
    copies = []
    for s in range(CHUNK // STEP):
        start = 0 if s == 0 else s * lanes + halo
        size = lanes + halo if s == 0 else lanes
        copies.append(
            pltpu.make_async_copy(
                x_hbm.at[:, 0, :, pl.ds(first_frame * NFFT + start, size)],
                x_vmem.at[:, :, pl.ds(start, size)],
                sems.at[s],
            )
        )
    for copy in copies:
        copy.start()
    rows = STEP * 8
    for s in range(CHUNK // STEP):
        copies[s].wait()

        def fir(t, carry):
            p = t // 16
            n0 = pl.multiple_of((t % 16) * 128, 128)

            def load(f, offset):
                lane = pl.multiple_of((s * STEP + f) * NFFT + offset + n0, 128)
                return x_vmem[p, :, pl.ds(lane, 128)].astype(jnp.float32)

            def tap(k, offset):
                return jnp.broadcast_to(taps_ref[k : k + 1, pl.ds(n0 + offset, 128)], (8, 128))

            taps = [[tap(k, offset) for k in range(TAPS)] for offset in (0, HALF)]
            window = [[load(f, offset) for f in range(TAPS - 1)] for offset in (0, HALF)]
            for pair in range(STEP // 2):
                even, odd = [], []
                for f in (2 * pair, 2 * pair + 1):
                    halves = []
                    for w, h, offset in zip(window, taps, (0, HALF)):
                        w.append(load(f + TAPS - 1, offset))
                        halves.append(((w[0] * h[0] + w[1] * h[1]) + w[2] * h[2]) + w[3] * h[3])
                        w.pop(0)
                    even.append(halves[0] + halves[1])
                    odd.append(halves[0] - halves[1])
                where = pl.ds(pl.multiple_of(p * rows, rows) + pair * 16, 16)
                for cls, both in enumerate((even, odd)):
                    value = jnp.concatenate(both, axis=0)
                    high = value.astype(jnp.bfloat16)
                    low = (value - high.astype(jnp.float32)).astype(jnp.bfloat16)
                    fold[cls, 0, where, pl.ds(n0, 128)] = high
                    fold[cls, 1, where, pl.ds(n0, 128)] = low
            return carry

        lax.fori_loop(0, 32, fir, 0)
        for cls in range(2):
            total = jnp.dot(fold[cls, 0], table_ref[cls, 0], preferred_element_type=jnp.float32)
            total += jnp.dot(fold[cls, 1], table_ref[cls, 0], preferred_element_type=jnp.float32)
            total += jnp.dot(fold[cls, 0], table_ref[cls, 1], preferred_element_type=jnp.float32)
            real = total[:rows, :128] + total[rows:, 128:]
            imag = total[rows:, :128] - total[:rows, 128:]
            weight = weight_ref[...]
            real = (real.reshape(STEP, 8, 128) * weight).reshape(rows, 128)
            imag = (imag.reshape(STEP, 8, 128) * weight).reshape(rows, 128)
            sums[cls, s * rows : (s + 1) * rows, :] = real
            sums[cls, CHUNK * 8 + s * rows : CHUNK * 8 + (s + 1) * rows, :] = imag
    for cls in range(2):
        for i in range(8):
            turned[cls, i * 128 : (i + 1) * 128, :] = sums[cls, pl.ds(i, 128, stride=8), :].T

    def emit(g, carry):
        for cls in range(2):
            for j in range(16):
                out_ref[g, cls, j] = turned[cls, pl.ds(g * 16 + j, 8, stride=128), :].astype(jnp.bfloat16)
        return carry

    lax.fori_loop(0, 8, emit, 0)


def spectra(first_frame, x, taps, tables, weight):
    return pl.pallas_call(
        functools.partial(spectra_kernel, first_frame),
        out_shape=jax.ShapeDtypeStruct((8, 2, 16, 8, 128), jnp.bfloat16),
        in_specs=[pl.BlockSpec(memory_space=pl.ANY)] + [pl.BlockSpec(memory_space=pltpu.VMEM)] * 3,
        out_specs=pl.BlockSpec(memory_space=pltpu.VMEM),
        scratch_shapes=[
            pltpu.VMEM((2, 8, (CHUNK + TAPS - 1) * NFFT), jnp.bfloat16),
            pltpu.VMEM((2, 2, 2 * STEP * 8, HALF), jnp.bfloat16),
            pltpu.VMEM((2, 2 * CHUNK * 8, 128), jnp.float32),
            pltpu.VMEM((2, 8 * 128, 128), jnp.float32),
            pltpu.SemaphoreType.DMA((CHUNK // STEP,)),
        ],
        compiler_params=pltpu.CompilerParams(vmem_limit_bytes=56 * 1024 * 1024),
        cost_estimate=pl.CostEstimate(flops=6_500_000_000, bytes_accessed=14_000_000, transcendentals=0),
        name="spectra",
    )(x, taps, tables, weight)


NJ = 2


def correlate_kernel(blk_ref, scale_ref, *refs):
    sources, (out_ref, held, sems) = refs[:32], refs[32:]
    step, steps = pl.program_id(0), pl.num_programs(0)
    blk = blk_ref[0]

    def copies(at):
        slot = at % 2
        made = []
        for m in range(16):
            row = pl.multiple_of((blk ^ m) * 64, 64)
            for part in range(2):
                made.append(
                    pltpu.make_async_copy(
                        sources[2 * m + part].at[:, pl.ds(at * NJ, NJ)],
                        held.at[slot, :, :, pl.ds(row, 64), pl.ds(part * 128, 128)],
                        sems.at[slot, 2 * m + part],
                    )
                )
        return made

    @pl.when(step == 0)
    def _():
        for copy in copies(step):
            copy.start()

    @pl.when(step + 1 < steps)
    def _():
        for copy in copies(step + 1):
            copy.start()

    for copy in copies(step):
        copy.wait()
    slot = step % 2
    own = pl.ds(pl.multiple_of(blk * 64, 64), 64)
    lane = lax.broadcasted_iota(jnp.int32, (64, 128), 1)
    sign = jnp.where(lane < 64, 1.0, -1.0)
    for cls in range(2):
        for jj in range(NJ):
            mine = held[slot, cls, jj, own, :]
            wide = mine.astype(jnp.float32)
            turned = [pltpu.roll(wide[:, h : h + 128], 64, 1) * sign for h in (0, 128)]
            left = jnp.concatenate([mine, jnp.concatenate(turned, axis=1).astype(jnp.bfloat16)], axis=0)
            total = lax.dot_general(
                left, held[slot, cls, jj], (((1,), (1,)), ((), ())), preferred_element_type=jnp.float32
            )
            channel = 2 * jj + cls
            total = (total * scale_ref[step * (2 * NJ) + channel]).astype(jnp.bfloat16)
            out_ref[channel, 0] = total[:64]
            out_ref[channel, 1] = total[64:]


def correlate(blk, scale, sources):
    return pl.pallas_call(
        correlate_kernel,
        out_shape=jax.ShapeDtypeStruct((32, 2, 64, 1024), jnp.bfloat16),
        grid=(16 // NJ,),
        in_specs=[pl.BlockSpec(memory_space=pltpu.SMEM)] * 2 + [pl.BlockSpec(memory_space=pltpu.HBM)] * 32,
        out_specs=pl.BlockSpec((2 * NJ, 2, 64, 1024), lambda s: (s, 0, 0, 0)),
        scratch_shapes=[
            pltpu.VMEM((2, 2, NJ, 1024, 256), jnp.bfloat16),
            pltpu.SemaphoreType.DMA((2, 32)),
        ],
        compiler_params=pltpu.CompilerParams(vmem_limit_bytes=56 * 1024 * 1024),
        cost_estimate=pl.CostEstimate(flops=2_200_000_000, bytes_accessed=25_000_000, transcendentals=0),
        name="correlate",
    )(blk, scale, *sources)


def send(array, bits):
    return lax.ppermute(array, "blk", [(b, b ^ bits) for b in range(16)])


X2, Z1, Z3, CORE = 8, 2, 6, 1


def turn(chunk):
    got = lax.all_to_all(chunk, "chan", split_axis=0, concat_axis=0, tiled=True)
    return got.transpose(1, 2, 0, 3, 4).reshape(2, 16, 64, 128)


def on_device(voltages, fir_taps, station_flags, bin_offsets):
    chan, blk = lax.axis_index("chan"), lax.axis_index("blk")
    flags = jnp.repeat(station_flags, 2).astype(jnp.float32)
    weight = lax.dynamic_slice_in_dim(flags, blk * 64 + chan * 8, 8, 0) / math.sqrt(2.0 * NFFT)
    weight = jnp.broadcast_to(weight[:, None], (8, 128))
    scales = jnp.exp2(-bin_offsets.astype(jnp.float32)) / FRAMES
    scale = lax.dynamic_slice_in_dim(scales, chan * 32, 32, 0)
    tables = jnp.asarray(dft_tables())

    first = turn(spectra(0, voltages, fir_taps, tables, weight))
    second = turn(spectra(CHUNK, voltages, fir_taps, tables, weight))
    one = {0: first}
    one[Z1] = send(first, Z1)
    one[Z3] = send(first, Z3)
    one[X2] = send(first, X2)
    one[Z1 ^ Z3] = send(one[Z3], Z1)
    one[X2 ^ Z1] = send(one[Z1], X2)
    one[X2 ^ Z3] = send(one[Z3], X2)
    one[X2 ^ Z1 ^ Z3] = send(one[Z1 ^ Z3], X2)
    two = {0: second}
    two[X2] = send(second, X2)
    for m in (0, X2):
        two[m ^ Z1] = send(two[m], Z1)
        two[m ^ Z3] = send(two[m], Z3)
    two[Z1 ^ Z3] = send(two[Z1], Z3)
    two[X2 ^ Z1 ^ Z3] = send(two[X2 ^ Z3], Z1)
    for part in (one, two):
        for m in list(part):
            part[m ^ CORE] = send(part[m], CORE)
    sources = []
    for m in range(16):
        sources += [one[m], two[m]]
    return correlate(blk.astype(jnp.int32).reshape(1), scale, sources)


def solution(mesh):
    in_specs = (P(None, "blk", "chan", None), P(), P(), P())
    out_specs = P("chan", None, "blk", None)
    return jax.shard_map(
        on_device, mesh=mesh, in_specs=in_specs, out_specs=out_specs, check_vma=False
    )
```

time: 397 us -> 168 us (0.42)
  matrix products: 125 us -> 0 us
  waiting for transfers between devices: 111 us -> 42.2 us
  other arithmetic: 69 us -> 0.77 us
  Pallas kernels: 0 us -> 63.2 us
  starting transfers between devices: 0.01 us -> 58.6 us
  local copies, waits for them, and re-layouts: 57.9 us -> 1.97 us
  blocking collectives: 20.7 us -> 0 us
  between operations: 13.5 us -> 0.44 us
    dot_general x3 -> x0, matrix products: 125 us -> none  [the longest x1 100 us: on_device(): jnp.einsum('pifn,pnqk->qkif', filtered, phase_table(NFFT, KEEP), precisio...]
    all_gather x1 -> x0, waiting for transfers between devices: 111 us -> none  [on_device(): sums = correlate(local, lax.all_gather(local, 'blk', axis=2, tiled=True))]
    pallas_call x0 -> x3, Pallas kernels: none -> 63.2 us  [the longest x2 48.9 us: spectra(): pl.pallas_call(functools.partial(spectra_kernel, first_frame), out_shape=...]
    ppermute x0 -> x30, starting transfers between devices: none -> 47.5 us  [send(): return lax.ppermute(array, 'blk', [(b, b ^ bits) for b in range(16)])]
    slice x2 -> x0, local copies, waits for them, and re-layouts: 44.1 us -> none  [the longest x1 44 us: on_device(): planes[:, :, tap_index:tap_index + FRAMES, :].astype(jnp.float32)]
    ppermute x0 -> x30, waiting for transfers between devices: none -> 42.1 us  [send(): return lax.ppermute(array, 'blk', [(b, b ^ bits) for b in range(16)])]
    neg x2 -> x0, other arithmetic: 28.2 us -> none  [the longest x1 16.5 us: phase_table(): upper = jnp.stack([cosine, -sine_part], axis=1)]
    all_to_all x1 -> x0, blocking collectives: 20.7 us -> none  [on_device(): lax.all_to_all(spectra, 'chan', split_axis=1, concat_axis=2, tiled=True)]
  transfers between devices with their start and end apart: 1 -> 32, of which waited for: 1 -> 11; matrix products, arithmetic and copies ran while one was open for 0% -> 1% of each run, Pallas kernels for 0% -> 15%
where the time goes in v1:
time: 168 us; the launch traced here: 167 us
  Pallas kernels  63.2 us (38%)
  starting transfers between devices  58.6 us (35%)
  waiting for transfers between devices  42.2 us (25%)
  local copies, waits for them, and re-layouts  1.97 us (1%)
    pallas_call x2, Pallas kernels, spectra(): pl.pallas_call(functools.partial(spectra_kernel, first_frame), out_shape=...  48.9 us
    ppermute x30, starting transfers between devices, send(): return lax.ppermute(array, 'blk', [(b, b ^ bits) for b in range(16)])  47.5 us
    ppermute x30, waiting for transfers between devices, send(): return lax.ppermute(array, 'blk', [(b, b ^ bits) for b in range(16)])  42.1 us
    pallas_call x1, Pallas kernels, correlate(): pl.pallas_call(correlate_kernel, out_shape=jax.ShapeDtypeStruct((32, 2, 6...  14.2 us
    all_to_all x2, starting transfers between devices, turn(): got = lax.all_to_all(chunk, 'chan', split_axis=0, concat_axis=0, tiled=True)  11.1 us
  transfers between devices with their start and end apart: 32, of which 11 were waited for; matrix products, arithmetic and copies ran while one was open for 1% of the time, Pallas kernels for 15%

profile of v1, /device:TPU:1, one launch (start us, length us, event | category | flops | bytes accessed | tf_op | source)
XLA Modules:
  0.0 167.1 jit_solution(10422856909100334756)
XLA Ops:
  1.7 24.4 %spectra.2 = bf16[8,2,16,8,128]{4,3,2,1,0:T(8,128)(2,1)} custom-call(bf16[2,1,8,536576]{3,2,1,0:T(8,128)(2,1)} %x_hbm.3, f32[4,4096]{1,0:T(4,128)} %taps_ref.3, bf16[2,2,2048,256]{3,2,1,0:T(8,128)(2,1)} %constant.31.clone.table_ref, f32[8,128]{1,0:T(8,128)} %broadcast_in_dim.10.weight_ref), custom_call_target="tpu_custom_call" | custom-call | flops 6499999744 | bytes 14000000 | tf_op jit(solution)/shard_map/spectra/pallas_call | solution.py:112
  26.2 6.0 %all-to-all-start = ((bf16[8,2,16,8,128]{4,3,2,1,0:T(8,128)(2,1)}), bf16[8,2,16,8,128]{4,3,2,1,0:T(8,128)(2,1)S(1)}, u32[]{:S(2)}, u32[]{:S(2)}) async-start(bf16[8,2,16,8,128]{4,3,2,1,0:T(8,128)(2,1)} %spectra.2), calls=%async_computation | async-start | bytes 1048576 | tf_op jit(solution)/shard_map/all_to_all | solution.py:209
  32.1 24.5 %spectra.3 = bf16[8,2,16,8,128]{4,3,2,1,0:T(8,128)(2,1)} custom-call(bf16[2,1,8,536576]{3,2,1,0:T(8,128)(2,1)} %x_hbm.3, f32[4,4096]{1,0:T(4,128)} %taps_ref.3, bf16[2,2,2048,256]{3,2,1,0:T(8,128)(2,1)} %constant.31.clone.table_ref, f32[8,128]{1,0:T(8,128)} %broadcast_in_dim.10.weight_ref), custom_call_target="tpu_custom_call" | custom-call | flops 6499999744 | bytes 14000000 | tf_op jit(solution)/shard_map/spectra/pallas_call | solution.py:112
  56.6 5.2 %all-to-all-start.1 = ((bf16[8,2,16,8,128]{4,3,2,1,0:T(8,128)(2,1)}), bf16[8,2,16,8,128]{4,3,2,1,0:T(8,128)(2,1)S(1)}, u32[]{:S(2)}, u32[]{:S(2)}) async-start(bf16[8,2,16,8,128]{4,3,2,1,0:T(8,128)(2,1)} %spectra.3), calls=%async_computation.1 | async-start | bytes 1048576 | tf_op jit(solution)/shard_map/all_to_all | solution.py:209
  61.9 2.5 %collective-permute-start.14 = (bf16[2,16,64,128]{3,2,1,0:T(8,128)(2,1)S(1)}, bf16[2,16,64,128]{3,2,1,0:T(8,128)(2,1)S(1)}, u32[]{:S(2)}, u32[]{:S(2)}) collective-permute-start(bf16[2,16,64,128]{3,2,1,0:T(8,128)(2,1)S(1)} %copy_bitcast_fusion.1.refs_0_), channel_id=1, source_target_pairs={{0,8},{1,9},{2,10},{3,11},{4,12},{5,13},{6,14},{7,15},{8,0},{9,1},... | collective-permute-start | bytes 1572872 | tf_op jit(solution)/shard_map/ppermute | solution.py:202
  64.5 3.8 %collective-permute-start.6 = (bf16[2,16,64,128]{3,2,1,0:T(8,128)(2,1)S(1)}, bf16[2,16,64,128]{3,2,1,0:T(8,128)(2,1)S(1)}, u32[]{:S(2)}, u32[]{:S(2)}) collective-permute-start(bf16[2,16,64,128]{3,2,1,0:T(8,128)(2,1)S(1)} %copy_bitcast_fusion.1.refs_0_), channel_id=1, source_target_pairs={{0,6},{1,7},{2,4},{3,5},{4,2},{5,3},{6,0},{7,1},{8,14},{9,15},{10,... | collective-permute-start | bytes 1572872 | tf_op jit(solution)/shard_map/ppermute | solution.py:202
  68.2 2.1 %collective-permute-start = (bf16[2,16,64,128]{3,2,1,0:T(8,128)(2,1)S(1)}, bf16[2,16,64,128]{3,2,1,0:T(8,128)(2,1)}, u32[]{:S(2)}, u32[]{:S(2)}) collective-permute-start(bf16[2,16,64,128]{3,2,1,0:T(8,128)(2,1)S(1)} %copy_bitcast_fusion.1.refs_0_), channel_id=1, source_target_pairs={{0,1},{1,0},{2,3},{3,2},{4,5},{5,4},{6,7},{7,6},{8,9},{9,8},{10,11... | collective-permute-start | bytes 1572872 | tf_op jit(solution)/shard_map/ppermute | solution.py:202
  70.5 2.5 %collective-permute-start.15 = (bf16[2,16,64,128]{3,2,1,0:T(8,128)(2,1)S(1)}, bf16[2,16,64,128]{3,2,1,0:T(8,128)(2,1)S(1)}, u32[]{:S(2)}, u32[]{:S(2)}) collective-permute-start(bf16[2,16,64,128]{3,2,1,0:T(8,128)(2,1)S(1)} %copy_bitcast_fusion.refs_1_), channel_id=1, source_target_pairs={{0,8},{1,9},{2,10},{3,11},{4,12},{5,13},{6,14},{7,15},{8,0},{9,1},... | collective-permute-start | bytes 1572872 | tf_op jit(solution)/shard_map/ppermute | solution.py:202
  73.1 7.8 %collective-permute-done.14.refs_16_ = bf16[2,16,64,128]{3,2,1,0:T(8,128)(2,1)S(1)} collective-permute-done((bf16[2,16,64,128]{3,2,1,0:T(8,128)(2,1)S(1)}, bf16[2,16,64,128]{3,2,1,0:T(8,128)(2,1)S(1)}, u32[]{:S(2)}, u32[]{:S(2)}) %collective-permute-start.14) | collective-permute-done | bytes 524320 | tf_op jit(solution)/shard_map/ppermute | solution.py:202
  80.8 3.8 %collective-permute-start.11 = (bf16[2,16,64,128]{3,2,1,0:T(8,128)(2,1)S(1)}, bf16[2,16,64,128]{3,2,1,0:T(8,128)(2,1)S(1)}, u32[]{:S(2)}, u32[]{:S(2)}) collective-permute-start(bf16[2,16,64,128]{3,2,1,0:T(8,128)(2,1)S(1)} %copy_bitcast_fusion.refs_1_), channel_id=1, source_target_pairs={{0,6},{1,7},{2,4},{3,5},{4,2},{5,3},{6,0},{7,1},{8,14},{9,15},{10,... | collective-permute-start | bytes 1572872 | tf_op jit(solution)/shard_map/ppermute | solution.py:202
  84.6 4.2 %collective-permute-start.1 = (bf16[2,16,64,128]{3,2,1,0:T(8,128)(2,1)S(1)}, bf16[2,16,64,128]{3,2,1,0:T(8,128)(2,1)S(1)}, u32[]{:S(2)}, u32[]{:S(2)}) collective-permute-start(bf16[2,16,64,128]{3,2,1,0:T(8,128)(2,1)S(1)} %copy_bitcast_fusion.refs_1_), channel_id=1, source_target_pairs={{0,1},{1,0},{2,3},{3,2},{4,5},{5,4},{6,7},{7,6},{8,9},{9,8},{10,11... | collective-permute-start | bytes 1572872 | tf_op jit(solution)/shard_map/ppermute | solution.py:202
  89.0 3.1 %collective-permute-done.15.refs_17_ = bf16[2,16,64,128]{3,2,1,0:T(8,128)(2,1)S(1)} collective-permute-done((bf16[2,16,64,128]{3,2,1,0:T(8,128)(2,1)S(1)}, bf16[2,16,64,128]{3,2,1,0:T(8,128)(2,1)S(1)}, u32[]{:S(2)}, u32[]{:S(2)}) %collective-permute-start.15) | collective-permute-done | bytes 524320 | tf_op jit(solution)/shard_map/ppermute | solution.py:202
  93.0 4.5 %collective-permute-start.12 = (bf16[2,16,64,128]{3,2,1,0:T(8,128)(2,1)S(1)}, bf16[2,16,64,128]{3,2,1,0:T(8,128)(2,1)S(1)}, u32[]{:S(2)}, u32[]{:S(2)}) collective-permute-start(bf16[2,16,64,128]{3,2,1,0:T(8,128)(2,1)S(1)} %collective-permute-done.6.refs_12_), channel_id=1, source_target_pairs={{0,1},{1,0},{2,3},{3,2},{4,5},{5,4},{6,7},{7,6},{8,9},{9,8},{10,11... | collective-permute-start | bytes 1572872 | tf_op jit(solution)/shard_map/ppermute | solution.py:202
  97.5 1.6 collective-permute-start.18
  100.0 4.8 %collective-permute-done.27.refs_28_ = bf16[2,16,64,128]{3,2,1,0:T(8,128)(2,1)S(1)} collective-permute-done((bf16[2,16,64,128]{3,2,1,0:T(8,128)(2,1)S(1)}, bf16[2,16,64,128]{3,2,1,0:T(8,128)(2,1)S(1)}, u32[]{:S(2)}, u32[]{:S(2)}) %collective-permute-start.27) | collective-permute-done | bytes 524320 | tf_op jit(solution)/shard_map/ppermute | solution.py:202
  104.9 3.8 %collective-permute-start.23 = (bf16[2,16,64,128]{3,2,1,0:T(8,128)(2,1)S(1)}, bf16[2,16,64,128]{3,2,1,0:T(8,128)(2,1)}, u32[]{:S(2)}, u32[]{:S(2)}) collective-permute-start(bf16[2,16,64,128]{3,2,1,0:T(8,128)(2,1)S(1)} %collective-permute-done.15.refs_17_), channel_id=1, source_target_pairs={{0,6},{1,7},{2,4},{3,5},{4,2},{5,3},{6,0},{7,1},{8,14},{9,15},{10,... | collective-permute-start | bytes 1572872 | tf_op jit(solution)/shard_map/ppermute | solution.py:202
  109.5 5.3 %collective-permute-start.17 = (bf16[2,16,64,128]{3,2,1,0:T(8,128)(2,1)S(1)}, bf16[2,16,64,128]{3,2,1,0:T(8,128)(2,1)S(1)}, u32[]{:S(2)}, u32[]{:S(2)}) collective-permute-start(bf16[2,16,64,128]{3,2,1,0:T(8,128)(2,1)S(1)} %collective-permute-done.15.refs_17_), channel_id=1, source_target_pairs={{0,1},{1,0},{2,3},{3,2},{4,5},{5,4},{6,7},{7,6},{8,9},{9,8},{10,11... | collective-permute-start | bytes 1572872 | tf_op jit(solution)/shard_map/ppermute | solution.py:202
  114.7 1.4 collective-permute-done.18.refs_20_
  116.1 3.0 %collective-permute-start.13 = (bf16[2,16,64,128]{3,2,1,0:T(8,128)(2,1)S(1)}, bf16[2,16,64,128]{3,2,1,0:T(8,128)(2,1)S(1)}, u32[]{:S(2)}, u32[]{:S(2)}) collective-permute-start(bf16[2,16,64,128]{3,2,1,0:T(8,128)(2,1)S(1)} %collective-permute-done.11.refs_13_), channel_id=1, source_target_pairs={{0,1},{1,0},{2,3},{3,2},{4,5},{5,4},{6,7},{7,6},{8,9},{9,8},{10,11... | collective-permute-start | bytes 1572872 | tf_op jit(solution)/shard_map/ppermute | solution.py:202
  119.2 3.8 %collective-permute-start.8 = (bf16[2,16,64,128]{3,2,1,0:T(8,128)(2,1)S(1)}, bf16[2,16,64,128]{3,2,1,0:T(8,128)(2,1)}, u32[]{:S(2)}, u32[]{:S(2)}) collective-permute-start(bf16[2,16,64,128]{3,2,1,0:T(8,128)(2,1)S(1)} %collective-permute-done.3.refs_5_), channel_id=1, source_target_pairs={{0,6},{1,7},{2,4},{3,5},{4,2},{5,3},{6,0},{7,1},{8,14},{9,15},{10,... | collective-permute-start | bytes 1572872 | tf_op jit(solution)/shard_map/ppermute | solution.py:202
  124.9 10.3 %collective-permute-done.8.refs_9_ = bf16[2,16,64,128]{3,2,1,0:T(8,128)(2,1)} collective-permute-done((bf16[2,16,64,128]{3,2,1,0:T(8,128)(2,1)S(1)}, bf16[2,16,64,128]{3,2,1,0:T(8,128)(2,1)}, u32[]{:S(2)}, u32[]{:S(2)}) %collective-permute-start.8) | collective-permute-done | bytes 524320 | tf_op jit(solution)/shard_map/ppermute | solution.py:202
  136.2 3.0 %collective-permute-done.22.refs_24_ = bf16[2,16,64,128]{3,2,1,0:T(8,128)(2,1)} collective-permute-done((bf16[2,16,64,128]{3,2,1,0:T(8,128)(2,1)S(1)}, bf16[2,16,64,128]{3,2,1,0:T(8,128)(2,1)}, u32[]{:S(2)}, u32[]{:S(2)}) %collective-permute-start.22) | collective-permute-done | bytes 524320 | tf_op jit(solution)/shard_map/ppermute | solution.py:202
  140.6 9.2 %collective-permute-done.24.refs_25_ = bf16[2,16,64,128]{3,2,1,0:T(8,128)(2,1)} collective-permute-done((bf16[2,16,64,128]{3,2,1,0:T(8,128)(2,1)}, bf16[2,16,64,128]{3,2,1,0:T(8,128)(2,1)}, u32[]{:S(2)}, u32[]{:S(2)}) %collective-permute-start.24) | collective-permute-done | bytes 524320 | tf_op jit(solution)/shard_map/ppermute | solution.py:202
  152.7 14.2 %correlate.1 = bf16[32,2,64,1024]{3,2,1,0:T(8,128)(2,1)} custom-call(s32[1]{0:T(128)} %bitcast.blk_ref, f32[32]{0:T(128)} %dynamic_slice.6.scale_ref, bf16[2,16,64,128]{3,2,1,0:T(8,128)(2,1)} %copy-done, bf16[2,16,64,128]{3,2,1,0:T(8,128)(2,1)} %copy-done.1, bf16[2,16,64,128]{3,2,1,0:T(8,128)(2,1)} %collective-permute-done.refs_2_, ...), custom_call_target="tpu_custom_call" | custom-call | flops 2200000000 | bytes 25000000 | tf_op jit(solution)/shard_map/correlate/pallas_call | solution.py:185
  (96 shorter events, 11.9 us)
Async XLA Ops:
  26.2 30.4 %all-to-all-start = ((bf16[8,2,16,8,128]{4,3,2,1,0:T(8,128)(2,1)}), bf16[8,2,16,8,128]{4,3,2,1,0:T(8,128)(2,1)S(1)}, u32[]{:S(2)}, u32[]{:S(2)}) async-start(bf16[8,2,16,8,128]{4,3,2,1,0:T(8,128)(2,1)} %spectra.2), calls=%async_computation | async-start | bytes 1048576 | tf_op jit(solution)/shard_map/all_to_all | solution.py:209
  56.6 13.8 %all-to-all-start.1 = ((bf16[8,2,16,8,128]{4,3,2,1,0:T(8,128)(2,1)}), bf16[8,2,16,8,128]{4,3,2,1,0:T(8,128)(2,1)S(1)}, u32[]{:S(2)}, u32[]{:S(2)}) async-start(bf16[8,2,16,8,128]{4,3,2,1,0:T(8,128)(2,1)} %spectra.3), calls=%async_computation.1 | async-start | bytes 1048576 | tf_op jit(solution)/shard_map/all_to_all | solution.py:209
  61.9 18.9 %collective-permute-start.14 = (bf16[2,16,64,128]{3,2,1,0:T(8,128)(2,1)S(1)}, bf16[2,16,64,128]{3,2,1,0:T(8,128)(2,1)S(1)}, u32[]{:S(2)}, u32[]{:S(2)}) collective-permute-start(bf16[2,16,64,128]{3,2,1,0:T(8,128)(2,1)S(1)} %copy_bitcast_fusion.1.refs_0_), channel_id=1, source_target_pairs={{0,8},{1,9},{2,10},{3,11},{4,12},{5,13},{6,14},{7,15},{8,0},{9,1},... | collective-permute-start | bytes 1572872 | tf_op jit(solution)/shard_map/ppermute | solution.py:202
  64.5 20.2 %collective-permute-start.6 = (bf16[2,16,64,128]{3,2,1,0:T(8,128)(2,1)S(1)}, bf16[2,16,64,128]{3,2,1,0:T(8,128)(2,1)S(1)}, u32[]{:S(2)}, u32[]{:S(2)}) collective-permute-start(bf16[2,16,64,128]{3,2,1,0:T(8,128)(2,1)S(1)} %copy_bitcast_fusion.1.refs_0_), channel_id=1, source_target_pairs={{0,6},{1,7},{2,4},{3,5},{4,2},{5,3},{6,0},{7,1},{8,14},{9,15},{10,... | collective-permute-start | bytes 1572872 | tf_op jit(solution)/shard_map/ppermute | solution.py:202
  68.2 16.4 %collective-permute-start.2 = (bf16[2,16,64,128]{3,2,1,0:T(8,128)(2,1)S(1)}, bf16[2,16,64,128]{3,2,1,0:T(8,128)(2,1)S(1)}, u32[]{:S(2)}, u32[]{:S(2)}) collective-permute-start(bf16[2,16,64,128]{3,2,1,0:T(8,128)(2,1)S(1)} %copy_bitcast_fusion.1.refs_0_), channel_id=1, source_target_pairs={{0,2},{1,3},{2,0},{3,1},{4,6},{5,7},{6,4},{7,5},{8,10},{9,11},{10,... | collective-permute-start | bytes 1572872 | tf_op jit(solution)/shard_map/ppermute | solution.py:202
  68.2 20.6 %collective-permute-start = (bf16[2,16,64,128]{3,2,1,0:T(8,128)(2,1)S(1)}, bf16[2,16,64,128]{3,2,1,0:T(8,128)(2,1)}, u32[]{:S(2)}, u32[]{:S(2)}) collective-permute-start(bf16[2,16,64,128]{3,2,1,0:T(8,128)(2,1)S(1)} %copy_bitcast_fusion.1.refs_0_), channel_id=1, source_target_pairs={{0,1},{1,0},{2,3},{3,2},{4,5},{5,4},{6,7},{7,6},{8,9},{9,8},{10,11... | collective-permute-start | bytes 1572872 | tf_op jit(solution)/shard_map/ppermute | solution.py:202
  70.5 21.6 %collective-permute-start.15 = (bf16[2,16,64,128]{3,2,1,0:T(8,128)(2,1)S(1)}, bf16[2,16,64,128]{3,2,1,0:T(8,128)(2,1)S(1)}, u32[]{:S(2)}, u32[]{:S(2)}) collective-permute-start(bf16[2,16,64,128]{3,2,1,0:T(8,128)(2,1)S(1)} %copy_bitcast_fusion.refs_1_), channel_id=1, source_target_pairs={{0,8},{1,9},{2,10},{3,11},{4,12},{5,13},{6,14},{7,15},{8,0},{9,1},... | collective-permute-start | bytes 1572872 | tf_op jit(solution)/shard_map/ppermute | solution.py:202
  84.6 12.9 %collective-permute-start.3 = (bf16[2,16,64,128]{3,2,1,0:T(8,128)(2,1)S(1)}, bf16[2,16,64,128]{3,2,1,0:T(8,128)(2,1)S(1)}, u32[]{:S(2)}, u32[]{:S(2)}) collective-permute-start(bf16[2,16,64,128]{3,2,1,0:T(8,128)(2,1)S(1)} %copy_bitcast_fusion.refs_1_), channel_id=1, source_target_pairs={{0,2},{1,3},{2,0},{3,1},{4,6},{5,7},{6,4},{7,5},{8,10},{9,11},{10,... | collective-permute-start | bytes 1572872 | tf_op jit(solution)/shard_map/ppermute | solution.py:202
  84.6 12.9 %collective-permute-start.1 = (bf16[2,16,64,128]{3,2,1,0:T(8,128)(2,1)S(1)}, bf16[2,16,64,128]{3,2,1,0:T(8,128)(2,1)S(1)}, u32[]{:S(2)}, u32[]{:S(2)}) collective-permute-start(bf16[2,16,64,128]{3,2,1,0:T(8,128)(2,1)S(1)} %copy_bitcast_fusion.refs_1_), channel_id=1, source_target_pairs={{0,1},{1,0},{2,3},{3,2},{4,5},{5,4},{6,7},{7,6},{8,9},{9,8},{10,11... | collective-permute-start | bytes 1572872 | tf_op jit(solution)/shard_map/ppermute | solution.py:202
  92.1 12.8 %collective-permute-start.27 = (bf16[2,16,64,128]{3,2,1,0:T(8,128)(2,1)S(1)}, bf16[2,16,64,128]{3,2,1,0:T(8,128)(2,1)S(1)}, u32[]{:S(2)}, u32[]{:S(2)}) collective-permute-start(bf16[2,16,64,128]{3,2,1,0:T(8,128)(2,1)S(1)} %collective-permute-done.6.refs_12_), channel_id=1, source_target_pairs={{0,8},{1,9},{2,10},{3,11},{4,12},{5,13},{6,14},{7,15},{8,0},{9,1},... | collective-permute-start | bytes 1572872 | tf_op jit(solution)/shard_map/ppermute | solution.py:202
  93.0 15.7 %collective-permute-start.12 = (bf16[2,16,64,128]{3,2,1,0:T(8,128)(2,1)S(1)}, bf16[2,16,64,128]{3,2,1,0:T(8,128)(2,1)S(1)}, u32[]{:S(2)}, u32[]{:S(2)}) collective-permute-start(bf16[2,16,64,128]{3,2,1,0:T(8,128)(2,1)S(1)} %collective-permute-done.6.refs_12_), channel_id=1, source_target_pairs={{0,1},{1,0},{2,3},{3,2},{4,5},{5,4},{6,7},{7,6},{8,9},{9,8},{10,11... | collective-permute-start | bytes 1572872 | tf_op jit(solution)/shard_map/ppermute | solution.py:202
  97.5 18.6 %collective-permute-start.18 = (bf16[2,16,64,128]{3,2,1,0:T(8,128)(2,1)S(1)}, bf16[2,16,64,128]{3,2,1,0:T(8,128)(2,1)S(1)}, u32[]{:S(2)}, u32[]{:S(2)}) collective-permute-start(bf16[2,16,64,128]{3,2,1,0:T(8,128)(2,1)S(1)} %collective-permute-done.2.refs_4_), channel_id=1, source_target_pairs={{0,8},{1,9},{2,10},{3,11},{4,12},{5,13},{6,14},{7,15},{8,0},{9,1},... | collective-permute-start | bytes 1572872 | tf_op jit(solution)/shard_map/ppermute | solution.py:202
  99.1 20.0 %collective-permute-start.4 = (bf16[2,16,64,128]{3,2,1,0:T(8,128)(2,1)S(1)}, bf16[2,16,64,128]{3,2,1,0:T(8,128)(2,1)S(1)}, u32[]{:S(2)}, u32[]{:S(2)}) collective-permute-start(bf16[2,16,64,128]{3,2,1,0:T(8,128)(2,1)S(1)} %collective-permute-done.2.refs_4_), channel_id=1, source_target_pairs={{0,1},{1,0},{2,3},{3,2},{4,5},{5,4},{6,7},{7,6},{8,9},{9,8},{10,11... | collective-permute-start | bytes 1572872 | tf_op jit(solution)/shard_map/ppermute | solution.py:202
  104.9 18.1 %collective-permute-start.23 = (bf16[2,16,64,128]{3,2,1,0:T(8,128)(2,1)S(1)}, bf16[2,16,64,128]{3,2,1,0:T(8,128)(2,1)}, u32[]{:S(2)}, u32[]{:S(2)}) collective-permute-start(bf16[2,16,64,128]{3,2,1,0:T(8,128)(2,1)S(1)} %collective-permute-done.15.refs_17_), channel_id=1, source_target_pairs={{0,6},{1,7},{2,4},{3,5},{4,2},{5,3},{6,0},{7,1},{8,14},{9,15},{10,... | collective-permute-start | bytes 1572872 | tf_op jit(solution)/shard_map/ppermute | solution.py:202
  108.6 14.7 %collective-permute-start.19 = (bf16[2,16,64,128]{3,2,1,0:T(8,128)(2,1)S(1)}, bf16[2,16,64,128]{3,2,1,0:T(8,128)(2,1)}, u32[]{:S(2)}, u32[]{:S(2)}) collective-permute-start(bf16[2,16,64,128]{3,2,1,0:T(8,128)(2,1)S(1)} %collective-permute-done.15.refs_17_), channel_id=1, source_target_pairs={{0,2},{1,3},{2,0},{3,1},{4,6},{5,7},{6,4},{7,5},{8,10},{9,11},{10,... | collective-permute-start | bytes 1572872 | tf_op jit(solution)/shard_map/ppermute | solution.py:202
  109.5 14.5 %collective-permute-start.17 = (bf16[2,16,64,128]{3,2,1,0:T(8,128)(2,1)S(1)}, bf16[2,16,64,128]{3,2,1,0:T(8,128)(2,1)S(1)}, u32[]{:S(2)}, u32[]{:S(2)}) collective-permute-start(bf16[2,16,64,128]{3,2,1,0:T(8,128)(2,1)S(1)} %collective-permute-done.15.refs_17_), channel_id=1, source_target_pairs={{0,1},{1,0},{2,3},{3,2},{4,5},{5,4},{6,7},{7,6},{8,9},{9,8},{10,11... | collective-permute-start | bytes 1572872 | tf_op jit(solution)/shard_map/ppermute | solution.py:202
  119.2 16.1 %collective-permute-start.8 = (bf16[2,16,64,128]{3,2,1,0:T(8,128)(2,1)S(1)}, bf16[2,16,64,128]{3,2,1,0:T(8,128)(2,1)}, u32[]{:S(2)}, u32[]{:S(2)}) collective-permute-start(bf16[2,16,64,128]{3,2,1,0:T(8,128)(2,1)S(1)} %collective-permute-done.3.refs_5_), channel_id=1, source_target_pairs={{0,6},{1,7},{2,4},{3,5},{4,2},{5,3},{6,0},{7,1},{8,14},{9,15},{10,... | collective-permute-start | bytes 1572872 | tf_op jit(solution)/shard_map/ppermute | solution.py:202
  123.0 13.0 %collective-permute-start.5 = (bf16[2,16,64,128]{3,2,1,0:T(8,128)(2,1)S(1)}, bf16[2,16,64,128]{3,2,1,0:T(8,128)(2,1)S(1)}, u32[]{:S(2)}, u32[]{:S(2)}) collective-permute-start(bf16[2,16,64,128]{3,2,1,0:T(8,128)(2,1)S(1)} %collective-permute-done.3.refs_5_), channel_id=1, source_target_pairs={{0,1},{1,0},{2,3},{3,2},{4,5},{5,4},{6,7},{7,6},{8,9},{9,8},{10,11... | collective-permute-start | bytes 1572872 | tf_op jit(solution)/shard_map/ppermute | solution.py:202
  123.3 12.7 %collective-permute-start.28 = (bf16[2,16,64,128]{3,2,1,0:T(8,128)(2,1)S(1)}, bf16[2,16,64,128]{3,2,1,0:T(8,128)(2,1)S(1)}, u32[]{:S(2)}, u32[]{:S(2)}) collective-permute-start(bf16[2,16,64,128]{3,2,1,0:T(8,128)(2,1)S(1)} %collective-permute-done.27.refs_28_), channel_id=1, source_target_pairs={{0,1},{1,0},{2,3},{3,2},{4,5},{5,4},{6,7},{7,6},{8,9},{9,8},{10,11... | collective-permute-start | bytes 1572872 | tf_op jit(solution)/shard_map/ppermute | solution.py:202
  123.9 15.2 %collective-permute-start.22 = (bf16[2,16,64,128]{3,2,1,0:T(8,128)(2,1)S(1)}, bf16[2,16,64,128]{3,2,1,0:T(8,128)(2,1)}, u32[]{:S(2)}, u32[]{:S(2)}) collective-permute-start(bf16[2,16,64,128]{3,2,1,0:T(8,128)(2,1)S(1)} %collective-permute-done.7.refs_8_), channel_id=1, source_target_pairs={{0,8},{1,9},{2,10},{3,11},{4,12},{5,13},{6,14},{7,15},{8,0},{9,1},... | collective-permute-start | bytes 1572872 | tf_op jit(solution)/shard_map/ppermute | solution.py:202
  124.5 15.4 %collective-permute-start.9 = (bf16[2,16,64,128]{3,2,1,0:T(8,128)(2,1)S(1)}, bf16[2,16,64,128]{3,2,1,0:T(8,128)(2,1)S(1)}, u32[]{:S(2)}, u32[]{:S(2)}) collective-permute-start(bf16[2,16,64,128]{3,2,1,0:T(8,128)(2,1)S(1)} %collective-permute-done.7.refs_8_), channel_id=1, source_target_pairs={{0,1},{1,0},{2,3},{3,2},{4,5},{5,4},{6,7},{7,6},{8,9},{9,8},{10,11... | collective-permute-start | bytes 1572872 | tf_op jit(solution)/shard_map/ppermute | solution.py:202
  135.9 13.9 %collective-permute-start.24 = (bf16[2,16,64,128]{3,2,1,0:T(8,128)(2,1)}, bf16[2,16,64,128]{3,2,1,0:T(8,128)(2,1)}, u32[]{:S(2)}, u32[]{:S(2)}) collective-permute-start(bf16[2,16,64,128]{3,2,1,0:T(8,128)(2,1)} %collective-permute-done.23.refs_29_), channel_id=1, source_target_pairs={{0,2},{1,3},{2,0},{3,1},{4,6},{5,7},{6,4},{7,5},{8,10},{9,11},{10,... | collective-permute-start | bytes 1572872 | tf_op jit(solution)/shard_map/ppermute | solution.py:202
  136.1 15.4 %collective-permute-start.29 = (bf16[2,16,64,128]{3,2,1,0:T(8,128)(2,1)}, bf16[2,16,64,128]{3,2,1,0:T(8,128)(2,1)}, u32[]{:S(2)}, u32[]{:S(2)}) collective-permute-start(bf16[2,16,64,128]{3,2,1,0:T(8,128)(2,1)} %collective-permute-done.23.refs_29_), channel_id=1, source_target_pairs={{0,1},{1,0},{2,3},{3,2},{4,5},{5,4},{6,7},{7,6},{8,9},{9,8},{10,11... | collective-permute-start | bytes 1572872 | tf_op jit(solution)/shard_map/ppermute | solution.py:202
  139.1 12.3 %collective-permute-start.21 = (bf16[2,16,64,128]{3,2,1,0:T(8,128)(2,1)}, bf16[2,16,64,128]{3,2,1,0:T(8,128)(2,1)}, u32[]{:S(2)}, u32[]{:S(2)}) collective-permute-start(bf16[2,16,64,128]{3,2,1,0:T(8,128)(2,1)} %collective-permute-done.19.refs_21_), channel_id=1, source_target_pairs={{0,1},{1,0},{2,3},{3,2},{4,5},{5,4},{6,7},{7,6},{8,9},{9,8},{10,11... | collective-permute-start | bytes 1572872 | tf_op jit(solution)/shard_map/ppermute | solution.py:202
  (30 other events, 989.1 us)

commit v2 on v1

--- a/solution.py
+++ b/solution.py
@@ -15,7 +15,6 @@
 TAPS = 4
 FRAMES = 128
 CHUNK = 64
-STEP = 32
 
 
 def dft_tables():
@@ -31,70 +30,116 @@
     return np.stack(tables)
 
 
-def spectra_kernel(first_frame, x_hbm, taps_ref, table_ref, weight_ref, out_ref, x_vmem, fold, sums, turned, sems):
-    lanes = STEP * NFFT
-    halo = (TAPS - 1) * NFFT
-    copies = []
-    for s in range(CHUNK // STEP):
-        start = 0 if s == 0 else s * lanes + halo
-        size = lanes + halo if s == 0 else lanes
-        copies.append(
-            pltpu.make_async_copy(
-                x_hbm.at[:, 0, :, pl.ds(first_frame * NFFT + start, size)],
-                x_vmem.at[:, :, pl.ds(start, size)],
-                sems.at[s],
+BLOCK = 256
+BLOCKS = HALF // BLOCK
+
+
+def spectra_kernel(
+    first_frame, x_hbm, taps_ref, table_hbm, weight_ref, out_ref,
+    x_vmem, table, fold_a, fold_b, total, sums, turned, x_sems, table_sems,
+):
+    frames = CHUNK + TAPS - 1
+    rows = CHUNK * 8
+    x_copies, table_copies = [], []
+    for kb in range(BLOCKS):
+        for half in range(2):
+            lanes = pl.ds(half * HALF + kb * BLOCK, BLOCK)
+            x_copies.append(
+                pltpu.make_async_copy(
+                    x_hbm.at[:, pl.ds(first_frame, frames), :, lanes],
+                    x_vmem.at[:, :, :, lanes],
+                    x_sems.at[kb, half],
+                )
             )
+        samples = pl.ds(kb * BLOCK, BLOCK)
+        table_copies.append(
+            pltpu.make_async_copy(table_hbm.at[:, :, samples], table.at[:, :, samples], table_sems.at[kb])
         )
-    for copy in copies:
-        copy.start()
-    rows = STEP * 8
-    for s in range(CHUNK // STEP):
-        copies[s].wait()
-
-        def fir(t, carry):
-            p = t // 16
-            n0 = pl.multiple_of((t % 16) * 128, 128)
-
-            def load(f, offset):
-                lane = pl.multiple_of((s * STEP + f) * NFFT + offset + n0, 128)
-                return x_vmem[p, :, pl.ds(lane, 128)].astype(jnp.float32)
-
-            def tap(k, offset):
-                return jnp.broadcast_to(taps_ref[k : k + 1, pl.ds(n0 + offset, 128)], (8, 128))
-
-            taps = [[tap(k, offset) for k in range(TAPS)] for offset in (0, HALF)]
-            window = [[load(f, offset) for f in range(TAPS - 1)] for offset in (0, HALF)]
-            for pair in range(STEP // 2):
-                even, odd = [], []
-                for f in (2 * pair, 2 * pair + 1):
-                    halves = []
-                    for w, h, offset in zip(window, taps, (0, HALF)):
-                        w.append(load(f + TAPS - 1, offset))
-                        halves.append(((w[0] * h[0] + w[1] * h[1]) + w[2] * h[2]) + w[3] * h[3])
-                        w.pop(0)
-                    even.append(halves[0] + halves[1])
-                    odd.append(halves[0] - halves[1])
-                where = pl.ds(pl.multiple_of(p * rows, rows) + pair * 16, 16)
-                for cls, both in enumerate((even, odd)):
-                    value = jnp.concatenate(both, axis=0)
-                    high = value.astype(jnp.bfloat16)
-                    low = (value - high.astype(jnp.float32)).astype(jnp.bfloat16)
-                    fold[cls, 0, where, pl.ds(n0, 128)] = high
-                    fold[cls, 1, where, pl.ds(n0, 128)] = low
+    for kb in range(BLOCKS):
+        x_copies[2 * kb].start()
+        x_copies[2 * kb + 1].start()
+        table_copies[kb].start()
+
+    def fir(kb, p, tile, fold):
+        n0 = pl.multiple_of(kb * BLOCK + tile * 128, 128)
+        to = pl.ds(pl.multiple_of(tile * 128, 128), 128)
+
+        def load(f, offset):
+            return x_vmem[p, f, :, pl.ds(n0 + offset, 128)].astype(jnp.float32)
+
+        def tap(k, offset):
+            return jnp.broadcast_to(taps_ref[k : k + 1, pl.ds(n0 + offset, 128)], (8, 128))
+
+        taps = [[tap(k, offset) for k in range(TAPS)] for offset in (0, HALF)]
+        window = [[load(f, offset) for f in range(TAPS - 1)] for offset in (0, HALF)]
+        for pair in range(CHUNK // 2):
+            even, odd = [], []
+            for f in (2 * pair, 2 * pair + 1):
+                halves = []
+                for w, h, offset in zip(window, taps, (0, HALF)):
+                    w.append(load(f + TAPS - 1, offset))
+                    halves.append(((w[0] * h[0] + w[1] * h[1]) + w[2] * h[2]) + w[3] * h[3])
+                    w.pop(0)
+                even.append(halves[0] + halves[1])
+                odd.append(halves[0] - halves[1])
+            for cls, both in enumerate((even, odd)):
+                value = jnp.concatenate(both, axis=0)
+                high = value.astype(jnp.bfloat16)
+                low = (value - high.astype(jnp.float32)).astype(jnp.bfloat16)
+                fold[p, cls, 0, pair * 16 : pair * 16 + 16, to] = high
+                fold[p, cls, 1, pair * 16 : pair * 16 + 16, to] = low
+
+    def product(kb, cls, p, fold):
+        samples = pl.ds(pl.multiple_of(kb * BLOCK, BLOCK), BLOCK)
+        high, low = fold[p, cls, 0], fold[p, cls, 1]
+        left = jnp.concatenate([high, low, high], axis=1)
+        table_high, table_low = table[cls, 0, samples, :], table[cls, 1, samples, :]
+        right = jnp.concatenate([table_high, table_high, table_low], axis=0)
+        return jnp.dot(left, right, preferred_element_type=jnp.float32)
+
+    def stage(kb, fold_in, fold_out, first=False):
+        def unit(u, carry):
+            a, b = u // 2, u % 2
+            if fold_out is not None:
+                fir(kb + 1, a, b, fold_out)
+            if fold_in is not None:
+                value = product(kb, a, b, fold_in)
+                if first:
+                    total[a, b] = value
+                else:
+                    total[a, b] += value
             return carry
 
-        lax.fori_loop(0, 32, fir, 0)
-        for cls in range(2):
-            total = jnp.dot(fold[cls, 0], table_ref[cls, 0], preferred_element_type=jnp.float32)
-            total += jnp.dot(fold[cls, 1], table_ref[cls, 0], preferred_element_type=jnp.float32)
-            total += jnp.dot(fold[cls, 0], table_ref[cls, 1], preferred_element_type=jnp.float32)
-            real = total[:rows, :128] + total[rows:, 128:]
-            imag = total[rows:, :128] - total[:rows, 128:]
-            weight = weight_ref[...]
-            real = (real.reshape(STEP, 8, 128) * weight).reshape(rows, 128)
-            imag = (imag.reshape(STEP, 8, 128) * weight).reshape(rows, 128)
-            sums[cls, s * rows : (s + 1) * rows, :] = real
-            sums[cls, CHUNK * 8 + s * rows : CHUNK * 8 + (s + 1) * rows, :] = imag
+        lax.fori_loop(0, 4, unit, 0)
+
+    def arrive(kb):
+        x_copies[2 * kb].wait()
+        x_copies[2 * kb + 1].wait()
+        table_copies[kb].wait()
+
+    arrive(0)
+    stage(-1, None, fold_a)
+    arrive(1)
+    stage(0, fold_a, fold_b, first=True)
+    arrive(2)
+    stage(1, fold_b, fold_a)
+    for kb in range(3, BLOCKS):
+        arrive(kb)
+
+    def two_stages(k, carry):
+        stage(2 * k, fold_a, fold_b)
+        stage(2 * k + 1, fold_b, fold_a)
+        return carry
+
+    lax.fori_loop(1, BLOCKS // 2 - 1, two_stages, 0)
+    stage(BLOCKS - 2, fold_a, fold_b)
+    stage(BLOCKS - 1, fold_b, None)
+    weight = weight_ref[...]
+    for cls in range(2):
+        real = total[cls, 0, :, :128] + total[cls, 1, :, 128:]
+        imag = total[cls, 1, :, :128] - total[cls, 0, :, 128:]
+        sums[cls, :rows, :] = (real.reshape(CHUNK, 8, 128) * weight).reshape(rows, 128)
+        sums[cls, rows:, :] = (imag.reshape(CHUNK, 8, 128) * weight).reshape(rows, 128)
     for cls in range(2):
         for i in range(8):
             turned[cls, i * 128 : (i + 1) * 128, :] = sums[cls, pl.ds(i, 128, stride=8), :].T
@@ -112,14 +157,23 @@
     return pl.pallas_call(
         functools.partial(spectra_kernel, first_frame),
         out_shape=jax.ShapeDtypeStruct((8, 2, 16, 8, 128), jnp.bfloat16),
-        in_specs=[pl.BlockSpec(memory_space=pl.ANY)] + [pl.BlockSpec(memory_space=pltpu.VMEM)] * 3,
+        in_specs=[
+            pl.BlockSpec(memory_space=pltpu.HBM),
+            pl.BlockSpec(memory_space=pltpu.VMEM),
+            pl.BlockSpec(memory_space=pltpu.HBM),
+            pl.BlockSpec(memory_space=pltpu.VMEM),
+        ],
         out_specs=pl.BlockSpec(memory_space=pltpu.VMEM),
         scratch_shapes=[
-            pltpu.VMEM((2, 8, (CHUNK + TAPS - 1) * NFFT), jnp.bfloat16),
-            pltpu.VMEM((2, 2, 2 * STEP * 8, HALF), jnp.bfloat16),
+            pltpu.VMEM((2, CHUNK + TAPS - 1, 8, NFFT), jnp.bfloat16),
+            pltpu.VMEM((2, 2, HALF, 256), jnp.bfloat16),
+            pltpu.VMEM((2, 2, 2, CHUNK * 8, BLOCK), jnp.bfloat16),
+            pltpu.VMEM((2, 2, 2, CHUNK * 8, BLOCK), jnp.bfloat16),
+            pltpu.VMEM((2, 2, CHUNK * 8, 256), jnp.float32),
             pltpu.VMEM((2, 2 * CHUNK * 8, 128), jnp.float32),
             pltpu.VMEM((2, 8 * 128, 128), jnp.float32),
-            pltpu.SemaphoreType.DMA((CHUNK // STEP,)),
+            pltpu.SemaphoreType.DMA((BLOCKS, 2)),
+            pltpu.SemaphoreType.DMA((BLOCKS,)),
         ],
         compiler_params=pltpu.CompilerParams(vmem_limit_bytes=56 * 1024 * 1024),
         cost_estimate=pl.CostEstimate(flops=6_500_000_000, bytes_accessed=14_000_000, transcendentals=0),
@@ -219,16 +273,20 @@
     scale = lax.dynamic_slice_in_dim(scales, chan * 32, 32, 0)
     tables = jnp.asarray(dft_tables())
 
-    first = turn(spectra(0, voltages, fir_taps, tables, weight))
-    second = turn(spectra(CHUNK, voltages, fir_taps, tables, weight))
+    planes = voltages.reshape(2, 8, FRAMES + TAPS - 1, NFFT).transpose(0, 2, 1, 3)
+
+    first = turn(spectra(0, planes, fir_taps, tables, weight))
+    weight, first = lax.optimization_barrier((weight, first))
+    later = spectra(CHUNK, planes, fir_taps, tables, weight)
     one = {0: first}
-    one[Z1] = send(first, Z1)
-    one[Z3] = send(first, Z3)
-    one[X2] = send(first, X2)
+    for bits in (Z1, Z3, X2):
+        one[bits] = send(first, bits)
+    later, one[Z1], one[Z3], one[X2] = lax.optimization_barrier((later, one[Z1], one[Z3], one[X2]))
     one[Z1 ^ Z3] = send(one[Z3], Z1)
     one[X2 ^ Z1] = send(one[Z1], X2)
     one[X2 ^ Z3] = send(one[Z3], X2)
     one[X2 ^ Z1 ^ Z3] = send(one[Z1 ^ Z3], X2)
+    second = turn(later)
     two = {0: second}
     two[X2] = send(second, X2)
     for m in (0, X2):

time: 168 us -> 158 us (0.940)
  starting transfers between devices: 58.6 us -> 34.1 us
  blocking collectives: 0 us -> 15.1 us
  Pallas kernels: 63.2 us -> 50.6 us
  waiting for transfers between devices: 42.2 us -> 54.2 us
    ppermute x30, starting transfers between devices: 47.5 us -> 30.6 us  [send(): return lax.ppermute(array, 'blk', [(b, b ^ bits) for b in range(16)])]
    all_to_all x0 -> x1, blocking collectives: none -> 15.1 us  [turn(): got = lax.all_to_all(chunk, 'chan', split_axis=0, concat_axis=0, tiled=True)]
    pallas_call x2, Pallas kernels: 48.9 us -> 36.4 us  [spectra(): pl.pallas_call(functools.partial(spectra_kernel, first_frame), out_shape=...]
    all_to_all x2 -> x1, starting transfers between devices: 11.1 us -> 3.49 us  [turn(): got = lax.all_to_all(chunk, 'chan', split_axis=0, concat_axis=0, tiled=True)]
    ppermute x30, waiting for transfers between devices: 42.1 us -> 49.5 us  [send(): return lax.ppermute(array, 'blk', [(b, b ^ bits) for b in range(16)])]
    all_to_all x2 -> x1, waiting for transfers between devices: 0.08 us -> 4.71 us  [turn(): got = lax.all_to_all(chunk, 'chan', split_axis=0, concat_axis=0, tiled=True)]
  transfers between devices with their start and end apart: 32 -> 31, of which waited for: 11 -> 10; matrix products, arithmetic and copies ran while one was open for 1% -> 1% of each run, Pallas kernels for 15% -> 12%
where the time goes in v2:
time: 158 us; the launch traced here: 157 us
  waiting for transfers between devices  54.2 us (34%)
  Pallas kernels  50.6 us (32%)
  starting transfers between devices  34.1 us (22%)
  blocking collectives  15.1 us (10%)
  local copies, waits for them, and re-layouts  2.14 us (1%)
    ppermute x30, waiting for transfers between devices, send(): return lax.ppermute(array, 'blk', [(b, b ^ bits) for b in range(16)])  49.5 us
    pallas_call x2, Pallas kernels, spectra(): pl.pallas_call(functools.partial(spectra_kernel, first_frame), out_shape=...  36.4 us
    ppermute x30, starting transfers between devices, send(): return lax.ppermute(array, 'blk', [(b, b ^ bits) for b in range(16)])  30.6 us
    all_to_all x1, blocking collectives, turn(): got = lax.all_to_all(chunk, 'chan', split_axis=0, concat_axis=0, tiled=True)  15.1 us
    pallas_call x1, Pallas kernels, correlate(): pl.pallas_call(correlate_kernel, out_shape=jax.ShapeDtypeStruct((32, 2, 6...  14.2 us
    all_to_all x1, waiting for transfers between devices, turn(): got = lax.all_to_all(chunk, 'chan', split_axis=0, concat_axis=0, tiled=True)  4.71 us
    all_to_all x1, starting transfers between devices, turn(): got = lax.all_to_all(chunk, 'chan', split_axis=0, concat_axis=0, tiled=True)  3.49 us
  transfers between devices with their start and end apart: 31, of which 10 were waited for; matrix products, arithmetic and copies ran while one was open for 1% of the time, Pallas kernels for 12%

profile of v2, /device:TPU:1, one launch (start us, length us, event | category | flops | bytes accessed | tf_op | source)
XLA Modules:
  0.0 157.3 jit_solution(4562786738721293966)
XLA Ops:
  1.7 18.2 %spectra.2 = bf16[8,2,16,8,128]{4,3,2,1,0:T(8,128)(2,1)} custom-call(bf16[2,131,8,4096]{3,2,1,0:T(8,128)(2,1)} %bitcast.14, f32[4,4096]{1,0:T(4,128)} %taps_ref.3, bf16[2,2,2048,256]{3,2,1,0:T(8,128)(2,1)} %constant.31.clone.table_hbm, f32[8,128]{1,0:T(8,128)} %broadcast_in_dim.10.weight_ref), custom_call_target="tpu_custom_call" | custom-call | flops 6499999744 | bytes 14000000 | tf_op jit(solution)/shard_map/spectra/pallas_call | solution.py:157
  19.9 15.1 %all_to_all.10 = bf16[8,2,16,8,128]{4,3,2,1,0:T(8,128)(2,1)S(1)} all-to-all(bf16[8,2,16,8,128]{4,3,2,1,0:T(8,128)(2,1)} %spectra.2), channel_id=1, replica_groups=mesh['chan'=8,'blk'=16] {'chan'}, dimensions={0} | all-to-all | bytes 1048576 | tf_op jit(solution)/shard_map/all_to_all | solution.py:263
  35.2 2.0 %collective-permute-start.3 = (bf16[2,16,64,128]{3,2,1,0:T(8,128)(2,1)S(1)}, bf16[2,16,64,128]{3,2,1,0:T(8,128)(2,1)S(1)}, u32[]{:S(2)}, u32[]{:S(2)}) collective-permute-start(bf16[2,16,64,128]{3,2,1,0:T(8,128)(2,1)S(1)} %copy_bitcast_fusion.1.refs_0_), channel_id=1, source_target_pairs={{0,1},{1,0},{2,3},{3,2},{4,5},{5,4},{6,7},{7,6},{8,9},{9,8},{10,11... | collective-permute-start | bytes 1572872 | tf_op jit(solution)/shard_map/ppermute | solution.py:256
  37.2 2.5 %collective-permute-start.2 = (bf16[2,16,64,128]{3,2,1,0:T(8,128)(2,1)S(1)}, bf16[2,16,64,128]{3,2,1,0:T(8,128)(2,1)S(1)}, u32[]{:S(2)}, u32[]{:S(2)}) collective-permute-start(bf16[2,16,64,128]{3,2,1,0:T(8,128)(2,1)S(1)} %copy_bitcast_fusion.1.refs_0_), channel_id=1, source_target_pairs={{0,8},{1,9},{2,10},{3,11},{4,12},{5,13},{6,14},{7,15},{8,0},{9,1},... | collective-permute-start | bytes 1572872 | tf_op jit(solution)/shard_map/ppermute | solution.py:256
  39.7 3.8 %collective-permute-start.1 = (bf16[2,16,64,128]{3,2,1,0:T(8,128)(2,1)S(1)}, bf16[2,16,64,128]{3,2,1,0:T(8,128)(2,1)S(1)}, u32[]{:S(2)}, u32[]{:S(2)}) collective-permute-start(bf16[2,16,64,128]{3,2,1,0:T(8,128)(2,1)S(1)} %copy_bitcast_fusion.1.refs_0_), channel_id=1, source_target_pairs={{0,6},{1,7},{2,4},{3,5},{4,2},{5,3},{6,0},{7,1},{8,14},{9,15},{10,... | collective-permute-start | bytes 1572872 | tf_op jit(solution)/shard_map/ppermute | solution.py:256
  43.4 18.2 %spectra.3 = bf16[8,2,16,8,128]{4,3,2,1,0:T(8,128)(2,1)} custom-call(bf16[2,131,8,4096]{3,2,1,0:T(8,128)(2,1)} %bitcast.15, f32[4,4096]{1,0:T(4,128)} %taps_ref.3, bf16[2,2,2048,256]{3,2,1,0:T(8,128)(2,1)} %constant.31.clone.table_hbm, f32[8,128]{1,0:T(8,128)} %broadcast_in_dim.10.weight_ref), custom_call_target="tpu_custom_call" | custom-call | flops 6499999744 | bytes 14000000 | tf_op jit(solution)/shard_map/spectra/pallas_call | solution.py:157
  62.4 3.5 %all-to-all-start.1 = ((bf16[8,2,16,8,128]{4,3,2,1,0:T(8,128)(2,1)}), bf16[8,2,16,8,128]{4,3,2,1,0:T(8,128)(2,1)S(1)}, u32[]{:S(2)}, u32[]{:S(2)}) async-start(bf16[8,2,16,8,128]{4,3,2,1,0:T(8,128)(2,1)} %spectra.3), calls=%async_computation.1 | async-start | bytes 1048576 | tf_op jit(solution)/shard_map/all_to_all | solution.py:263
  66.8 2.4 %collective-permute-start.27 = (bf16[2,16,64,128]{3,2,1,0:T(8,128)(2,1)S(1)}, bf16[2,16,64,128]{3,2,1,0:T(8,128)(2,1)}, u32[]{:S(2)}, u32[]{:S(2)}) collective-permute-start(bf16[2,16,64,128]{3,2,1,0:T(8,128)(2,1)S(1)} %collective-permute-done.1.refs_12_), channel_id=1, source_target_pairs={{0,8},{1,9},{2,10},{3,11},{4,12},{5,13},{6,14},{7,15},{8,0},{9,1},... | collective-permute-start | bytes 1572872 | tf_op jit(solution)/shard_map/ppermute | solution.py:256
  69.8 1.8 %collective-permute-start.8 = (bf16[2,16,64,128]{3,2,1,0:T(8,128)(2,1)S(1)}, bf16[2,16,64,128]{3,2,1,0:T(8,128)(2,1)}, u32[]{:S(2)}, u32[]{:S(2)}) collective-permute-start(bf16[2,16,64,128]{3,2,1,0:T(8,128)(2,1)S(1)} %collective-permute-done.1.refs_12_), channel_id=1, source_target_pairs={{0,2},{1,3},{2,0},{3,1},{4,6},{5,7},{6,4},{7,5},{8,10},{9,11},{10,... | collective-permute-start | bytes 1572872 | tf_op jit(solution)/shard_map/ppermute | solution.py:256
  71.5 4.7 %all-to-all-done.1 = bf16[8,2,16,8,128]{4,3,2,1,0:T(8,128)(2,1)S(1)} async-done(((bf16[8,2,16,8,128]{4,3,2,1,0:T(8,128)(2,1)}), bf16[8,2,16,8,128]{4,3,2,1,0:T(8,128)(2,1)S(1)}, u32[]{:S(2)}, u32[]{:S(2)}) %all-to-all-start.1) | async-done | bytes 524320 | tf_op jit(solution)/shard_map/all_to_all | solution.py:263
  76.4 8.3 %collective-permute-done.18.refs_20_ = bf16[2,16,64,128]{3,2,1,0:T(8,128)(2,1)} collective-permute-done((bf16[2,16,64,128]{3,2,1,0:T(8,128)(2,1)S(1)}, bf16[2,16,64,128]{3,2,1,0:T(8,128)(2,1)}, u32[]{:S(2)}, u32[]{:S(2)}) %collective-permute-start.18) | collective-permute-done | bytes 524320 | tf_op jit(solution)/shard_map/ppermute | solution.py:256
  84.6 2.4 %collective-permute-start.15 = (bf16[2,16,64,128]{3,2,1,0:T(8,128)(2,1)S(1)}, bf16[2,16,64,128]{3,2,1,0:T(8,128)(2,1)S(1)}, u32[]{:S(2)}, u32[]{:S(2)}) collective-permute-start(bf16[2,16,64,128]{3,2,1,0:T(8,128)(2,1)S(1)} %copy_bitcast_fusion.refs_1_), channel_id=1, source_target_pairs={{0,8},{1,9},{2,10},{3,11},{4,12},{5,13},{6,14},{7,15},{8,0},{9,1},... | collective-permute-start | bytes 1572872 | tf_op jit(solution)/shard_map/ppermute | solution.py:256
  87.3 8.6 %collective-permute-done.27.refs_28_ = bf16[2,16,64,128]{3,2,1,0:T(8,128)(2,1)} collective-permute-done((bf16[2,16,64,128]{3,2,1,0:T(8,128)(2,1)S(1)}, bf16[2,16,64,128]{3,2,1,0:T(8,128)(2,1)}, u32[]{:S(2)}, u32[]{:S(2)}) %collective-permute-start.27) | collective-permute-done | bytes 524320 | tf_op jit(solution)/shard_map/ppermute | solution.py:256
  95.9 1.7 %collective-permute-start.5 = (bf16[2,16,64,128]{3,2,1,0:T(8,128)(2,1)S(1)}, bf16[2,16,64,128]{3,2,1,0:T(8,128)(2,1)S(1)}, u32[]{:S(2)}, u32[]{:S(2)}) collective-permute-start(bf16[2,16,64,128]{3,2,1,0:T(8,128)(2,1)S(1)} %copy_bitcast_fusion.refs_1_), channel_id=1, source_target_pairs={{0,2},{1,3},{2,0},{3,1},{4,6},{5,7},{6,4},{7,5},{8,10},{9,11},{10,... | collective-permute-start | bytes 1572872 | tf_op jit(solution)/shard_map/ppermute | solution.py:256
  97.6 1.1 collective-permute-start.4
  98.8 8.2 %collective-permute-done.15.refs_17_ = bf16[2,16,64,128]{3,2,1,0:T(8,128)(2,1)S(1)} collective-permute-done((bf16[2,16,64,128]{3,2,1,0:T(8,128)(2,1)S(1)}, bf16[2,16,64,128]{3,2,1,0:T(8,128)(2,1)S(1)}, u32[]{:S(2)}, u32[]{:S(2)}) %collective-permute-start.15) | collective-permute-done | bytes 524320 | tf_op jit(solution)/shard_map/ppermute | solution.py:256
  107.6 2.5 %collective-permute-start.22 = (bf16[2,16,64,128]{3,2,1,0:T(8,128)(2,1)}, bf16[2,16,64,128]{3,2,1,0:T(8,128)(2,1)}, u32[]{:S(2)}, u32[]{:S(2)}) collective-permute-start(bf16[2,16,64,128]{3,2,1,0:T(8,128)(2,1)} %collective-permute-done.8.refs_8_), channel_id=1, source_target_pairs={{0,8},{1,9},{2,10},{3,11},{4,12},{5,13},{6,14},{7,15},{8,0},{9,1},... | collective-permute-start | bytes 1572872 | tf_op jit(solution)/shard_map/ppermute | solution.py:256
  110.7 1.6 %collective-permute-start.19 = (bf16[2,16,64,128]{3,2,1,0:T(8,128)(2,1)S(1)}, bf16[2,16,64,128]{3,2,1,0:T(8,128)(2,1)}, u32[]{:S(2)}, u32[]{:S(2)}) collective-permute-start(bf16[2,16,64,128]{3,2,1,0:T(8,128)(2,1)S(1)} %collective-permute-done.15.refs_17_), channel_id=1, source_target_pairs={{0,2},{1,3},{2,0},{3,1},{4,6},{5,7},{6,4},{7,5},{8,10},{9,11},{10,... | collective-permute-start | bytes 1572872 | tf_op jit(solution)/shard_map/ppermute | solution.py:256
  112.7 10.2 %collective-permute-done.22.refs_24_ = bf16[2,16,64,128]{3,2,1,0:T(8,128)(2,1)} collective-permute-done((bf16[2,16,64,128]{3,2,1,0:T(8,128)(2,1)}, bf16[2,16,64,128]{3,2,1,0:T(8,128)(2,1)}, u32[]{:S(2)}, u32[]{:S(2)}) %collective-permute-start.22) | collective-permute-done | bytes 524320 | tf_op jit(solution)/shard_map/ppermute | solution.py:256
  122.9 0.9 collective-permute-start.14
  124.0 1.3 collective-permute-done.23.refs_29_
  125.3 0.9 collective-permute-start.7
  127.3 11.3 %collective-permute-done.9.refs_9_ = bf16[2,16,64,128]{3,2,1,0:T(8,128)(2,1)} collective-permute-done((bf16[2,16,64,128]{3,2,1,0:T(8,128)(2,1)S(1)}, bf16[2,16,64,128]{3,2,1,0:T(8,128)(2,1)}, u32[]{:S(2)}, u32[]{:S(2)}) %collective-permute-start.9) | collective-permute-done | bytes 524320 | tf_op jit(solution)/shard_map/ppermute | solution.py:256
  142.9 14.2 %correlate.1 = bf16[32,2,64,1024]{3,2,1,0:T(8,128)(2,1)} custom-call(s32[1]{0:T(128)} %bitcast.blk_ref, f32[32]{0:T(128)} %dynamic_slice.6.scale_ref, bf16[2,16,64,128]{3,2,1,0:T(8,128)(2,1)} %copy-done, bf16[2,16,64,128]{3,2,1,0:T(8,128)(2,1)} %copy-done.1, bf16[2,16,64,128]{3,2,1,0:T(8,128)(2,1)} %copy-done.2, bf16[2,16,64,128]{3,2,1,0:T(8,128)(2,1)} %copy-done.9, ...), custom_call_target="tpu_custom_call" | custom-call | flops 2200000000 | bytes 25000000 | tf_op jit(solution)/shard_map/correlate/pallas_call | solution.py:239
  (85 shorter events, 11.7 us)
Async XLA Ops:
  35.2 34.1 %collective-permute-start.3 = (bf16[2,16,64,128]{3,2,1,0:T(8,128)(2,1)S(1)}, bf16[2,16,64,128]{3,2,1,0:T(8,128)(2,1)S(1)}, u32[]{:S(2)}, u32[]{:S(2)}) collective-permute-start(bf16[2,16,64,128]{3,2,1,0:T(8,128)(2,1)S(1)} %copy_bitcast_fusion.1.refs_0_), channel_id=1, source_target_pairs={{0,1},{1,0},{2,3},{3,2},{4,5},{5,4},{6,7},{7,6},{8,9},{9,8},{10,11... | collective-permute-start | bytes 1572872 | tf_op jit(solution)/shard_map/ppermute | solution.py:256
  37.2 24.4 %collective-permute-start.2 = (bf16[2,16,64,128]{3,2,1,0:T(8,128)(2,1)S(1)}, bf16[2,16,64,128]{3,2,1,0:T(8,128)(2,1)S(1)}, u32[]{:S(2)}, u32[]{:S(2)}) collective-permute-start(bf16[2,16,64,128]{3,2,1,0:T(8,128)(2,1)S(1)} %copy_bitcast_fusion.1.refs_0_), channel_id=1, source_target_pairs={{0,8},{1,9},{2,10},{3,11},{4,12},{5,13},{6,14},{7,15},{8,0},{9,1},... | collective-permute-start | bytes 1572872 | tf_op jit(solution)/shard_map/ppermute | solution.py:256
  39.7 22.0 %collective-permute-start.1 = (bf16[2,16,64,128]{3,2,1,0:T(8,128)(2,1)S(1)}, bf16[2,16,64,128]{3,2,1,0:T(8,128)(2,1)S(1)}, u32[]{:S(2)}, u32[]{:S(2)}) collective-permute-start(bf16[2,16,64,128]{3,2,1,0:T(8,128)(2,1)S(1)} %copy_bitcast_fusion.1.refs_0_), channel_id=1, source_target_pairs={{0,6},{1,7},{2,4},{3,5},{4,2},{5,3},{6,0},{7,1},{8,14},{9,15},{10,... | collective-permute-start | bytes 1572872 | tf_op jit(solution)/shard_map/ppermute | solution.py:256
  43.4 18.3 %collective-permute-start = (bf16[2,16,64,128]{3,2,1,0:T(8,128)(2,1)S(1)}, bf16[2,16,64,128]{3,2,1,0:T(8,128)(2,1)S(1)}, u32[]{:S(2)}, u32[]{:S(2)}) collective-permute-start(bf16[2,16,64,128]{3,2,1,0:T(8,128)(2,1)S(1)} %copy_bitcast_fusion.1.refs_0_), channel_id=1, source_target_pairs={{0,2},{1,3},{2,0},{3,1},{4,6},{5,7},{6,4},{7,5},{8,10},{9,11},{10,... | collective-permute-start | bytes 1572872 | tf_op jit(solution)/shard_map/ppermute | solution.py:256
  62.4 13.8 %all-to-all-start.1 = ((bf16[8,2,16,8,128]{4,3,2,1,0:T(8,128)(2,1)}), bf16[8,2,16,8,128]{4,3,2,1,0:T(8,128)(2,1)S(1)}, u32[]{:S(2)}, u32[]{:S(2)}) async-start(bf16[8,2,16,8,128]{4,3,2,1,0:T(8,128)(2,1)} %spectra.3), calls=%async_computation.1 | async-start | bytes 1048576 | tf_op jit(solution)/shard_map/all_to_all | solution.py:263
  65.9 18.7 %collective-permute-start.18 = (bf16[2,16,64,128]{3,2,1,0:T(8,128)(2,1)S(1)}, bf16[2,16,64,128]{3,2,1,0:T(8,128)(2,1)}, u32[]{:S(2)}, u32[]{:S(2)}) collective-permute-start(bf16[2,16,64,128]{3,2,1,0:T(8,128)(2,1)S(1)} %collective-permute-done.refs_4_), channel_id=1, source_target_pairs={{0,8},{1,9},{2,10},{3,11},{4,12},{5,13},{6,14},{7,15},{8,0},{9,1},... | collective-permute-start | bytes 1572872 | tf_op jit(solution)/shard_map/ppermute | solution.py:256
  66.5 20.6 %collective-permute-start.6 = (bf16[2,16,64,128]{3,2,1,0:T(8,128)(2,1)S(1)}, bf16[2,16,64,128]{3,2,1,0:T(8,128)(2,1)}, u32[]{:S(2)}, u32[]{:S(2)}) collective-permute-start(bf16[2,16,64,128]{3,2,1,0:T(8,128)(2,1)S(1)} %collective-permute-done.refs_4_), channel_id=1, source_target_pairs={{0,1},{1,0},{2,3},{3,2},{4,5},{5,4},{6,7},{7,6},{8,9},{9,8},{10,11... | collective-permute-start | bytes 1572872 | tf_op jit(solution)/shard_map/ppermute | solution.py:256
  66.8 29.0 %collective-permute-start.27 = (bf16[2,16,64,128]{3,2,1,0:T(8,128)(2,1)S(1)}, bf16[2,16,64,128]{3,2,1,0:T(8,128)(2,1)}, u32[]{:S(2)}, u32[]{:S(2)}) collective-permute-start(bf16[2,16,64,128]{3,2,1,0:T(8,128)(2,1)S(1)} %collective-permute-done.1.refs_12_), channel_id=1, source_target_pairs={{0,8},{1,9},{2,10},{3,11},{4,12},{5,13},{6,14},{7,15},{8,0},{9,1},... | collective-permute-start | bytes 1572872 | tf_op jit(solution)/shard_map/ppermute | solution.py:256
  69.3 28.3 %collective-permute-start.13 = (bf16[2,16,64,128]{3,2,1,0:T(8,128)(2,1)S(1)}, bf16[2,16,64,128]{3,2,1,0:T(8,128)(2,1)}, u32[]{:S(2)}, u32[]{:S(2)}) collective-permute-start(bf16[2,16,64,128]{3,2,1,0:T(8,128)(2,1)S(1)} %collective-permute-done.1.refs_12_), channel_id=1, source_target_pairs={{0,1},{1,0},{2,3},{3,2},{4,5},{5,4},{6,7},{7,6},{8,9},{9,8},{10,11... | collective-permute-start | bytes 1572872 | tf_op jit(solution)/shard_map/ppermute | solution.py:256
  69.8 28.9 %collective-permute-start.8 = (bf16[2,16,64,128]{3,2,1,0:T(8,128)(2,1)S(1)}, bf16[2,16,64,128]{3,2,1,0:T(8,128)(2,1)}, u32[]{:S(2)}, u32[]{:S(2)}) collective-permute-start(bf16[2,16,64,128]{3,2,1,0:T(8,128)(2,1)S(1)} %collective-permute-done.1.refs_12_), channel_id=1, source_target_pairs={{0,2},{1,3},{2,0},{3,1},{4,6},{5,7},{6,4},{7,5},{8,10},{9,11},{10,... | collective-permute-start | bytes 1572872 | tf_op jit(solution)/shard_map/ppermute | solution.py:256
  84.6 22.4 %collective-permute-start.15 = (bf16[2,16,64,128]{3,2,1,0:T(8,128)(2,1)S(1)}, bf16[2,16,64,128]{3,2,1,0:T(8,128)(2,1)S(1)}, u32[]{:S(2)}, u32[]{:S(2)}) collective-permute-start(bf16[2,16,64,128]{3,2,1,0:T(8,128)(2,1)S(1)} %copy_bitcast_fusion.refs_1_), channel_id=1, source_target_pairs={{0,8},{1,9},{2,10},{3,11},{4,12},{5,13},{6,14},{7,15},{8,0},{9,1},... | collective-permute-start | bytes 1572872 | tf_op jit(solution)/shard_map/ppermute | solution.py:256
  87.1 20.5 %collective-permute-start.12 = (bf16[2,16,64,128]{3,2,1,0:T(8,128)(2,1)S(1)}, bf16[2,16,64,128]{3,2,1,0:T(8,128)(2,1)S(1)}, u32[]{:S(2)}, u32[]{:S(2)}) collective-permute-start(bf16[2,16,64,128]{3,2,1,0:T(8,128)(2,1)S(1)} %copy_bitcast_fusion.refs_1_), channel_id=1, source_target_pairs={{0,6},{1,7},{2,4},{3,5},{4,2},{5,3},{6,0},{7,1},{8,14},{9,15},{10,... | collective-permute-start | bytes 1572872 | tf_op jit(solution)/shard_map/ppermute | solution.py:256
  95.9 14.2 %collective-permute-start.5 = (bf16[2,16,64,128]{3,2,1,0:T(8,128)(2,1)S(1)}, bf16[2,16,64,128]{3,2,1,0:T(8,128)(2,1)S(1)}, u32[]{:S(2)}, u32[]{:S(2)}) collective-permute-start(bf16[2,16,64,128]{3,2,1,0:T(8,128)(2,1)S(1)} %copy_bitcast_fusion.refs_1_), channel_id=1, source_target_pairs={{0,2},{1,3},{2,0},{3,1},{4,6},{5,7},{6,4},{7,5},{8,10},{9,11},{10,... | collective-permute-start | bytes 1572872 | tf_op jit(solution)/shard_map/ppermute | solution.py:256
  97.6 12.9 %collective-permute-start.4 = (bf16[2,16,64,128]{3,2,1,0:T(8,128)(2,1)S(1)}, bf16[2,16,64,128]{3,2,1,0:T(8,128)(2,1)S(1)}, u32[]{:S(2)}, u32[]{:S(2)}) collective-permute-start(bf16[2,16,64,128]{3,2,1,0:T(8,128)(2,1)S(1)} %copy_bitcast_fusion.refs_1_), channel_id=1, source_target_pairs={{0,1},{1,0},{2,3},{3,2},{4,5},{5,4},{6,7},{7,6},{8,9},{9,8},{10,11... | collective-permute-start | bytes 1572872 | tf_op jit(solution)/shard_map/ppermute | solution.py:256
  107.6 15.3 %collective-permute-start.22 = (bf16[2,16,64,128]{3,2,1,0:T(8,128)(2,1)}, bf16[2,16,64,128]{3,2,1,0:T(8,128)(2,1)}, u32[]{:S(2)}, u32[]{:S(2)}) collective-permute-start(bf16[2,16,64,128]{3,2,1,0:T(8,128)(2,1)} %collective-permute-done.8.refs_8_), channel_id=1, source_target_pairs={{0,8},{1,9},{2,10},{3,11},{4,12},{5,13},{6,14},{7,15},{8,0},{9,1},... | collective-permute-start | bytes 1572872 | tf_op jit(solution)/shard_map/ppermute | solution.py:256
  110.1 13.7 %collective-permute-start.10 = (bf16[2,16,64,128]{3,2,1,0:T(8,128)(2,1)}, bf16[2,16,64,128]{3,2,1,0:T(8,128)(2,1)S(1)}, u32[]{:S(2)}, u32[]{:S(2)}) collective-permute-start(bf16[2,16,64,128]{3,2,1,0:T(8,128)(2,1)} %collective-permute-done.8.refs_8_), channel_id=1, source_target_pairs={{0,1},{1,0},{2,3},{3,2},{4,5},{5,4},{6,7},{7,6},{8,9},{9,8},{10,11... | collective-permute-start | bytes 1572872 | tf_op jit(solution)/shard_map/ppermute | solution.py:256
  110.5 14.8 %collective-permute-start.23 = (bf16[2,16,64,128]{3,2,1,0:T(8,128)(2,1)S(1)}, bf16[2,16,64,128]{3,2,1,0:T(8,128)(2,1)}, u32[]{:S(2)}, u32[]{:S(2)}) collective-permute-start(bf16[2,16,64,128]{3,2,1,0:T(8,128)(2,1)S(1)} %collective-permute-done.15.refs_17_), channel_id=1, source_target_pairs={{0,6},{1,7},{2,4},{3,5},{4,2},{5,3},{6,0},{7,1},{8,14},{9,15},{10,... | collective-permute-start | bytes 1572872 | tf_op jit(solution)/shard_map/ppermute | solution.py:256
  110.7 15.5 %collective-permute-start.19 = (bf16[2,16,64,128]{3,2,1,0:T(8,128)(2,1)S(1)}, bf16[2,16,64,128]{3,2,1,0:T(8,128)(2,1)}, u32[]{:S(2)}, u32[]{:S(2)}) collective-permute-start(bf16[2,16,64,128]{3,2,1,0:T(8,128)(2,1)S(1)} %collective-permute-done.15.refs_17_), channel_id=1, source_target_pairs={{0,2},{1,3},{2,0},{3,1},{4,6},{5,7},{6,4},{7,5},{8,10},{9,11},{10,... | collective-permute-start | bytes 1572872 | tf_op jit(solution)/shard_map/ppermute | solution.py:256
  112.3 14.4 %collective-permute-start.17 = (bf16[2,16,64,128]{3,2,1,0:T(8,128)(2,1)S(1)}, bf16[2,16,64,128]{3,2,1,0:T(8,128)(2,1)S(1)}, u32[]{:S(2)}, u32[]{:S(2)}) collective-permute-start(bf16[2,16,64,128]{3,2,1,0:T(8,128)(2,1)S(1)} %collective-permute-done.15.refs_17_), channel_id=1, source_target_pairs={{0,1},{1,0},{2,3},{3,2},{4,5},{5,4},{6,7},{7,6},{8,9},{9,8},{10,11... | collective-permute-start | bytes 1572872 | tf_op jit(solution)/shard_map/ppermute | solution.py:256
  123.8 14.8 %collective-permute-start.9 = (bf16[2,16,64,128]{3,2,1,0:T(8,128)(2,1)S(1)}, bf16[2,16,64,128]{3,2,1,0:T(8,128)(2,1)}, u32[]{:S(2)}, u32[]{:S(2)}) collective-permute-start(bf16[2,16,64,128]{3,2,1,0:T(8,128)(2,1)S(1)} %collective-permute-done.5.refs_5_), channel_id=1, source_target_pairs={{0,6},{1,7},{2,4},{3,5},{4,2},{5,3},{6,0},{7,1},{8,14},{9,15},{10,... | collective-permute-start | bytes 1572872 | tf_op jit(solution)/shard_map/ppermute | solution.py:256
  125.3 14.2 %collective-permute-start.7 = (bf16[2,16,64,128]{3,2,1,0:T(8,128)(2,1)S(1)}, bf16[2,16,64,128]{3,2,1,0:T(8,128)(2,1)S(1)}, u32[]{:S(2)}, u32[]{:S(2)}) collective-permute-start(bf16[2,16,64,128]{3,2,1,0:T(8,128)(2,1)S(1)} %collective-permute-done.5.refs_5_), channel_id=1, source_target_pairs={{0,1},{1,0},{2,3},{3,2},{4,5},{5,4},{6,7},{7,6},{8,9},{9,8},{10,11... | collective-permute-start | bytes 1572872 | tf_op jit(solution)/shard_map/ppermute | solution.py:256
  126.2 13.9 %collective-permute-start.24 = (bf16[2,16,64,128]{3,2,1,0:T(8,128)(2,1)}, bf16[2,16,64,128]{3,2,1,0:T(8,128)(2,1)}, u32[]{:S(2)}, u32[]{:S(2)}) collective-permute-start(bf16[2,16,64,128]{3,2,1,0:T(8,128)(2,1)} %collective-permute-done.23.refs_29_), channel_id=1, source_target_pairs={{0,2},{1,3},{2,0},{3,1},{4,6},{5,7},{6,4},{7,5},{8,10},{9,11},{10,... | collective-permute-start | bytes 1572872 | tf_op jit(solution)/shard_map/ppermute | solution.py:256
  126.7 14.9 %collective-permute-start.25 = (bf16[2,16,64,128]{3,2,1,0:T(8,128)(2,1)}, bf16[2,16,64,128]{3,2,1,0:T(8,128)(2,1)}, u32[]{:S(2)}, u32[]{:S(2)}) collective-permute-start(bf16[2,16,64,128]{3,2,1,0:T(8,128)(2,1)} %collective-permute-done.22.refs_24_), channel_id=1, source_target_pairs={{0,1},{1,0},{2,3},{3,2},{4,5},{5,4},{6,7},{7,6},{8,9},{9,8},{10,11... | collective-permute-start | bytes 1572872 | tf_op jit(solution)/shard_map/ppermute | solution.py:256
  127.1 14.5 %collective-permute-start.29 = (bf16[2,16,64,128]{3,2,1,0:T(8,128)(2,1)}, bf16[2,16,64,128]{3,2,1,0:T(8,128)(2,1)}, u32[]{:S(2)}, u32[]{:S(2)}) collective-permute-start(bf16[2,16,64,128]{3,2,1,0:T(8,128)(2,1)} %collective-permute-done.23.refs_29_), channel_id=1, source_target_pairs={{0,1},{1,0},{2,3},{3,2},{4,5},{5,4},{6,7},{7,6},{8,9},{9,8},{10,11... | collective-permute-start | bytes 1572872 | tf_op jit(solution)/shard_map/ppermute | solution.py:256
  (24 other events, 754.4 us)

commit v3 on v2

--- a/solution.py
+++ b/solution.py
@@ -55,10 +55,14 @@
         table_copies.append(
             pltpu.make_async_copy(table_hbm.at[:, :, samples], table.at[:, :, samples], table_sems.at[kb])
         )
-    for kb in range(BLOCKS):
+
+    def fetch(kb):
         x_copies[2 * kb].start()
         x_copies[2 * kb + 1].start()
         table_copies[kb].start()
+
+    fetch(0)
+    fetch(1)
 
     def fir(kb, p, tile, fold):
         n0 = pl.multiple_of(kb * BLOCK + tile * 128, 128)
@@ -98,19 +102,20 @@
         return jnp.dot(left, right, preferred_element_type=jnp.float32)
 
     def stage(kb, fold_in, fold_out, first=False):
-        def unit(u, carry):
-            a, b = u // 2, u % 2
+        def unit(a, carry):
             if fold_out is not None:
-                fir(kb + 1, a, b, fold_out)
-            if fold_in is not None:
-                value = product(kb, a, b, fold_in)
-                if first:
-                    total[a, b] = value
-                else:
-                    total[a, b] += value
+                fir(kb + 1, a, 0, fold_out)
+                fir(kb + 1, a, 1, fold_out)
+            for b in range(2):
+                if fold_in is not None:
+                    value = product(kb, a, b, fold_in)
+                    if first:
+                        total[a, b] = value
+                    else:
+                        total[a, b] += value
             return carry
 
-        lax.fori_loop(0, 4, unit, 0)
+        lax.fori_loop(0, 2, unit, 0)
 
     def arrive(kb):
         x_copies[2 * kb].wait()
@@ -118,6 +123,8 @@
         table_copies[kb].wait()
 
     arrive(0)
+    for kb in range(2, BLOCKS):
+        fetch(kb)
     stage(-1, None, fold_a)
     arrive(1)
     stage(0, fold_a, fold_b, first=True)
@@ -184,128 +191,195 @@
 NJ = 2
 
 
-def correlate_kernel(blk_ref, scale_ref, *refs):
-    sources, (out_ref, held, sems) = refs[:32], refs[32:]
+STEPS_Z = (0, 1, 3, 2)
+
+
+def correlate_kernel(far, places, place_ref, scale_ref, *refs):
+    out_ref, token_ref, staged, sems = refs[-4:]
     step, steps = pl.program_id(0), pl.num_programs(0)
-    blk = blk_ref[0]
-
-    def copies(at):
-        slot = at % 2
-        made = []
-        for m in range(16):
-            row = pl.multiple_of((blk ^ m) * 64, 64)
-            for part in range(2):
-                made.append(
-                    pltpu.make_async_copy(
-                        sources[2 * m + part].at[:, pl.ds(at * NJ, NJ)],
-                        held.at[slot, :, :, pl.ds(row, 64), pl.ds(part * 128, 128)],
-                        sems.at[slot, 2 * m + part],
-                    )
-                )
-        return made
-
-    @pl.when(step == 0)
+    slot = step % 2
+    first_column = (place_ref[0] ^ far) * 512
+    place_z = place_ref[1]
+    at_core_0 = place_ref[2] == 0
+    token_ref[...] = jnp.zeros_like(token_ref)
+
+    def copy(at):
+        column = pl.multiple_of(first_column, 512)
+        return pltpu.make_async_copy(
+            staged.at[at % 2],
+            out_ref.at[pl.ds(at * (2 * NJ), 2 * NJ), :, :, pl.ds(column, 512)],
+            sems.at[at % 2],
+        )
+
+    @pl.when(step >= 2)
     def _():
-        for copy in copies(step):
-            copy.start()
-
-    @pl.when(step + 1 < steps)
-    def _():
-        for copy in copies(step + 1):
-            copy.start()
-
-    for copy in copies(step):
-        copy.wait()
-    slot = step % 2
-    own = pl.ds(pl.multiple_of(blk * 64, 64), 64)
+        copy(step - 2).wait()
+
     lane = lax.broadcasted_iota(jnp.int32, (64, 128), 1)
     sign = jnp.where(lane < 64, 1.0, -1.0)
     for cls in range(2):
         for jj in range(NJ):
-            mine = held[slot, cls, jj, own, :]
-            wide = mine.astype(jnp.float32)
-            turned = [pltpu.roll(wide[:, h : h + 128], 64, 1) * sign for h in (0, 128)]
-            left = jnp.concatenate([mine, jnp.concatenate(turned, axis=1).astype(jnp.bfloat16)], axis=0)
-            total = lax.dot_general(
-                left, held[slot, cls, jj], (((1,), (1,)), ((), ())), preferred_element_type=jnp.float32
-            )
+
+            def load(place):
+                ref, *lead = place
+                return refs[ref][(*lead, cls, jj)]
+
+            own = [load(place) for place in places[:2]]
+            turned = [(pltpu.roll(o.astype(jnp.float32), 64, 1) * sign).astype(jnp.bfloat16) for o in own]
+            left = jnp.concatenate([jnp.concatenate(own, axis=1), jnp.concatenate(turned, axis=1)], axis=0)
             channel = 2 * jj + cls
-            total = (total * scale_ref[step * (2 * NJ) + channel]).astype(jnp.bfloat16)
-            out_ref[channel, 0] = total[:64]
-            out_ref[channel, 1] = total[64:]
-
-
-def correlate(blk, scale, sources):
+            scale = scale_ref[step * (2 * NJ) + channel]
+            for half in range(2):
+                rows = []
+                for k in (2 * half, 2 * half + 1):
+                    same_p, other_p, same_q, other_q = [load(place) for place in places[2 + 4 * k : 6 + 4 * k]]
+                    same = jnp.concatenate([same_p, same_q], axis=1)
+                    other = jnp.concatenate([other_p, other_q], axis=1)
+                    rows += [jnp.where(at_core_0, same, other), jnp.where(at_core_0, other, same)]
+                right = jnp.concatenate(rows, axis=0)
+                total = lax.dot_general(
+                    left, right, (((1,), (1,)), ((), ())), preferred_element_type=jnp.float32
+                )
+                total = (total * scale).astype(jnp.bfloat16)
+                for k in (2 * half, 2 * half + 1):
+                    to = pl.ds(pl.multiple_of((place_z ^ STEPS_Z[k]) * 128, 128), 128)
+                    lanes = slice(128 * (k % 2), 128 * (k % 2) + 128)
+                    for plane in range(2):
+                        staged[slot, channel, plane, :, to] = total[64 * plane : 64 * plane + 64, lanes]
+    copy(step).start()
+
+    @pl.when(step == steps - 1)
+    def _():
+        for at in (steps - 2, steps - 1):
+            copy(at).wait()
+
+
+def block_index(lead, step):
+    return (0,) * lead + (step, 0, 0)
+
+
+def correlate(far, place, scale, parts, token, out=None):
+    operands, places = [], []
+    for part in parts:
+        array, *lead = part if isinstance(part, tuple) else (part,)
+        known = [at for at, operand in enumerate(operands) if operand is array]
+        if not known:
+            operands.append(array)
+        places.append((known[0] if known else len(operands) - 1, *lead))
+    specs = [pl.BlockSpec(memory_space=pltpu.SMEM)] * 2
+    for block in operands:
+        lead = block.shape[:-4]
+        specs.append(pl.BlockSpec((*lead, 2, NJ, 64, 128), functools.partial(block_index, len(lead) + 1)))
+    specs.append(pl.BlockSpec(memory_space=pltpu.HBM))
+    operands.append(token)
+    aliases = {}
+    if out is not None:
+        specs.append(pl.BlockSpec(memory_space=pltpu.HBM))
+        aliases = {2 + len(operands): 0}
+        operands.append(out)
     return pl.pallas_call(
-        correlate_kernel,
-        out_shape=jax.ShapeDtypeStruct((32, 2, 64, 1024), jnp.bfloat16),
+        functools.partial(correlate_kernel, far, places),
+        out_shape=(
+            jax.ShapeDtypeStruct((32, 2, 64, 1024), jnp.bfloat16),
+            jax.ShapeDtypeStruct((8, 128), jnp.float32),
+        ),
         grid=(16 // NJ,),
-        in_specs=[pl.BlockSpec(memory_space=pltpu.SMEM)] * 2 + [pl.BlockSpec(memory_space=pltpu.HBM)] * 32,
-        out_specs=pl.BlockSpec((2 * NJ, 2, 64, 1024), lambda s: (s, 0, 0, 0)),
+        in_specs=specs,
+        out_specs=(pl.BlockSpec(memory_space=pltpu.HBM), pl.BlockSpec((8, 128), lambda s: (0, 0))),
+        input_output_aliases=aliases,
         scratch_shapes=[
-            pltpu.VMEM((2, 2, NJ, 1024, 256), jnp.bfloat16),
-            pltpu.SemaphoreType.DMA((2, 32)),
+            pltpu.VMEM((2, 2 * NJ, 2, 64, 512), jnp.bfloat16),
+            pltpu.SemaphoreType.DMA((2,)),
         ],
         compiler_params=pltpu.CompilerParams(vmem_limit_bytes=56 * 1024 * 1024),
-        cost_estimate=pl.CostEstimate(flops=2_200_000_000, bytes_accessed=25_000_000, transcendentals=0),
+        cost_estimate=pl.CostEstimate(flops=2_000_000_000, bytes_accessed=13_000_000, transcendentals=0),
         name="correlate",
-    )(blk, scale, *sources)
-
-
-def send(array, bits):
-    return lax.ppermute(array, "blk", [(b, b ^ bits) for b in range(16)])
-
-
-X2, Z1, Z3, CORE = 8, 2, 6, 1
+    )(place, scale, *operands)
+
+
+class Block:
+    def __init__(self, value):
+        self.value = value
+
+
+def together(*blocks):
+    values = lax.optimization_barrier(tuple(block.value for block in blocks))
+    for block, value in zip(blocks, values):
+        block.value = value
+
+
+def along_x(block):
+    return Block(lax.ppermute(block.value, "x_hi", [(0, 1), (1, 0)]))
+
+
+def along_z(block, bits):
+    return Block(lax.ppermute(block.value, "z", [(z, z ^ bits) for z in range(4)]))
+
+
+def to_core(*blocks):
+    return lax.ppermute(jnp.stack([block.value for block in blocks]), "core", [(0, 1), (1, 0)])
 
 
 def turn(chunk):
-    got = lax.all_to_all(chunk, "chan", split_axis=0, concat_axis=0, tiled=True)
+    got = lax.all_to_all(chunk, ("y", "x_lo"), split_axis=0, concat_axis=0, tiled=True)
     return got.transpose(1, 2, 0, 3, 4).reshape(2, 16, 64, 128)
 
 
 def on_device(voltages, fir_taps, station_flags, bin_offsets):
-    chan, blk = lax.axis_index("chan"), lax.axis_index("blk")
+    chan = lax.axis_index(("y", "x_lo"))
+    x_hi, z, core = [lax.axis_index(axis) for axis in ("x_hi", "z", "core")]
+    blk = (x_hi * 4 + z) * 2 + core
     flags = jnp.repeat(station_flags, 2).astype(jnp.float32)
     weight = lax.dynamic_slice_in_dim(flags, blk * 64 + chan * 8, 8, 0) / math.sqrt(2.0 * NFFT)
     weight = jnp.broadcast_to(weight[:, None], (8, 128))
     scales = jnp.exp2(-bin_offsets.astype(jnp.float32)) / FRAMES
     scale = lax.dynamic_slice_in_dim(scales, chan * 32, 32, 0)
     tables = jnp.asarray(dft_tables())
-
     planes = voltages.reshape(2, 8, FRAMES + TAPS - 1, NFFT).transpose(0, 2, 1, 3)
 
-    first = turn(spectra(0, planes, fir_taps, tables, weight))
-    weight, first = lax.optimization_barrier((weight, first))
-    later = spectra(CHUNK, planes, fir_taps, tables, weight)
-    one = {0: first}
-    for bits in (Z1, Z3, X2):
-        one[bits] = send(first, bits)
-    later, one[Z1], one[Z3], one[X2] = lax.optimization_barrier((later, one[Z1], one[Z3], one[X2]))
-    one[Z1 ^ Z3] = send(one[Z3], Z1)
-    one[X2 ^ Z1] = send(one[Z1], X2)
-    one[X2 ^ Z3] = send(one[Z3], X2)
-    one[X2 ^ Z1 ^ Z3] = send(one[Z1 ^ Z3], X2)
-    second = turn(later)
-    two = {0: second}
-    two[X2] = send(second, X2)
-    for m in (0, X2):
-        two[m ^ Z1] = send(two[m], Z1)
-        two[m ^ Z3] = send(two[m], Z3)
-    two[Z1 ^ Z3] = send(two[Z1], Z3)
-    two[X2 ^ Z1 ^ Z3] = send(two[X2 ^ Z3], Z1)
-    for part in (one, two):
-        for m in list(part):
-            part[m ^ CORE] = send(part[m], CORE)
-    sources = []
-    for m in range(16):
-        sources += [one[m], two[m]]
-    return correlate(blk.astype(jnp.int32).reshape(1), scale, sources)
+    place = jnp.stack([x_hi, z, core]).astype(jnp.int32)
+    p = {0: Block(turn(spectra(0, planes, fir_taps, tables, weight)))}
+    weight = Block(weight)
+    together(weight, p[0])
+    spectra_q = Block(spectra(CHUNK, planes, fir_taps, tables, weight.value))
+    xp, q, xq = {0: along_x(p[0])}, {}, {}
+    p[1], p[3] = along_z(p[0], 1), along_z(p[0], 3)
+    together(spectra_q, xp[0], p[1], p[3])
+    p[2], xp[3] = along_z(p[3], 1), along_z(xp[0], 3)
+    q[0] = Block(turn(spectra_q.value))
+    together(q[0], p[2], xp[3])
+    xq[0] = along_x(q[0])
+    q[1], q[3] = along_z(q[0], 1), along_z(q[0], 3)
+    p_other = to_core(*[p[k] for k in STEPS_Z])
+    together(xq[0], q[1], q[3])
+    xq[1] = along_x(q[1])
+    xp[2], q[2] = along_z(xp[3], 1), along_z(q[1], 3)
+    far_a = to_core(xp[0], xp[3], xq[0])
+    together(xq[1], xp[2], q[2])
+    xq[3] = along_x(q[3])
+    xp[1], xq[2] = along_z(xp[0], 1), along_z(xq[1], 3)
+    q_other = to_core(*[q[k] for k in STEPS_Z])
+    far_b = to_core(xp[2], xq[1])
+    token = Block(jnp.zeros((8, 128), jnp.float32))
+    parts = [p[0].value, q[0].value]
+    for at, k in enumerate(STEPS_Z):
+        parts += [p[k].value, (p_other, at), q[k].value, (q_other, at)]
+    out, token.value = correlate(0, place, scale, parts, token.value)
+    together(token, xq[3], xp[1], xq[2])
+    far_c = to_core(xp[1], xq[3], xq[2])
+    parts = [p[0].value, q[0].value]
+    parts += [xp[0].value, (far_a, 0), xq[0].value, (far_a, 2)]
+    parts += [xp[1].value, (far_c, 0), xq[1].value, (far_b, 1)]
+    parts += [xp[3].value, (far_a, 1), xq[3].value, (far_c, 1)]
+    parts += [xp[2].value, (far_b, 0), xq[2].value, (far_c, 2)]
+    return correlate(1, place, scale, parts, token.value, out)[0]
 
 
 def solution(mesh):
-    in_specs = (P(None, "blk", "chan", None), P(), P(), P())
-    out_specs = P("chan", None, "blk", None)
+    names = ("y", "x_lo", "x_hi", "z", "core")
+    mesh = jax.sharding.Mesh(mesh.devices.reshape(4, 2, 2, 4, 2), names)
+    in_specs = (P(None, ("x_hi", "z", "core"), ("y", "x_lo"), None), P(), P(), P())
+    out_specs = P(("y", "x_lo"), None, ("x_hi", "z", "core"), None)
     return jax.shard_map(
         on_device, mesh=mesh, in_specs=in_specs, out_specs=out_specs, check_vma=False
     )

time: 158 us -> 144 us (0.911)
  waiting for transfers between devices: 54.2 us -> 24.9 us
  other arithmetic: 0.77 us -> 9.86 us
  local copies, waits for them, and re-layouts: 2.14 us -> 4.47 us
  starting transfers between devices: 34.1 us -> 36.1 us
    ppermute x30 -> x19, waiting for transfers between devices: 49.5 us -> 18.9 us  [the longest x10 14 us: along_z(): lax.ppermute(block.value, 'z', [(z, z ^ bits) for z in range(4)])]
    another operation x0 -> x6, other arithmetic: none -> 9.09 us  [the longest x5 8.49 us: to_core(): jnp.stack([block.value for block in blocks])]
    pallas_call x1 -> x2, Pallas kernels: 14.2 us -> 19.5 us  [correlate(): pl.pallas_call(functools.partial(correlate_kernel, far, places), out_shap...]
    pallas_call x2, Pallas kernels: 36.4 us -> 32.6 us  [spectra(): pl.pallas_call(functools.partial(spectra_kernel, first_frame), out_shape=...]
    ppermute x30 -> x19, starting transfers between devices: 30.6 us -> 32.6 us  [the longest x5 19.1 us: to_core(): lax.ppermute(jnp.stack([block.value for block in blocks]), 'core', [(0, 1...]
    unnamed x34 -> x32, local copies, waits for them, and re-layouts: 0.27 us -> 2.04 us
  transfers between devices with their start and end apart: 31 -> 20, of which waited for: 10 -> 8; matrix products, arithmetic and copies ran while one was open for 1% -> 7% of each run, Pallas kernels for 12% -> 18%
where the time goes in v3:
time: 144 us; the launch traced here: 143 us
  Pallas kernels  52.1 us (36%)
  starting transfers between devices  36.1 us (25%)
  waiting for transfers between devices  24.9 us (17%)
  blocking collectives  15.2 us (11%)
  other arithmetic  9.86 us (7%)
  local copies, waits for them, and re-layouts  4.47 us (3%)
    pallas_call x2, Pallas kernels, spectra(): pl.pallas_call(functools.partial(spectra_kernel, first_frame), out_shape=...  32.6 us
    pallas_call x2, Pallas kernels, correlate(): pl.pallas_call(functools.partial(correlate_kernel, far, places), out_shap...  19.5 us
    ppermute x5, starting transfers between devices, to_core(): lax.ppermute(jnp.stack([block.value for block in blocks]), 'core', [(0, 1...  19.1 us
    all_to_all x1, blocking collectives, turn(): lax.all_to_all(chunk, ('y', 'x_lo'), split_axis=0, concat_axis=0, tiled=T...  15.2 us
    ppermute x10, waiting for transfers between devices, along_z(): lax.ppermute(block.value, 'z', [(z, z ^ bits) for z in range(4)])  14 us
    ppermute x10, starting transfers between devices, along_z(): lax.ppermute(block.value, 'z', [(z, z ^ bits) for z in range(4)])  9.43 us
    another operation x5, other arithmetic, to_core(): jnp.stack([block.value for block in blocks])  8.49 us
    all_to_all x1, waiting for transfers between devices, turn(): lax.all_to_all(chunk, ('y', 'x_lo'), split_axis=0, concat_axis=0, tiled=T...  5.94 us
  transfers between devices with their start and end apart: 20, of which 8 were waited for; matrix products, arithmetic and copies ran while one was open for 7% of the time, Pallas kernels for 18%

profile of v3, /device:TPU:1, one launch (start us, length us, event | category | flops | bytes accessed | tf_op | source)
XLA Modules:
  0.0 143.0 jit_solution(13559672565760402285)
XLA Ops:
  1.7 16.3 %spectra.2 = bf16[8,2,16,8,128]{4,3,2,1,0:T(8,128)(2,1)} custom-call(bf16[2,131,8,4096]{3,2,1,0:T(8,128)(2,1)} %bitcast.42, f32[4,4096]{1,0:T(4,128)} %taps_ref.3, bf16[2,2,2048,256]{3,2,1,0:T(8,128)(2,1)} %constant.47.clone.table_hbm, f32[8,128]{1,0:T(8,128)} %broadcast_in_dim.13.weight_ref), custom_call_target="tpu_custom_call" | custom-call | flops 6499999744 | bytes 14000000 | tf_op jit(solution)/shard_map/spectra/pallas_call | solution.py:164
  18.0 15.2 %all_to_all.10 = bf16[8,2,16,8,128]{4,3,2,1,0:T(8,128)(2,1)S(1)} all-to-all(bf16[8,2,16,8,128]{4,3,2,1,0:T(8,128)(2,1)} %spectra.2), channel_id=1, replica_groups=mesh['y'=4,'x_lo'=2,'x_hi'=2,'z'=4,'core'=2] {'y','x_lo'}, dimensions={0} | all-to-all | bytes 1048576 | tf_op jit(solution)/shard_map/all_to_all | solution.py:324
  33.4 3.8 %collective-permute-start.2 = (bf16[2,16,64,128]{3,2,1,0:T(8,128)(2,1)S(1)}, bf16[2,16,64,128]{3,2,1,0:T(8,128)(2,1)S(1)}, u32[]{:S(2)}, u32[]{:S(2)}) collective-permute-start(bf16[2,16,64,128]{3,2,1,0:T(8,128)(2,1)S(1)} %copy_bitcast_fusion.1.refs_0_), channel_id=1, source_target_pairs={{0,6},{2,4},{4,2},{6,0},{1,7},{3,5},{5,3},{7,1},{8,14},{10,12},{12... | collective-permute-start | bytes 1572872 | tf_op jit(solution)/shard_map/ppermute | solution.py:316
  37.2 2.5 %collective-permute-start = (bf16[2,16,64,128]{3,2,1,0:T(8,128)(2,1)S(1)}, bf16[2,16,64,128]{3,2,1,0:T(8,128)(2,1)S(1)}, u32[]{:S(2)}, u32[]{:S(2)}) collective-permute-start(bf16[2,16,64,128]{3,2,1,0:T(8,128)(2,1)S(1)} %copy_bitcast_fusion.1.refs_0_), channel_id=1, source_target_pairs={{0,8},{8,0},{1,9},{9,1},{2,10},{10,2},{3,11},{11,3},{4,12},{12,4},... | collective-permute-start | bytes 1572872 | tf_op jit(solution)/shard_map/ppermute | solution.py:312
  39.6 16.3 %spectra.3 = bf16[8,2,16,8,128]{4,3,2,1,0:T(8,128)(2,1)} custom-call(bf16[2,131,8,4096]{3,2,1,0:T(8,128)(2,1)} %bitcast.43, f32[4,4096]{1,0:T(4,128)} %taps_ref.3, bf16[2,2,2048,256]{3,2,1,0:T(8,128)(2,1)} %constant.47.clone.table_hbm, f32[8,128]{1,0:T(8,128)} %broadcast_in_dim.13.weight_ref), custom_call_target="tpu_custom_call" | custom-call | flops 6499999744 | bytes 14000000 | tf_op jit(solution)/shard_map/spectra/pallas_call | solution.py:164
  56.0 3.5 %all-to-all-start.1 = ((bf16[8,2,16,8,128]{4,3,2,1,0:T(8,128)(2,1)}), bf16[8,2,16,8,128]{4,3,2,1,0:T(8,128)(2,1)S(1)}, u32[]{:S(2)}, u32[]{:S(2)}) async-start(bf16[8,2,16,8,128]{4,3,2,1,0:T(8,128)(2,1)} %spectra.3), calls=%async_computation.1 | async-start | bytes 1048576 | tf_op jit(solution)/shard_map/all_to_all | solution.py:324
  59.5 1.5 %collective-permute-start.3 = (bf16[2,16,64,128]{3,2,1,0:T(8,128)(2,1)S(1)}, bf16[2,16,64,128]{3,2,1,0:T(8,128)(2,1)S(1)}, u32[]{:S(2)}, u32[]{:S(2)}) collective-permute-start(bf16[2,16,64,128]{3,2,1,0:T(8,128)(2,1)S(1)} %collective-permute-done.2.refs_6_), channel_id=1, source_target_pairs={{0,2},{2,0},{4,6},{6,4},{1,3},{3,1},{5,7},{7,5},{8,10},{10,8},{12,... | collective-permute-start | bytes 1572872 | tf_op jit(solution)/shard_map/ppermute | solution.py:316
  61.2 5.9 %all-to-all-done.1 = bf16[8,2,16,8,128]{4,3,2,1,0:T(8,128)(2,1)S(1)} async-done(((bf16[8,2,16,8,128]{4,3,2,1,0:T(8,128)(2,1)}), bf16[8,2,16,8,128]{4,3,2,1,0:T(8,128)(2,1)S(1)}, u32[]{:S(2)}, u32[]{:S(2)}) %all-to-all-start.1) | async-done | bytes 524320 | tf_op jit(solution)/shard_map/all_to_all | solution.py:324
  67.3 3.4 %collective-permute-done.3.refs_8_ = bf16[2,16,64,128]{3,2,1,0:T(8,128)(2,1)S(1)} collective-permute-done((bf16[2,16,64,128]{3,2,1,0:T(8,128)(2,1)S(1)}, bf16[2,16,64,128]{3,2,1,0:T(8,128)(2,1)S(1)}, u32[]{:S(2)}, u32[]{:S(2)}) %collective-permute-start.3) | collective-permute-done | bytes 524320 | tf_op jit(solution)/shard_map/ppermute | solution.py:316
  70.7 2.1 %collective-permute-done.4.refs_9_ = bf16[2,16,64,128]{3,2,1,0:T(8,128)(2,1)} collective-permute-done((bf16[2,16,64,128]{3,2,1,0:T(8,128)(2,1)S(1)}, bf16[2,16,64,128]{3,2,1,0:T(8,128)(2,1)}, u32[]{:S(2)}, u32[]{:S(2)}) %collective-permute-start.4) | collective-permute-done | bytes 524320 | tf_op jit(solution)/shard_map/ppermute | solution.py:316
  73.7 1.5 %collective-permute-start.11 = (bf16[2,16,64,128]{3,2,1,0:T(8,128)(2,1)}, bf16[2,16,64,128]{3,2,1,0:T(8,128)(2,1)S(1)}, u32[]{:S(2)}, u32[]{:S(2)}) collective-permute-start(bf16[2,16,64,128]{3,2,1,0:T(8,128)(2,1)} %collective-permute-done.4.refs_9_), channel_id=1, source_target_pairs={{0,2},{2,0},{4,6},{6,4},{1,3},{3,1},{5,7},{7,5},{8,10},{10,8},{12,... | collective-permute-start | bytes 1572872 | tf_op jit(solution)/shard_map/ppermute | solution.py:316
  75.2 8.5 %collective-permute-done.7.refs_7_ = bf16[2,16,64,128]{3,2,1,0:T(8,128)(2,1)} collective-permute-done((bf16[2,16,64,128]{3,2,1,0:T(8,128)(2,1)S(1)}, bf16[2,16,64,128]{3,2,1,0:T(8,128)(2,1)}, u32[]{:S(2)}, u32[]{:S(2)}) %collective-permute-start.7) | collective-permute-done | bytes 524320 | tf_op jit(solution)/shard_map/ppermute | solution.py:316
  84.2 2.0 %collective-permute-start.12 = (bf16[2,16,64,128]{3,2,1,0:T(8,128)(2,1)S(1)}, bf16[2,16,64,128]{3,2,1,0:T(8,128)(2,1)S(1)}, u32[]{:S(2)}, u32[]{:S(2)}) collective-permute-start(bf16[2,16,64,128]{3,2,1,0:T(8,128)(2,1)S(1)} %collective-permute-done.6.refs_5_), channel_id=1, source_target_pairs={{0,6},{2,4},{4,2},{6,0},{1,7},{3,5},{5,3},{7,1},{8,14},{10,12},{12... | collective-permute-start | bytes 1572872 | tf_op jit(solution)/shard_map/ppermute | solution.py:316
  86.9 1.6 %pad_maximum_fusion = bf16[4,2,16,64,128]{4,3,2,1,0:T(8,128)(2,1)S(1)} fusion(bf16[1,2,16,64,128]{4,3,2,1,0:T(8,128)(2,1)} %bitcast.39, bf16[1,2,16,64,128]{4,3,2,1,0:T(8,128)(2,1)} %bitcast.37, bf16[1,2,16,64,128]{4,3,2,1,0:T(8,128)(2,1)} %bitcast.38, bf16[1,2,16,64,128]{4,3,2,1,0:T(8,128)(2,1)S(1)} %bitcast.32), kind=kLoop, calls=%fused_computation | loop fusion | flops 3145728 | bytes 4194304 | tf_op jit(solution)/shard_map/stack | solution.py:320
  88.5 8.9 %collective-permute-start.9 = (bf16[4,2,16,64,128]{4,3,2,1,0:T(8,128)(2,1)S(1)}, bf16[4,2,16,64,128]{4,3,2,1,0:T(8,128)(2,1)}, u32[]{:S(2)}, u32[]{:S(2)}) collective-permute-start(bf16[4,2,16,64,128]{4,3,2,1,0:T(8,128)(2,1)S(1)} %pad_maximum_fusion), channel_id=1, source_target_pairs={{0,1},{1,0},{2,3},{3,2},{4,5},{5,4},{6,7},{7,6},{8,9},{9,8},{10,11... | collective-permute-start | bytes 6291464 | tf_op jit(solution)/shard_map/ppermute | solution.py:320
  97.5 3.0 %pad_maximum_fusion.1 = bf16[4,2,16,64,128]{4,3,2,1,0:T(8,128)(2,1)} fusion(bf16[1,2,16,64,128]{4,3,2,1,0:T(8,128)(2,1)S(1)} %bitcast.41, bf16[1,2,16,64,128]{4,3,2,1,0:T(8,128)(2,1)} %bitcast.19, bf16[1,2,16,64,128]{4,3,2,1,0:T(8,128)(2,1)S(1)} %bitcast.40, bf16[1,2,16,64,128]{4,3,2,1,0:T(8,128)(2,1)S(1)} %bitcast.33), kind=kLoop, calls=%fused_computation.1 | loop fusion | flops 3145728 | bytes 4194304 | tf_op jit(solution)/shard_map/stack | solution.py:320
  100.5 7.9 %collective-permute-start.13 = (bf16[4,2,16,64,128]{4,3,2,1,0:T(8,128)(2,1)}, bf16[4,2,16,64,128]{4,3,2,1,0:T(8,128)(2,1)}, u32[]{:S(2)}, u32[]{:S(2)}) collective-permute-start(bf16[4,2,16,64,128]{4,3,2,1,0:T(8,128)(2,1)} %pad_maximum_fusion.1), channel_id=1, source_target_pairs={{0,1},{1,0},{2,3},{3,2},{4,5},{5,4},{6,7},{7,6},{8,9},{9,8},{10,11... | collective-permute-start | bytes 6291464 | tf_op jit(solution)/shard_map/ppermute | solution.py:320
  110.3 1.2 pad_maximum_fusion.2
  113.1 9.6 %correlate.2 = (bf16[32,2,64,1024]{3,2,1,0:T(8,128)(2,1)}, f32[8,128]{1,0:T(8,128)}) custom-call(s32[3]{0:T(128)} %pad_add_fusion.place_ref, f32[32]{0:T(128)} %dynamic_slice.6.scale_ref, bf16[2,16,64,128]{3,2,1,0:T(8,128)(2,1)} %copy-done, bf16[2,16,64,128]{3,2,1,0:T(8,128)(2,1)} %copy-done.1, bf16[4,2,16,64,128]{4,3,2,1,0:T(8,128)(2,1)} %collective-permute-done.9.refs_2_, ...), custom_call_target="tpu_custom_call" | custom-call | flops 2000000000 | bytes 13000000 | tf_op jit(solution)/shard_map/correlate/pallas_call | solution.py:280
  123.6 1.5 %pad_maximum_fusion.3 = bf16[3,2,16,64,128]{4,3,2,1,0:T(8,128)(2,1)S(1)} fusion(bf16[1,2,16,64,128]{4,3,2,1,0:T(8,128)(2,1)} %bitcast.23, bf16[1,2,16,64,128]{4,3,2,1,0:T(8,128)(2,1)} %bitcast.22, bf16[1,2,16,64,128]{4,3,2,1,0:T(8,128)(2,1)} %bitcast.21), kind=kLoop, calls=%fused_computation.3 | loop fusion | flops 1572864 | bytes 3145728 | tf_op jit(solution)/shard_map/stack | solution.py:320
  125.1 1.3 collective-permute-start.17
  126.4 1.1 pad_maximum_fusion.4
  127.7 3.3 %collective-permute-done.18.refs_8_ = bf16[2,2,16,64,128]{4,3,2,1,0:T(8,128)(2,1)S(1)} collective-permute-done((bf16[2,2,16,64,128]{4,3,2,1,0:T(8,128)(2,1)S(1)}, bf16[2,2,16,64,128]{4,3,2,1,0:T(8,128)(2,1)S(1)}, u32[]{:S(2)}, u32[]{:S(2)}) %collective-permute-start.18) | collective-permute-done | bytes 1048608 | tf_op jit(solution)/shard_map/ppermute | solution.py:320
  133.0 9.9 %correlate.3 = (bf16[32,2,64,1024]{3,2,1,0:T(8,128)(2,1)}, f32[8,128]{1,0:T(8,128)}) custom-call(s32[3]{0:T(128)} %pad_add_fusion.place_ref, f32[32]{0:T(128)} %dynamic_slice.6.scale_ref, bf16[2,16,64,128]{3,2,1,0:T(8,128)(2,1)} %copy-done, bf16[2,16,64,128]{3,2,1,0:T(8,128)(2,1)} %copy-done.1, ...), custom_call_target="tpu_custom_call", output_to_operand_aliasing={{0}: (16, {})} | custom-call | flops 2000000000 | bytes 13000000 | tf_op jit(solution)/shard_map/correlate/pallas_call | solution.py:280
  (69 shorter events, 10.6 us)
Async XLA Ops:
  33.3 53.5 %copy-start = (bf16[2,16,64,128]{3,2,1,0:T(8,128)(2,1)}, bf16[2,16,64,128]{3,2,1,0:T(8,128)(2,1)S(1)}, u32[]{:S(2)}) copy-start(bf16[2,16,64,128]{3,2,1,0:T(8,128)(2,1)S(1)} %copy_bitcast_fusion.1.refs_0_) | copy-start | bytes 1572868
  33.4 22.6 %collective-permute-start.2 = (bf16[2,16,64,128]{3,2,1,0:T(8,128)(2,1)S(1)}, bf16[2,16,64,128]{3,2,1,0:T(8,128)(2,1)S(1)}, u32[]{:S(2)}, u32[]{:S(2)}) collective-permute-start(bf16[2,16,64,128]{3,2,1,0:T(8,128)(2,1)S(1)} %copy_bitcast_fusion.1.refs_0_), channel_id=1, source_target_pairs={{0,6},{2,4},{4,2},{6,0},{1,7},{3,5},{5,3},{7,1},{8,14},{10,12},{12... | collective-permute-start | bytes 1572872 | tf_op jit(solution)/shard_map/ppermute | solution.py:316
  37.2 18.8 %collective-permute-start.1 = (bf16[2,16,64,128]{3,2,1,0:T(8,128)(2,1)S(1)}, bf16[2,16,64,128]{3,2,1,0:T(8,128)(2,1)S(1)}, u32[]{:S(2)}, u32[]{:S(2)}) collective-permute-start(bf16[2,16,64,128]{3,2,1,0:T(8,128)(2,1)S(1)} %copy_bitcast_fusion.1.refs_0_), channel_id=1, source_target_pairs={{0,2},{2,0},{4,6},{6,4},{1,3},{3,1},{5,7},{7,5},{8,10},{10,8},{12,... | collective-permute-start | bytes 1572872 | tf_op jit(solution)/shard_map/ppermute | solution.py:316
  37.2 18.8 %collective-permute-start = (bf16[2,16,64,128]{3,2,1,0:T(8,128)(2,1)S(1)}, bf16[2,16,64,128]{3,2,1,0:T(8,128)(2,1)S(1)}, u32[]{:S(2)}, u32[]{:S(2)}) collective-permute-start(bf16[2,16,64,128]{3,2,1,0:T(8,128)(2,1)S(1)} %copy_bitcast_fusion.1.refs_0_), channel_id=1, source_target_pairs={{0,8},{8,0},{1,9},{9,1},{2,10},{10,2},{3,11},{11,3},{4,12},{12,4},... | collective-permute-start | bytes 1572872 | tf_op jit(solution)/shard_map/ppermute | solution.py:312
  56.0 30.9 %copy-start.7 = (bf16[2,16,64,128]{3,2,1,0:T(8,128)(2,1)}, bf16[2,16,64,128]{3,2,1,0:T(8,128)(2,1)S(1)}, u32[]{:S(2)}) copy-start(bf16[2,16,64,128]{3,2,1,0:T(8,128)(2,1)S(1)} %collective-permute-done.2.refs_6_) | copy-start | bytes 1572868
  56.0 30.9 %copy-start.8 = (bf16[2,16,64,128]{3,2,1,0:T(8,128)(2,1)}, bf16[2,16,64,128]{3,2,1,0:T(8,128)(2,1)S(1)}, u32[]{:S(2)}) copy-start(bf16[2,16,64,128]{3,2,1,0:T(8,128)(2,1)S(1)} %collective-permute-done.1.refs_4_) | copy-start | bytes 1572868
  56.0 11.1 %all-to-all-start.1 = ((bf16[8,2,16,8,128]{4,3,2,1,0:T(8,128)(2,1)}), bf16[8,2,16,8,128]{4,3,2,1,0:T(8,128)(2,1)S(1)}, u32[]{:S(2)}, u32[]{:S(2)}) async-start(bf16[8,2,16,8,128]{4,3,2,1,0:T(8,128)(2,1)} %spectra.3), calls=%async_computation.1 | async-start | bytes 1048576 | tf_op jit(solution)/shard_map/all_to_all | solution.py:324
  59.5 11.2 %collective-permute-start.3 = (bf16[2,16,64,128]{3,2,1,0:T(8,128)(2,1)S(1)}, bf16[2,16,64,128]{3,2,1,0:T(8,128)(2,1)S(1)}, u32[]{:S(2)}, u32[]{:S(2)}) collective-permute-start(bf16[2,16,64,128]{3,2,1,0:T(8,128)(2,1)S(1)} %collective-permute-done.2.refs_6_), channel_id=1, source_target_pairs={{0,2},{2,0},{4,6},{6,4},{1,3},{3,1},{5,7},{7,5},{8,10},{10,8},{12,... | collective-permute-start | bytes 1572872 | tf_op jit(solution)/shard_map/ppermute | solution.py:316
  61.1 11.7 %collective-permute-start.4 = (bf16[2,16,64,128]{3,2,1,0:T(8,128)(2,1)S(1)}, bf16[2,16,64,128]{3,2,1,0:T(8,128)(2,1)}, u32[]{:S(2)}, u32[]{:S(2)}) collective-permute-start(bf16[2,16,64,128]{3,2,1,0:T(8,128)(2,1)S(1)} %collective-permute-done.refs_2_), channel_id=1, source_target_pairs={{0,6},{2,4},{4,2},{6,0},{1,7},{3,5},{5,3},{7,1},{8,14},{10,12},{12... | collective-permute-start | bytes 1572872 | tf_op jit(solution)/shard_map/ppermute | solution.py:316
  72.8 10.8 %collective-permute-start.7 = (bf16[2,16,64,128]{3,2,1,0:T(8,128)(2,1)S(1)}, bf16[2,16,64,128]{3,2,1,0:T(8,128)(2,1)}, u32[]{:S(2)}, u32[]{:S(2)}) collective-permute-start(bf16[2,16,64,128]{3,2,1,0:T(8,128)(2,1)S(1)} %copy_bitcast_fusion.refs_1_), channel_id=1, source_target_pairs={{0,6},{2,4},{4,2},{6,0},{1,7},{3,5},{5,3},{7,1},{8,14},{10,12},{12... | collective-permute-start | bytes 1572872 | tf_op jit(solution)/shard_map/ppermute | solution.py:316
  73.2 10.4 %collective-permute-start.6 = (bf16[2,16,64,128]{3,2,1,0:T(8,128)(2,1)S(1)}, bf16[2,16,64,128]{3,2,1,0:T(8,128)(2,1)S(1)}, u32[]{:S(2)}, u32[]{:S(2)}) collective-permute-start(bf16[2,16,64,128]{3,2,1,0:T(8,128)(2,1)S(1)} %copy_bitcast_fusion.refs_1_), channel_id=1, source_target_pairs={{0,2},{2,0},{4,6},{6,4},{1,3},{3,1},{5,7},{7,5},{8,10},{10,8},{12,... | collective-permute-start | bytes 1572872 | tf_op jit(solution)/shard_map/ppermute | solution.py:316
  73.2 11.0 %collective-permute-start.5 = (bf16[2,16,64,128]{3,2,1,0:T(8,128)(2,1)S(1)}, bf16[2,16,64,128]{3,2,1,0:T(8,128)(2,1)S(1)}, u32[]{:S(2)}, u32[]{:S(2)}) collective-permute-start(bf16[2,16,64,128]{3,2,1,0:T(8,128)(2,1)S(1)} %copy_bitcast_fusion.refs_1_), channel_id=1, source_target_pairs={{0,8},{8,0},{1,9},{9,1},{2,10},{10,2},{3,11},{11,3},{4,12},{12,4},... | collective-permute-start | bytes 1572872 | tf_op jit(solution)/shard_map/ppermute | solution.py:312
  73.7 23.7 %collective-permute-start.11 = (bf16[2,16,64,128]{3,2,1,0:T(8,128)(2,1)}, bf16[2,16,64,128]{3,2,1,0:T(8,128)(2,1)S(1)}, u32[]{:S(2)}, u32[]{:S(2)}) collective-permute-start(bf16[2,16,64,128]{3,2,1,0:T(8,128)(2,1)} %collective-permute-done.4.refs_9_), channel_id=1, source_target_pairs={{0,2},{2,0},{4,6},{6,4},{1,3},{3,1},{5,7},{7,5},{8,10},{10,8},{12,... | collective-permute-start | bytes 1572872 | tf_op jit(solution)/shard_map/ppermute | solution.py:316
  84.2 38.5 %copy-start.4 = (bf16[2,16,64,128]{3,2,1,0:T(8,128)(2,1)}, bf16[2,16,64,128]{3,2,1,0:T(8,128)(2,1)S(1)}, u32[]{:S(2)}) copy-start(bf16[2,16,64,128]{3,2,1,0:T(8,128)(2,1)S(1)} %collective-permute-done.5.refs_4_) | copy-start | bytes 1572868
  84.2 13.2 %collective-permute-start.12 = (bf16[2,16,64,128]{3,2,1,0:T(8,128)(2,1)S(1)}, bf16[2,16,64,128]{3,2,1,0:T(8,128)(2,1)S(1)}, u32[]{:S(2)}, u32[]{:S(2)}) collective-permute-start(bf16[2,16,64,128]{3,2,1,0:T(8,128)(2,1)S(1)} %collective-permute-done.6.refs_5_), channel_id=1, source_target_pairs={{0,6},{2,4},{4,2},{6,0},{1,7},{3,5},{5,3},{7,1},{8,14},{10,12},{12... | collective-permute-start | bytes 1572872 | tf_op jit(solution)/shard_map/ppermute | solution.py:316
  86.2 11.2 %collective-permute-start.10 = (bf16[2,16,64,128]{3,2,1,0:T(8,128)(2,1)S(1)}, bf16[2,16,64,128]{3,2,1,0:T(8,128)(2,1)}, u32[]{:S(2)}, u32[]{:S(2)}) collective-permute-start(bf16[2,16,64,128]{3,2,1,0:T(8,128)(2,1)S(1)} %collective-permute-done.6.refs_5_), channel_id=1, source_target_pairs={{0,8},{8,0},{1,9},{9,1},{2,10},{10,2},{3,11},{11,3},{4,12},{12,4},... | collective-permute-start | bytes 1572872 | tf_op jit(solution)/shard_map/ppermute | solution.py:312
  88.5 23.0 %collective-permute-start.9 = (bf16[4,2,16,64,128]{4,3,2,1,0:T(8,128)(2,1)S(1)}, bf16[4,2,16,64,128]{4,3,2,1,0:T(8,128)(2,1)}, u32[]{:S(2)}, u32[]{:S(2)}) collective-permute-start(bf16[4,2,16,64,128]{4,3,2,1,0:T(8,128)(2,1)S(1)} %pad_maximum_fusion), channel_id=1, source_target_pairs={{0,1},{1,0},{2,3},{3,2},{4,5},{5,4},{6,7},{7,6},{8,9},{9,8},{10,11... | collective-permute-start | bytes 6291464 | tf_op jit(solution)/shard_map/ppermute | solution.py:320
  100.5 12.0 %collective-permute-start.13 = (bf16[4,2,16,64,128]{4,3,2,1,0:T(8,128)(2,1)}, bf16[4,2,16,64,128]{4,3,2,1,0:T(8,128)(2,1)}, u32[]{:S(2)}, u32[]{:S(2)}) collective-permute-start(bf16[4,2,16,64,128]{4,3,2,1,0:T(8,128)(2,1)} %pad_maximum_fusion.1), channel_id=1, source_target_pairs={{0,1},{1,0},{2,3},{3,2},{4,5},{5,4},{6,7},{7,6},{8,9},{9,8},{10,11... | collective-permute-start | bytes 6291464 | tf_op jit(solution)/shard_map/ppermute | solution.py:320
  108.4 14.3 %collective-permute-start.15 = (bf16[2,16,64,128]{3,2,1,0:T(8,128)(2,1)S(1)}, bf16[2,16,64,128]{3,2,1,0:T(8,128)(2,1)}, u32[]{:S(2)}, u32[]{:S(2)}) collective-permute-start(bf16[2,16,64,128]{3,2,1,0:T(8,128)(2,1)S(1)} %copy-done.3), channel_id=1, source_target_pairs={{0,2},{2,0},{4,6},{6,4},{1,3},{3,1},{5,7},{7,5},{8,10},{10,8},{12,... | collective-permute-start | bytes 1572872 | tf_op jit(solution)/shard_map/ppermute | solution.py:316
  108.4 15.2 %collective-permute-start.14 = (bf16[2,16,64,128]{3,2,1,0:T(8,128)(2,1)}, bf16[2,16,64,128]{3,2,1,0:T(8,128)(2,1)}, u32[]{:S(2)}, u32[]{:S(2)}) collective-permute-start(bf16[2,16,64,128]{3,2,1,0:T(8,128)(2,1)} %collective-permute-done.7.refs_7_), channel_id=1, source_target_pairs={{0,8},{8,0},{1,9},{9,1},{2,10},{10,2},{3,11},{11,3},{4,12},{12,4},... | collective-permute-start | bytes 1572872 | tf_op jit(solution)/shard_map/ppermute | solution.py:312
  108.9 14.7 %collective-permute-start.16 = (bf16[2,16,64,128]{3,2,1,0:T(8,128)(2,1)}, bf16[2,16,64,128]{3,2,1,0:T(8,128)(2,1)}, u32[]{:S(2)}, u32[]{:S(2)}) collective-permute-start(bf16[2,16,64,128]{3,2,1,0:T(8,128)(2,1)} %collective-permute-done.10.refs_7_), channel_id=1, source_target_pairs={{0,6},{2,4},{4,2},{6,0},{1,7},{3,5},{5,3},{7,1},{8,14},{10,12},{12... | collective-permute-start | bytes 1572872 | tf_op jit(solution)/shard_map/ppermute | solution.py:316
  111.5 19.5 %collective-permute-start.8 = (bf16[3,2,16,64,128]{4,3,2,1,0:T(8,128)(2,1)S(1)}, bf16[3,2,16,64,128]{4,3,2,1,0:T(8,128)(2,1)S(1)}, u32[]{:S(2)}, u32[]{:S(2)}) collective-permute-start(bf16[3,2,16,64,128]{4,3,2,1,0:T(8,128)(2,1)S(1)} %pad_maximum_fusion.2), channel_id=1, source_target_pairs={{0,1},{1,0},{2,3},{3,2},{4,5},{5,4},{6,7},{7,6},{8,9},{9,8},{10,11... | collective-permute-start | bytes 4718600 | tf_op jit(solution)/shard_map/ppermute | solution.py:320
  125.1 5.8 %collective-permute-start.17 = (bf16[3,2,16,64,128]{4,3,2,1,0:T(8,128)(2,1)S(1)}, bf16[3,2,16,64,128]{4,3,2,1,0:T(8,128)(2,1)S(1)}, u32[]{:S(2)}, u32[]{:S(2)}) collective-permute-start(bf16[3,2,16,64,128]{4,3,2,1,0:T(8,128)(2,1)S(1)} %pad_maximum_fusion.3), channel_id=1, source_target_pairs={{0,1},{1,0},{2,3},{3,2},{4,5},{5,4},{6,7},{7,6},{8,9},{9,8},{10,11... | collective-permute-start | bytes 4718600 | tf_op jit(solution)/shard_map/ppermute | solution.py:320
  127.6 3.4 %collective-permute-start.18 = (bf16[2,2,16,64,128]{4,3,2,1,0:T(8,128)(2,1)S(1)}, bf16[2,2,16,64,128]{4,3,2,1,0:T(8,128)(2,1)S(1)}, u32[]{:S(2)}, u32[]{:S(2)}) collective-permute-start(bf16[2,2,16,64,128]{4,3,2,1,0:T(8,128)(2,1)S(1)} %pad_maximum_fusion.4), channel_id=1, source_target_pairs={{0,1},{1,0},{2,3},{3,2},{4,5},{5,4},{6,7},{7,6},{8,9},{9,8},{10,11... | collective-permute-start | bytes 3145736 | tf_op jit(solution)/shard_map/ppermute | solution.py:320
  (12 other events, 127.8 us)

commit v4 on v3

--- a/solution.py
+++ b/solution.py
@@ -35,11 +35,11 @@
 
 
 def spectra_kernel(
-    first_frame, x_hbm, taps_ref, table_hbm, weight_ref, out_ref,
+    first_frame, count, last, x_hbm, taps_ref, table_hbm, flags_ref, before_ref, out_ref,
     x_vmem, table, fold_a, fold_b, total, sums, turned, x_sems, table_sems,
 ):
-    frames = CHUNK + TAPS - 1
-    rows = CHUNK * 8
+    frames = count + TAPS - 1
+    rows = count * 8
     x_copies, table_copies = [], []
     for kb in range(BLOCKS):
         for half in range(2):
@@ -76,7 +76,7 @@
 
         taps = [[tap(k, offset) for k in range(TAPS)] for offset in (0, HALF)]
         window = [[load(f, offset) for f in range(TAPS - 1)] for offset in (0, HALF)]
-        for pair in range(CHUNK // 2):
+        for pair in range(count // 2):
             even, odd = [], []
             for f in (2 * pair, 2 * pair + 1):
                 halves = []
@@ -141,12 +141,27 @@
     lax.fori_loop(1, BLOCKS // 2 - 1, two_stages, 0)
     stage(BLOCKS - 2, fold_a, fold_b)
     stage(BLOCKS - 1, fold_b, None)
-    weight = weight_ref[...]
+    blk = (lax.axis_index("x_hi") * 4 + lax.axis_index("z")) * 2 + lax.axis_index("core")
+    chan = lax.axis_index("y") * 2 + lax.axis_index("x_lo")
+    station = lax.broadcasted_iota(jnp.int32, (8, 128), 0) // 2
+    weight = jnp.zeros((8, 128), jnp.float32)
+    for k in range(4):
+        flag = flags_ref[blk * 32 + chan * 4 + k].astype(jnp.float32) / math.sqrt(2.0 * NFFT)
+        weight = jnp.where(station == k, flag, weight)
     for cls in range(2):
         real = total[cls, 0, :, :128] + total[cls, 1, :, 128:]
         imag = total[cls, 1, :, :128] - total[cls, 0, :, 128:]
-        sums[cls, :rows, :] = (real.reshape(CHUNK, 8, 128) * weight).reshape(rows, 128)
-        sums[cls, rows:, :] = (imag.reshape(CHUNK, 8, 128) * weight).reshape(rows, 128)
+        for plane, value in enumerate((real, imag)):
+            value = (value.reshape(count, 8, 128) * weight).reshape(rows, 128)
+            if not last:
+                out_ref[cls, plane] = value
+                continue
+            end = (plane + 1) * CHUNK * 8
+            sums[cls, end - rows : end, :] = value
+            if count < CHUNK:
+                sums[cls, end - CHUNK * 8 : end - rows, :] = before_ref[cls, plane]
+    if not last:
+        return
     for cls in range(2):
         for i in range(8):
             turned[cls, i * 128 : (i + 1) * 128, :] = sums[cls, pl.ds(i, 128, stride=8), :].T
@@ -160,60 +175,71 @@
     lax.fori_loop(0, 8, emit, 0)
 
 
-def spectra(first_frame, x, taps, tables, weight):
+def spectra(first_frame, count, last, x, taps, tables, flags, before):
+    if last:
+        out_shape = jax.ShapeDtypeStruct((8, 2, 16, 8, 128), jnp.bfloat16)
+    else:
+        out_shape = jax.ShapeDtypeStruct((2, 2, count * 8, 128), jnp.float32)
     return pl.pallas_call(
-        functools.partial(spectra_kernel, first_frame),
-        out_shape=jax.ShapeDtypeStruct((8, 2, 16, 8, 128), jnp.bfloat16),
+        functools.partial(spectra_kernel, first_frame, count, last),
+        out_shape=out_shape,
         in_specs=[
             pl.BlockSpec(memory_space=pltpu.HBM),
             pl.BlockSpec(memory_space=pltpu.VMEM),
             pl.BlockSpec(memory_space=pltpu.HBM),
+            pl.BlockSpec(memory_space=pltpu.SMEM),
             pl.BlockSpec(memory_space=pltpu.VMEM),
         ],
         out_specs=pl.BlockSpec(memory_space=pltpu.VMEM),
         scratch_shapes=[
-            pltpu.VMEM((2, CHUNK + TAPS - 1, 8, NFFT), jnp.bfloat16),
+            pltpu.VMEM((2, count + TAPS - 1, 8, NFFT), jnp.bfloat16),
             pltpu.VMEM((2, 2, HALF, 256), jnp.bfloat16),
-            pltpu.VMEM((2, 2, 2, CHUNK * 8, BLOCK), jnp.bfloat16),
-            pltpu.VMEM((2, 2, 2, CHUNK * 8, BLOCK), jnp.bfloat16),
-            pltpu.VMEM((2, 2, CHUNK * 8, 256), jnp.float32),
+            pltpu.VMEM((2, 2, 2, count * 8, BLOCK), jnp.bfloat16),
+            pltpu.VMEM((2, 2, 2, count * 8, BLOCK), jnp.bfloat16),
+            pltpu.VMEM((2, 2, count * 8, 256), jnp.float32),
             pltpu.VMEM((2, 2 * CHUNK * 8, 128), jnp.float32),
             pltpu.VMEM((2, 8 * 128, 128), jnp.float32),
             pltpu.SemaphoreType.DMA((BLOCKS, 2)),
             pltpu.SemaphoreType.DMA((BLOCKS,)),
         ],
         compiler_params=pltpu.CompilerParams(vmem_limit_bytes=56 * 1024 * 1024),
-        cost_estimate=pl.CostEstimate(flops=6_500_000_000, bytes_accessed=14_000_000, transcendentals=0),
+        cost_estimate=pl.CostEstimate(
+            flops=100_000_000 * count, bytes_accessed=140_000 * count + 4_000_000, transcendentals=0
+        ),
         name="spectra",
-    )(x, taps, tables, weight)
-
-
-NJ = 2
+    )(x, taps, tables, flags, before)
+
+
+NJ = 4
 
 
 STEPS_Z = (0, 1, 3, 2)
 
 
-def correlate_kernel(far, places, place_ref, scale_ref, *refs):
+def correlate_kernel(pairs, places, place_ref, scale_ref, *refs):
     out_ref, token_ref, staged, sems = refs[-4:]
     step, steps = pl.program_id(0), pl.num_programs(0)
     slot = step % 2
-    first_column = (place_ref[0] ^ far) * 512
-    place_z = place_ref[1]
     at_core_0 = place_ref[2] == 0
     token_ref[...] = jnp.zeros_like(token_ref)
 
-    def copy(at):
-        column = pl.multiple_of(first_column, 512)
-        return pltpu.make_async_copy(
-            staged.at[at % 2],
-            out_ref.at[pl.ds(at * (2 * NJ), 2 * NJ), :, :, pl.ds(column, 512)],
-            sems.at[at % 2],
-        )
+    def copies(at):
+        made = []
+        for q, (far, bits) in enumerate(pairs):
+            column = pl.multiple_of((place_ref[0] ^ far) * 512 + (place_ref[1] ^ bits) * 128, 128)
+            made.append(
+                pltpu.make_async_copy(
+                    staged.at[at % 2, q],
+                    out_ref.at[pl.ds(at * (2 * NJ), 2 * NJ), :, :, pl.ds(column, 128)],
+                    sems.at[at % 2, q],
+                )
+            )
+        return made
 
     @pl.when(step >= 2)
     def _():
-        copy(step - 2).wait()
+        for copy in copies(step - 2):
+            copy.wait()
 
     lane = lax.broadcasted_iota(jnp.int32, (64, 128), 1)
     sign = jnp.where(lane < 64, 1.0, -1.0)
@@ -229,9 +255,10 @@
             left = jnp.concatenate([jnp.concatenate(own, axis=1), jnp.concatenate(turned, axis=1)], axis=0)
             channel = 2 * jj + cls
             scale = scale_ref[step * (2 * NJ) + channel]
-            for half in range(2):
+            for q in range(0, len(pairs), 2):
+                group = range(q, min(q + 2, len(pairs)))
                 rows = []
-                for k in (2 * half, 2 * half + 1):
+                for k in group:
                     same_p, other_p, same_q, other_q = [load(place) for place in places[2 + 4 * k : 6 + 4 * k]]
                     same = jnp.concatenate([same_p, same_q], axis=1)
                     other = jnp.concatenate([other_p, other_q], axis=1)
@@ -241,24 +268,25 @@
                     left, right, (((1,), (1,)), ((), ())), preferred_element_type=jnp.float32
                 )
                 total = (total * scale).astype(jnp.bfloat16)
-                for k in (2 * half, 2 * half + 1):
-                    to = pl.ds(pl.multiple_of((place_z ^ STEPS_Z[k]) * 128, 128), 128)
-                    lanes = slice(128 * (k % 2), 128 * (k % 2) + 128)
+                for k in group:
+                    lanes = slice(128 * (k - q), 128 * (k - q) + 128)
                     for plane in range(2):
-                        staged[slot, channel, plane, :, to] = total[64 * plane : 64 * plane + 64, lanes]
-    copy(step).start()
+                        staged[slot, k, channel, plane] = total[64 * plane : 64 * plane + 64, lanes]
+    for copy in copies(step):
+        copy.start()
 
     @pl.when(step == steps - 1)
     def _():
         for at in (steps - 2, steps - 1):
-            copy(at).wait()
+            for copy in copies(at):
+                copy.wait()
 
 
 def block_index(lead, step):
     return (0,) * lead + (step, 0, 0)
 
 
-def correlate(far, place, scale, parts, token, out=None):
+def correlate(pairs, place, scale, parts, token, out=None):
     operands, places = [], []
     for part in parts:
         array, *lead = part if isinstance(part, tuple) else (part,)
@@ -278,7 +306,7 @@
         aliases = {2 + len(operands): 0}
         operands.append(out)
     return pl.pallas_call(
-        functools.partial(correlate_kernel, far, places),
+        functools.partial(correlate_kernel, pairs, places),
         out_shape=(
             jax.ShapeDtypeStruct((32, 2, 64, 1024), jnp.bfloat16),
             jax.ShapeDtypeStruct((8, 128), jnp.float32),
@@ -288,11 +316,11 @@
         out_specs=(pl.BlockSpec(memory_space=pltpu.HBM), pl.BlockSpec((8, 128), lambda s: (0, 0))),
         input_output_aliases=aliases,
         scratch_shapes=[
-            pltpu.VMEM((2, 2 * NJ, 2, 64, 512), jnp.bfloat16),
-            pltpu.SemaphoreType.DMA((2,)),
+            pltpu.VMEM((2, len(pairs), 2 * NJ, 2, 64, 128), jnp.bfloat16),
+            pltpu.SemaphoreType.DMA((2, len(pairs))),
         ],
         compiler_params=pltpu.CompilerParams(vmem_limit_bytes=56 * 1024 * 1024),
-        cost_estimate=pl.CostEstimate(flops=2_000_000_000, bytes_accessed=13_000_000, transcendentals=0),
+        cost_estimate=pl.CostEstimate(flops=500_000_000 * len(pairs), bytes_accessed=3_300_000 * len(pairs), transcendentals=0),
         name="correlate",
     )(place, scale, *operands)
 
@@ -317,7 +345,8 @@
 
 
 def to_core(*blocks):
-    return lax.ppermute(jnp.stack([block.value for block in blocks]), "core", [(0, 1), (1, 0)])
+    array = blocks[0].value if len(blocks) == 1 else jnp.stack([block.value for block in blocks])
+    return lax.ppermute(array, "core", [(0, 1), (1, 0)])
 
 
 def turn(chunk):
@@ -328,51 +357,58 @@
 def on_device(voltages, fir_taps, station_flags, bin_offsets):
     chan = lax.axis_index(("y", "x_lo"))
     x_hi, z, core = [lax.axis_index(axis) for axis in ("x_hi", "z", "core")]
-    blk = (x_hi * 4 + z) * 2 + core
-    flags = jnp.repeat(station_flags, 2).astype(jnp.float32)
-    weight = lax.dynamic_slice_in_dim(flags, blk * 64 + chan * 8, 8, 0) / math.sqrt(2.0 * NFFT)
-    weight = jnp.broadcast_to(weight[:, None], (8, 128))
     scales = jnp.exp2(-bin_offsets.astype(jnp.float32)) / FRAMES
     scale = lax.dynamic_slice_in_dim(scales, chan * 32, 32, 0)
     tables = jnp.asarray(dft_tables())
     planes = voltages.reshape(2, 8, FRAMES + TAPS - 1, NFFT).transpose(0, 2, 1, 3)
 
     place = jnp.stack([x_hi, z, core]).astype(jnp.int32)
-    p = {0: Block(turn(spectra(0, planes, fir_taps, tables, weight)))}
-    weight = Block(weight)
-    together(weight, p[0])
-    spectra_q = Block(spectra(CHUNK, planes, fir_taps, tables, weight.value))
+    p = {0: Block(turn(spectra(0, CHUNK, True, planes, fir_taps, tables, station_flags, fir_taps)))}
+    part = Block(spectra(CHUNK, CHUNK // 2, False, planes, fir_taps, tables, station_flags, fir_taps))
+    together(part, p[0])
+    spectra_q = Block(
+        spectra(CHUNK + CHUNK // 2, CHUNK // 2, True, planes, fir_taps, tables, station_flags, part.value)
+    )
     xp, q, xq = {0: along_x(p[0])}, {}, {}
     p[1], p[3] = along_z(p[0], 1), along_z(p[0], 3)
     together(spectra_q, xp[0], p[1], p[3])
     p[2], xp[3] = along_z(p[3], 1), along_z(xp[0], 3)
     q[0] = Block(turn(spectra_q.value))
-    together(q[0], p[2], xp[3])
     xq[0] = along_x(q[0])
-    q[1], q[3] = along_z(q[0], 1), along_z(q[0], 3)
-    p_other = to_core(*[p[k] for k in STEPS_Z])
-    together(xq[0], q[1], q[3])
+    from_0 = Block(q[0].value), Block(q[0].value)
+    together(from_0[0], p[2])
+    together(from_0[1], xp[3])
+    q[1], q[3] = along_z(from_0[0], 1), along_z(from_0[1], 3)
+    together(q[1], xq[0])
     xq[1] = along_x(q[1])
-    xp[2], q[2] = along_z(xp[3], 1), along_z(q[1], 3)
-    far_a = to_core(xp[0], xp[3], xq[0])
-    together(xq[1], xp[2], q[2])
+    others_a = to_core(*[p[k] for k in STEPS_Z], xp[0], xp[3], xq[0])
+    from_3 = Block(xp[3].value)
+    together(from_3, q[1])
+    xp[2] = along_z(from_3, 1)
+    together(q[3], q[1])
+    q[2] = along_z(q[1], 3)
+    together(q[3], xq[1])
     xq[3] = along_x(q[3])
-    xp[1], xq[2] = along_z(xp[0], 1), along_z(xq[1], 3)
-    q_other = to_core(*[q[k] for k in STEPS_Z])
-    far_b = to_core(xp[2], xq[1])
+    from_0 = Block(xp[0].value)
+    together(from_0, xp[2])
+    xp[1] = along_z(from_0, 1)
+    together(xq[1], q[2])
+    xq[2] = along_z(xq[1], 3)
+    others_b = to_core(*[q[k] for k in STEPS_Z], xp[2], xq[1])
     token = Block(jnp.zeros((8, 128), jnp.float32))
-    parts = [p[0].value, q[0].value]
+    own = [p[0].value, q[0].value]
+    parts = list(own)
     for at, k in enumerate(STEPS_Z):
-        parts += [p[k].value, (p_other, at), q[k].value, (q_other, at)]
-    out, token.value = correlate(0, place, scale, parts, token.value)
+        parts += [p[k].value, (others_a, at), q[k].value, (others_b, at)]
+    parts += [xp[0].value, (others_a, 4), xq[0].value, (others_a, 6)]
+    early = [(0, k) for k in STEPS_Z] + [(1, 0)]
+    out, token.value = correlate(early, place, scale, parts, token.value)
     together(token, xq[3], xp[1], xq[2])
-    far_c = to_core(xp[1], xq[3], xq[2])
-    parts = [p[0].value, q[0].value]
-    parts += [xp[0].value, (far_a, 0), xq[0].value, (far_a, 2)]
-    parts += [xp[1].value, (far_c, 0), xq[1].value, (far_b, 1)]
-    parts += [xp[3].value, (far_a, 1), xq[3].value, (far_c, 1)]
-    parts += [xp[2].value, (far_b, 0), xq[2].value, (far_c, 2)]
-    return correlate(1, place, scale, parts, token.value, out)[0]
+    parts = list(own)
+    parts += [xp[1].value, to_core(xp[1]), xq[1].value, (others_b, 5)]
+    parts += [xp[3].value, (others_a, 5), xq[3].value, to_core(xq[3])]
+    parts += [xp[2].value, (others_b, 4), xq[2].value, to_core(xq[2])]
+    return correlate([(1, 1), (1, 3), (1, 2)], place, scale, parts, token.value, out)[0]
 
 
 def solution(mesh):

time: 144 us -> 132 us (0.917)
  blocking collectives: 15.2 us -> 0 us
  local copies, waits for them, and re-layouts: 4.47 us -> 14.5 us
  other arithmetic: 9.86 us -> 0.66 us
  Pallas kernels: 52.1 us -> 57.1 us
  waiting for transfers between devices: 24.9 us -> 20.6 us
  starting transfers between devices: 36.1 us -> 37.8 us
    all_to_all x1 -> x0, blocking collectives: 15.2 us -> none  [turn(): lax.all_to_all(chunk, ('y', 'x_lo'), split_axis=0, concat_axis=0, tiled=T...]
    unnamed x32 -> x53, local copies, waits for them, and re-layouts: 2.04 us -> 11.3 us
    another operation x5 -> x0, other arithmetic: 8.49 us -> none  [to_core(): jnp.stack([block.value for block in blocks])]
    ppermute x5, starting transfers between devices: 19.1 us -> 11.4 us  [to_core(): return lax.ppermute(array, 'core', [(0, 1), (1, 0)])]
    all_to_all x1 -> x2, starting transfers between devices: 3.51 us -> 10.5 us  [turn(): lax.all_to_all(chunk, ('y', 'x_lo'), split_axis=0, concat_axis=0, tiled=T...]
    ppermute x10, waiting for transfers between devices: 14 us -> 7.95 us  [along_z(): lax.ppermute(block.value, 'z', [(z, z ^ bits) for z in range(4)])]
    pallas_call x4 -> x5, Pallas kernels: 52.1 us -> 57.1 us  [the longest x3 39.7 us: spectra(): pl.pallas_call(functools.partial(spectra_kernel, first_frame, count, last...]
    ppermute x4, starting transfers between devices: 4.11 us -> 7.79 us  [along_x(): return Block(lax.ppermute(block.value, 'x_hi', [(0, 1), (1, 0)]))]
  transfers between devices with their start and end apart: 20 -> 21, of which waited for: 8 -> 12; matrix products, arithmetic and copies ran while one was open for 7% -> 10% of each run, Pallas kernels for 18% -> 25%
where the time goes in v4:
time: 132 us; the launch traced here: 131 us
  Pallas kernels  57.1 us (43%)
  starting transfers between devices  37.8 us (29%)
  waiting for transfers between devices  20.6 us (16%)
  local copies, waits for them, and re-layouts  14.5 us (11%)
    pallas_call x3, Pallas kernels, spectra(): pl.pallas_call(functools.partial(spectra_kernel, first_frame, count, last...  39.7 us
    pallas_call x2, Pallas kernels, correlate(): pl.pallas_call(functools.partial(correlate_kernel, pairs, places), out_sh...  17.4 us
    ppermute x5, starting transfers between devices, to_core(): return lax.ppermute(array, 'core', [(0, 1), (1, 0)])  11.4 us
    unnamed x53, local copies, waits for them, and re-layouts  11.3 us
    all_to_all x2, starting transfers between devices, turn(): lax.all_to_all(chunk, ('y', 'x_lo'), split_axis=0, concat_axis=0, tiled=T...  10.5 us
    ppermute x10, starting transfers between devices, along_z(): lax.ppermute(block.value, 'z', [(z, z ^ bits) for z in range(4)])  8.02 us
    ppermute x10, waiting for transfers between devices, along_z(): lax.ppermute(block.value, 'z', [(z, z ^ bits) for z in range(4)])  7.95 us
    ppermute x4, starting transfers between devices, along_x(): return Block(lax.ppermute(block.value, 'x_hi', [(0, 1), (1, 0)]))  7.79 us
  transfers between devices with their start and end apart: 21, of which 12 were waited for; matrix products, arithmetic and copies ran while one was open for 10% of the time, Pallas kernels for 25%

profile of v4, /device:TPU:1, one launch (start us, length us, event | category | flops | bytes accessed | tf_op | source)
XLA Modules:
  0.0 131.1 jit_solution(2464748473432586903)
XLA Ops:
  0.0 16.4 %spectra.4 = bf16[8,2,16,8,128]{4,3,2,1,0:T(8,128)(2,1)} custom-call(bf16[2,131,8,4096]{3,2,1,0:T(8,128)(2,1)} %bitcast.44, f32[4,4096]{1,0:T(4,128)} %taps_ref.5, bf16[2,2,2048,256]{3,2,1,0:T(8,128)(2,1)} %constant.36.clone.table_hbm, s32[512]{0:T(512)} %flags_ref.5, f32[4,4096]{1,0:T(4,128)} %taps_ref.5), custom_call_target="tpu_custom_call" | custom-call | flops 6400000000 | bytes 12960000 | tf_op jit(solution)/shard_map/spectra/pallas_call | solution.py:183
  16.4 6.0 %all-to-all-start = ((bf16[8,2,16,8,128]{4,3,2,1,0:T(8,128)(2,1)}), bf16[8,2,16,8,128]{4,3,2,1,0:T(8,128)(2,1)S(1)}, u32[]{:S(2)}, u32[]{:S(2)}) async-start(bf16[8,2,16,8,128]{4,3,2,1,0:T(8,128)(2,1)} %spectra.4), calls=%async_computation | async-start | bytes 1048576 | tf_op jit(solution)/shard_map/all_to_all | solution.py:353
  22.4 11.1 %spectra.3.before_ref = f32[2,2,256,128]{3,2,1,0:T(8,128)} custom-call(bf16[2,131,8,4096]{3,2,1,0:T(8,128)(2,1)} %bitcast.45, f32[4,4096]{1,0:T(4,128)} %taps_ref.5, bf16[2,2,2048,256]{3,2,1,0:T(8,128)(2,1)} %constant.36.clone.table_hbm, s32[512]{0:T(512)} %flags_ref.5, f32[4,4096]{1,0:T(4,128)} %taps_ref.5), custom_call_target="tpu_custom_call" | custom-call | flops 3200000000 | bytes 8480000 | tf_op jit(solution)/shard_map/spectra/pallas_call | solution.py:183
  33.6 3.8 %collective-permute-start.2 = (bf16[2,16,64,128]{3,2,1,0:T(8,128)(2,1)S(1)}, bf16[2,16,64,128]{3,2,1,0:T(8,128)(2,1)S(1)}, u32[]{:S(2)}, u32[]{:S(2)}) collective-permute-start(bf16[2,16,64,128]{3,2,1,0:T(8,128)(2,1)S(1)} %copy_bitcast_fusion.refs_0_), channel_id=1, source_target_pairs={{0,6},{2,4},{4,2},{6,0},{1,7},{3,5},{5,3},{7,1},{8,14},{10,12},{12... | collective-permute-start | bytes 1572872 | tf_op jit(solution)/shard_map/ppermute | solution.py:344
  37.5 2.5 %collective-permute-start = (bf16[2,16,64,128]{3,2,1,0:T(8,128)(2,1)S(1)}, bf16[2,16,64,128]{3,2,1,0:T(8,128)(2,1)S(1)}, u32[]{:S(2)}, u32[]{:S(2)}) collective-permute-start(bf16[2,16,64,128]{3,2,1,0:T(8,128)(2,1)S(1)} %copy_bitcast_fusion.refs_0_), channel_id=1, source_target_pairs={{0,8},{8,0},{1,9},{9,1},{2,10},{10,2},{3,11},{11,3},{4,12},{12,4},... | collective-permute-start | bytes 1572872 | tf_op jit(solution)/shard_map/ppermute | solution.py:340
  40.7 12.2 %spectra.5 = bf16[8,2,16,8,128]{4,3,2,1,0:T(8,128)(2,1)} custom-call(bf16[2,131,8,4096]{3,2,1,0:T(8,128)(2,1)} %bitcast.46, f32[4,4096]{1,0:T(4,128)} %taps_ref.5, bf16[2,2,2048,256]{3,2,1,0:T(8,128)(2,1)} %constant.36.clone.table_hbm, s32[512]{0:T(512)} %flags_ref.5, f32[2,2,256,128]{3,2,1,0:T(8,128)} %spectra.3.before_ref), custom_call_target="tpu_custom_call" | custom-call | flops 3200000000 | bytes 8480000 | tf_op jit(solution)/shard_map/spectra/pallas_call | solution.py:183
  53.1 4.5 %all-to-all-start.1 = ((bf16[8,2,16,8,128]{4,3,2,1,0:T(8,128)(2,1)}), bf16[8,2,16,8,128]{4,3,2,1,0:T(8,128)(2,1)S(1)}, u32[]{:S(2)}, u32[]{:S(2)}) async-start(bf16[8,2,16,8,128]{4,3,2,1,0:T(8,128)(2,1)} %spectra.5), calls=%async_computation.1 | async-start | bytes 1048576 | tf_op jit(solution)/shard_map/all_to_all | solution.py:353
  57.6 1.5 %collective-permute-start.3 = (bf16[2,16,64,128]{3,2,1,0:T(8,128)(2,1)S(1)}, bf16[2,16,64,128]{3,2,1,0:T(8,128)(2,1)S(1)}, u32[]{:S(2)}, u32[]{:S(2)}) collective-permute-start(bf16[2,16,64,128]{3,2,1,0:T(8,128)(2,1)S(1)} %collective-permute-done.2.refs_6_), channel_id=1, source_target_pairs={{0,2},{2,0},{4,6},{6,4},{1,3},{3,1},{5,7},{7,5},{8,10},{10,8},{12,... | collective-permute-start | bytes 1572872 | tf_op jit(solution)/shard_map/ppermute | solution.py:344
  60.8 4.5 %all-to-all-done.1 = bf16[8,2,16,8,128]{4,3,2,1,0:T(8,128)(2,1)S(1)} async-done(((bf16[8,2,16,8,128]{4,3,2,1,0:T(8,128)(2,1)}), bf16[8,2,16,8,128]{4,3,2,1,0:T(8,128)(2,1)S(1)}, u32[]{:S(2)}, u32[]{:S(2)}) %all-to-all-start.1) | async-done | bytes 524320 | tf_op jit(solution)/shard_map/all_to_all | solution.py:353
  65.5 1.8 %collective-permute-start.6 = (bf16[2,16,64,128]{3,2,1,0:T(8,128)(2,1)S(1)}, bf16[2,16,64,128]{3,2,1,0:T(8,128)(2,1)S(1)}, u32[]{:S(2)}, u32[]{:S(2)}) collective-permute-start(bf16[2,16,64,128]{3,2,1,0:T(8,128)(2,1)S(1)} %copy_bitcast_fusion.1.refs_1_), channel_id=1, source_target_pairs={{0,8},{8,0},{1,9},{9,1},{2,10},{10,2},{3,11},{11,3},{4,12},{12,4},... | collective-permute-start | bytes 1572872 | tf_op jit(solution)/shard_map/ppermute | solution.py:340
  67.3 1.6 %collective-permute-done.3.refs_8_ = bf16[2,16,64,128]{3,2,1,0:T(8,128)(2,1)S(1)} collective-permute-done((bf16[2,16,64,128]{3,2,1,0:T(8,128)(2,1)S(1)}, bf16[2,16,64,128]{3,2,1,0:T(8,128)(2,1)S(1)}, u32[]{:S(2)}, u32[]{:S(2)}) %collective-permute-start.3) | collective-permute-done | bytes 524320 | tf_op jit(solution)/shard_map/ppermute | solution.py:344
  68.9 1.2 collective-permute-start.5
  74.0 3.1 %collective-permute-done.6.refs_11_ = bf16[2,16,64,128]{3,2,1,0:T(8,128)(2,1)S(1)} collective-permute-done((bf16[2,16,64,128]{3,2,1,0:T(8,128)(2,1)S(1)}, bf16[2,16,64,128]{3,2,1,0:T(8,128)(2,1)S(1)}, u32[]{:S(2)}, u32[]{:S(2)}) %collective-permute-start.6) | collective-permute-done | bytes 524320 | tf_op jit(solution)/shard_map/ppermute | solution.py:340
  77.2 2.2 %collective-permute-done.5.refs_5_ = bf16[2,16,64,128]{3,2,1,0:T(8,128)(2,1)S(1)} collective-permute-done((bf16[2,16,64,128]{3,2,1,0:T(8,128)(2,1)S(1)}, bf16[2,16,64,128]{3,2,1,0:T(8,128)(2,1)S(1)}, u32[]{:S(2)}, u32[]{:S(2)}) %collective-permute-start.5) | collective-permute-done | bytes 524320 | tf_op jit(solution)/shard_map/ppermute | solution.py:344
  79.4 1.8 %collective-permute-start.9 = (bf16[2,16,64,128]{3,2,1,0:T(8,128)(2,1)S(1)}, bf16[2,16,64,128]{3,2,1,0:T(8,128)(2,1)S(1)}, u32[]{:S(2)}, u32[]{:S(2)}) collective-permute-start(bf16[2,16,64,128]{3,2,1,0:T(8,128)(2,1)S(1)} %collective-permute-done.5.refs_5_), channel_id=1, source_target_pairs={{0,8},{8,0},{1,9},{9,1},{2,10},{10,2},{3,11},{11,3},{4,12},{12,4},... | collective-permute-start | bytes 1572872 | tf_op jit(solution)/shard_map/ppermute | solution.py:340
  85.2 4.5 %collective-permute-start.7 = (bf16[7,2,16,64,128]{4,3,2,1,0:T(8,128)(2,1)}, bf16[7,2,16,64,128]{4,3,2,1,0:T(8,128)(2,1)}, u32[]{:S(2)}, u32[]{:S(2)}) collective-permute-start(bf16[7,2,16,64,128]{4,3,2,1,0:T(8,128)(2,1)} %bitcast_dynamic-update-slice_fusion.6), channel_id=1, source_target_pairs={{0,1},{1,0},{2,3},{3,2},{4,5},{5,4},{6,7},{7,6},{8,9},{9,8},{10,11... | collective-permute-start | bytes 11010056 | tf_op jit(solution)/shard_map/ppermute | solution.py:349
  90.3 2.2 %collective-permute-done.10.refs_9_ = bf16[2,16,64,128]{3,2,1,0:T(8,128)(2,1)S(1)} collective-permute-done((bf16[2,16,64,128]{3,2,1,0:T(8,128)(2,1)S(1)}, bf16[2,16,64,128]{3,2,1,0:T(8,128)(2,1)S(1)}, u32[]{:S(2)}, u32[]{:S(2)}) %collective-permute-start.10) | collective-permute-done | bytes 524320 | tf_op jit(solution)/shard_map/ppermute | solution.py:344
  96.0 5.4 %collective-permute-start.12 = (bf16[6,2,16,64,128]{4,3,2,1,0:T(8,128)(2,1)}, bf16[6,2,16,64,128]{4,3,2,1,0:T(8,128)(2,1)S(1)}, u32[]{:S(2)}, u32[]{:S(2)}) collective-permute-start(bf16[6,2,16,64,128]{4,3,2,1,0:T(8,128)(2,1)} %bitcast_dynamic-update-slice_fusion), channel_id=1, source_target_pairs={{0,1},{1,0},{2,3},{3,2},{4,5},{5,4},{6,7},{7,6},{8,9},{9,8},{10,11... | collective-permute-start | bytes 9437192 | tf_op jit(solution)/shard_map/ppermute | solution.py:349
  101.4 1.8 %collective-permute-start.13 = (bf16[2,16,64,128]{3,2,1,0:T(8,128)(2,1)}, bf16[2,16,64,128]{3,2,1,0:T(8,128)(2,1)S(1)}, u32[]{:S(2)}, u32[]{:S(2)}) collective-permute-start(bf16[2,16,64,128]{3,2,1,0:T(8,128)(2,1)} %copy-done.12), channel_id=1, source_target_pairs={{0,8},{8,0},{1,9},{9,1},{2,10},{10,2},{3,11},{11,3},{4,12},{12,4},... | collective-permute-start | bytes 1572872 | tf_op jit(solution)/shard_map/ppermute | solution.py:340
  105.0 1.9 %collective-permute-done.12.refs_3_.refs_5_ = bf16[6,2,16,64,128]{4,3,2,1,0:T(8,128)(2,1)S(1)} collective-permute-done((bf16[6,2,16,64,128]{4,3,2,1,0:T(8,128)(2,1)}, bf16[6,2,16,64,128]{4,3,2,1,0:T(8,128)(2,1)S(1)}, u32[]{:S(2)}, u32[]{:S(2)}) %collective-permute-start.12) | collective-permute-done | bytes 3145760 | tf_op jit(solution)/shard_map/ppermute | solution.py:349
  107.6 1.0 copy-done
  108.6 9.3 %correlate.2 = (bf16[32,2,64,1024]{3,2,1,0:T(8,128)(2,1)}, f32[8,128]{1,0:T(8,128)}) custom-call(s32[3]{0:T(128)} %pad_add_fusion.place_ref, f32[32]{0:T(128)} %dynamic_slice.3.scale_ref, bf16[2,16,64,128]{3,2,1,0:T(8,128)(2,1)} %copy-done.1, bf16[2,16,64,128]{3,2,1,0:T(8,128)(2,1)} %copy-done.2, ...), custom_call_target="tpu_custom_call" | custom-call | flops 2500000000 | bytes 16500000 | tf_op jit(solution)/shard_map/correlate/pallas_call | solution.py:308
  119.5 1.0 collective-permute-done.16.refs_3_
  122.8 8.1 %correlate.3 = (bf16[32,2,64,1024]{3,2,1,0:T(8,128)(2,1)}, f32[8,128]{1,0:T(8,128)}) custom-call(s32[3]{0:T(128)} %pad_add_fusion.place_ref, f32[32]{0:T(128)} %dynamic_slice.3.scale_ref, bf16[2,16,64,128]{3,2,1,0:T(8,128)(2,1)} %copy-done.1, bf16[2,16,64,128]{3,2,1,0:T(8,128)(2,1)} %copy-done.2, ...), custom_call_target="tpu_custom_call", output_to_operand_aliasing={{0}: (16, {})} | custom-call | flops 1500000000 | bytes 9900000 | tf_op jit(solution)/shard_map/correlate/pallas_call | solution.py:308
  (84 shorter events, 21.2 us)
Async XLA Ops:
  16.4 17.1 %all-to-all-start = ((bf16[8,2,16,8,128]{4,3,2,1,0:T(8,128)(2,1)}), bf16[8,2,16,8,128]{4,3,2,1,0:T(8,128)(2,1)S(1)}, u32[]{:S(2)}, u32[]{:S(2)}) async-start(bf16[8,2,16,8,128]{4,3,2,1,0:T(8,128)(2,1)} %spectra.4), calls=%async_computation | async-start | bytes 1048576 | tf_op jit(solution)/shard_map/all_to_all | solution.py:353
  33.6 19.4 %collective-permute-start.2 = (bf16[2,16,64,128]{3,2,1,0:T(8,128)(2,1)S(1)}, bf16[2,16,64,128]{3,2,1,0:T(8,128)(2,1)S(1)}, u32[]{:S(2)}, u32[]{:S(2)}) collective-permute-start(bf16[2,16,64,128]{3,2,1,0:T(8,128)(2,1)S(1)} %copy_bitcast_fusion.refs_0_), channel_id=1, source_target_pairs={{0,6},{2,4},{4,2},{6,0},{1,7},{3,5},{5,3},{7,1},{8,14},{10,12},{12... | collective-permute-start | bytes 1572872 | tf_op jit(solution)/shard_map/ppermute | solution.py:344
  37.5 15.6 %collective-permute-start.1 = (bf16[2,16,64,128]{3,2,1,0:T(8,128)(2,1)S(1)}, bf16[2,16,64,128]{3,2,1,0:T(8,128)(2,1)S(1)}, u32[]{:S(2)}, u32[]{:S(2)}) collective-permute-start(bf16[2,16,64,128]{3,2,1,0:T(8,128)(2,1)S(1)} %copy_bitcast_fusion.refs_0_), channel_id=1, source_target_pairs={{0,2},{2,0},{4,6},{6,4},{1,3},{3,1},{5,7},{7,5},{8,10},{10,8},{12,... | collective-permute-start | bytes 1572872 | tf_op jit(solution)/shard_map/ppermute | solution.py:344
  37.5 15.6 %collective-permute-start = (bf16[2,16,64,128]{3,2,1,0:T(8,128)(2,1)S(1)}, bf16[2,16,64,128]{3,2,1,0:T(8,128)(2,1)S(1)}, u32[]{:S(2)}, u32[]{:S(2)}) collective-permute-start(bf16[2,16,64,128]{3,2,1,0:T(8,128)(2,1)S(1)} %copy_bitcast_fusion.refs_0_), channel_id=1, source_target_pairs={{0,8},{8,0},{1,9},{9,1},{2,10},{10,2},{3,11},{11,3},{4,12},{12,4},... | collective-permute-start | bytes 1572872 | tf_op jit(solution)/shard_map/ppermute | solution.py:340
  53.1 12.3 %all-to-all-start.1 = ((bf16[8,2,16,8,128]{4,3,2,1,0:T(8,128)(2,1)}), bf16[8,2,16,8,128]{4,3,2,1,0:T(8,128)(2,1)S(1)}, u32[]{:S(2)}, u32[]{:S(2)}) async-start(bf16[8,2,16,8,128]{4,3,2,1,0:T(8,128)(2,1)} %spectra.5), calls=%async_computation.1 | async-start | bytes 1048576 | tf_op jit(solution)/shard_map/all_to_all | solution.py:353
  57.6 11.3 %collective-permute-start.3 = (bf16[2,16,64,128]{3,2,1,0:T(8,128)(2,1)S(1)}, bf16[2,16,64,128]{3,2,1,0:T(8,128)(2,1)S(1)}, u32[]{:S(2)}, u32[]{:S(2)}) collective-permute-start(bf16[2,16,64,128]{3,2,1,0:T(8,128)(2,1)S(1)} %collective-permute-done.2.refs_6_), channel_id=1, source_target_pairs={{0,2},{2,0},{4,6},{6,4},{1,3},{3,1},{5,7},{7,5},{8,10},{10,8},{12,... | collective-permute-start | bytes 1572872 | tf_op jit(solution)/shard_map/ppermute | solution.py:344
  59.1 12.0 %collective-permute-start.4 = (bf16[2,16,64,128]{3,2,1,0:T(8,128)(2,1)S(1)}, bf16[2,16,64,128]{3,2,1,0:T(8,128)(2,1)S(1)}, u32[]{:S(2)}, u32[]{:S(2)}) collective-permute-start(bf16[2,16,64,128]{3,2,1,0:T(8,128)(2,1)S(1)} %collective-permute-done.refs_10_), channel_id=1, source_target_pairs={{0,6},{2,4},{4,2},{6,0},{1,7},{3,5},{5,3},{7,1},{8,14},{10,12},{12... | collective-permute-start | bytes 1572872 | tf_op jit(solution)/shard_map/ppermute | solution.py:344
  65.5 28.0 %copy-start.2 = (bf16[2,16,64,128]{3,2,1,0:T(8,128)(2,1)}, bf16[2,16,64,128]{3,2,1,0:T(8,128)(2,1)S(1)}, u32[]{:S(2)}) copy-start(bf16[2,16,64,128]{3,2,1,0:T(8,128)(2,1)S(1)} %copy_bitcast_fusion.1.refs_1_) | copy-start | bytes 1572868
  65.5 11.7 %collective-permute-start.6 = (bf16[2,16,64,128]{3,2,1,0:T(8,128)(2,1)S(1)}, bf16[2,16,64,128]{3,2,1,0:T(8,128)(2,1)S(1)}, u32[]{:S(2)}, u32[]{:S(2)}) collective-permute-start(bf16[2,16,64,128]{3,2,1,0:T(8,128)(2,1)S(1)} %copy_bitcast_fusion.1.refs_1_), channel_id=1, source_target_pairs={{0,8},{8,0},{1,9},{9,1},{2,10},{10,2},{3,11},{11,3},{4,12},{12,4},... | collective-permute-start | bytes 1572872 | tf_op jit(solution)/shard_map/ppermute | solution.py:340
  68.9 24.5 %copy-start.7 = (bf16[2,16,64,128]{3,2,1,0:T(8,128)(2,1)}, bf16[2,16,64,128]{3,2,1,0:T(8,128)(2,1)S(1)}, u32[]{:S(2)}) copy-start(bf16[2,16,64,128]{3,2,1,0:T(8,128)(2,1)S(1)} %collective-permute-done.3.refs_8_) | copy-start | bytes 1572868
  68.9 10.4 %collective-permute-start.5 = (bf16[2,16,64,128]{3,2,1,0:T(8,128)(2,1)S(1)}, bf16[2,16,64,128]{3,2,1,0:T(8,128)(2,1)S(1)}, u32[]{:S(2)}, u32[]{:S(2)}) collective-permute-start(bf16[2,16,64,128]{3,2,1,0:T(8,128)(2,1)S(1)} %copy_bitcast_fusion.1.refs_1_), channel_id=1, source_target_pairs={{0,2},{2,0},{4,6},{6,4},{1,3},{3,1},{5,7},{7,5},{8,10},{10,8},{12,... | collective-permute-start | bytes 1572872 | tf_op jit(solution)/shard_map/ppermute | solution.py:344
  71.1 11.1 %collective-permute-start.8 = (bf16[2,16,64,128]{3,2,1,0:T(8,128)(2,1)S(1)}, bf16[2,16,64,128]{3,2,1,0:T(8,128)(2,1)S(1)}, u32[]{:S(2)}, u32[]{:S(2)}) collective-permute-start(bf16[2,16,64,128]{3,2,1,0:T(8,128)(2,1)S(1)} %copy_bitcast_fusion.1.refs_1_), channel_id=1, source_target_pairs={{0,6},{2,4},{4,2},{6,0},{1,7},{3,5},{5,3},{7,1},{8,14},{10,12},{12... | collective-permute-start | bytes 1572872 | tf_op jit(solution)/shard_map/ppermute | solution.py:344
  74.0 29.7 %copy-start.20 = (s32[256]{0:T(256)S(1)}, s32[256]{0:T(256)}, u32[]{:S(2)}) copy-start(s32[256]{0:T(256)} %param.8) | copy-start | bytes 3076
  79.4 11.0 %collective-permute-start.9 = (bf16[2,16,64,128]{3,2,1,0:T(8,128)(2,1)S(1)}, bf16[2,16,64,128]{3,2,1,0:T(8,128)(2,1)S(1)}, u32[]{:S(2)}, u32[]{:S(2)}) collective-permute-start(bf16[2,16,64,128]{3,2,1,0:T(8,128)(2,1)S(1)} %collective-permute-done.5.refs_5_), channel_id=1, source_target_pairs={{0,8},{8,0},{1,9},{9,1},{2,10},{10,2},{3,11},{11,3},{4,12},{12,4},... | collective-permute-start | bytes 1572872 | tf_op jit(solution)/shard_map/ppermute | solution.py:340
  82.1 10.4 %collective-permute-start.10 = (bf16[2,16,64,128]{3,2,1,0:T(8,128)(2,1)S(1)}, bf16[2,16,64,128]{3,2,1,0:T(8,128)(2,1)S(1)}, u32[]{:S(2)}, u32[]{:S(2)}) collective-permute-start(bf16[2,16,64,128]{3,2,1,0:T(8,128)(2,1)S(1)} %collective-permute-done.5.refs_5_), channel_id=1, source_target_pairs={{0,6},{2,4},{4,2},{6,0},{1,7},{3,5},{5,3},{7,1},{8,14},{10,12},{12... | collective-permute-start | bytes 1572872 | tf_op jit(solution)/shard_map/ppermute | solution.py:344
  83.6 10.7 %collective-permute-start.11 = (bf16[2,16,64,128]{3,2,1,0:T(8,128)(2,1)S(1)}, bf16[2,16,64,128]{3,2,1,0:T(8,128)(2,1)S(1)}, u32[]{:S(2)}, u32[]{:S(2)}) collective-permute-start(bf16[2,16,64,128]{3,2,1,0:T(8,128)(2,1)S(1)} %collective-permute-done.4.refs_6_), channel_id=1, source_target_pairs={{0,2},{2,0},{4,6},{6,4},{1,3},{3,1},{5,7},{7,5},{8,10},{10,8},{12,... | collective-permute-start | bytes 1572872 | tf_op jit(solution)/shard_map/ppermute | solution.py:344
  85.2 21.7 %collective-permute-start.7 = (bf16[7,2,16,64,128]{4,3,2,1,0:T(8,128)(2,1)}, bf16[7,2,16,64,128]{4,3,2,1,0:T(8,128)(2,1)}, u32[]{:S(2)}, u32[]{:S(2)}) collective-permute-start(bf16[7,2,16,64,128]{4,3,2,1,0:T(8,128)(2,1)} %bitcast_dynamic-update-slice_fusion.6), channel_id=1, source_target_pairs={{0,1},{1,0},{2,3},{3,2},{4,5},{5,4},{6,7},{7,6},{8,9},{9,8},{10,11... | collective-permute-start | bytes 11010056 | tf_op jit(solution)/shard_map/ppermute | solution.py:349
  96.0 10.9 %collective-permute-start.12 = (bf16[6,2,16,64,128]{4,3,2,1,0:T(8,128)(2,1)}, bf16[6,2,16,64,128]{4,3,2,1,0:T(8,128)(2,1)S(1)}, u32[]{:S(2)}, u32[]{:S(2)}) collective-permute-start(bf16[6,2,16,64,128]{4,3,2,1,0:T(8,128)(2,1)} %bitcast_dynamic-update-slice_fusion), channel_id=1, source_target_pairs={{0,1},{1,0},{2,3},{3,2},{4,5},{5,4},{6,7},{7,6},{8,9},{9,8},{10,11... | collective-permute-start | bytes 9437192 | tf_op jit(solution)/shard_map/ppermute | solution.py:349
  101.4 16.5 %collective-permute-start.13 = (bf16[2,16,64,128]{3,2,1,0:T(8,128)(2,1)}, bf16[2,16,64,128]{3,2,1,0:T(8,128)(2,1)S(1)}, u32[]{:S(2)}, u32[]{:S(2)}) collective-permute-start(bf16[2,16,64,128]{3,2,1,0:T(8,128)(2,1)} %copy-done.12), channel_id=1, source_target_pairs={{0,8},{8,0},{1,9},{9,1},{2,10},{10,2},{3,11},{11,3},{4,12},{12,4},... | collective-permute-start | bytes 1572872 | tf_op jit(solution)/shard_map/ppermute | solution.py:340
  103.2 14.7 %collective-permute-start.15 = (bf16[2,16,64,128]{3,2,1,0:T(8,128)(2,1)}, bf16[2,16,64,128]{3,2,1,0:T(8,128)(2,1)S(1)}, u32[]{:S(2)}, u32[]{:S(2)}) collective-permute-start(bf16[2,16,64,128]{3,2,1,0:T(8,128)(2,1)} %copy-done.8), channel_id=1, source_target_pairs={{0,6},{2,4},{4,2},{6,0},{1,7},{3,5},{5,3},{7,1},{8,14},{10,12},{12... | collective-permute-start | bytes 1572872 | tf_op jit(solution)/shard_map/ppermute | solution.py:344
  103.7 14.2 %collective-permute-start.14 = (bf16[2,16,64,128]{3,2,1,0:T(8,128)(2,1)}, bf16[2,16,64,128]{3,2,1,0:T(8,128)(2,1)S(1)}, u32[]{:S(2)}, u32[]{:S(2)}) collective-permute-start(bf16[2,16,64,128]{3,2,1,0:T(8,128)(2,1)} %copy-done.5), channel_id=1, source_target_pairs={{0,2},{2,0},{4,6},{6,4},{1,3},{3,1},{5,7},{7,5},{8,10},{10,8},{12,... | collective-permute-start | bytes 1572872 | tf_op jit(solution)/shard_map/ppermute | solution.py:344
  118.0 2.5 %collective-permute-start.16 = (bf16[2,16,64,128]{3,2,1,0:T(8,128)(2,1)S(1)}, bf16[2,16,64,128]{3,2,1,0:T(8,128)(2,1)S(1)}, u32[]{:S(2)}, u32[]{:S(2)}) collective-permute-start(bf16[2,16,64,128]{3,2,1,0:T(8,128)(2,1)S(1)} %collective-permute-done.14.refs_2_), channel_id=1, source_target_pairs={{0,1},{1,0},{2,3},{3,2},{4,5},{5,4},{6,7},{7,6},{8,9},{9,8},{10,11... | collective-permute-start | bytes 1572872 | tf_op jit(solution)/shard_map/ppermute | solution.py:349
  118.9 2.3 %collective-permute-start.17 = (bf16[2,16,64,128]{3,2,1,0:T(8,128)(2,1)S(1)}, bf16[2,16,64,128]{3,2,1,0:T(8,128)(2,1)S(1)}, u32[]{:S(2)}, u32[]{:S(2)}) collective-permute-start(bf16[2,16,64,128]{3,2,1,0:T(8,128)(2,1)S(1)} %collective-permute-done.13.refs_8_), channel_id=1, source_target_pairs={{0,1},{1,0},{2,3},{3,2},{4,5},{5,4},{6,7},{7,6},{8,9},{9,8},{10,11... | collective-permute-start | bytes 1572872 | tf_op jit(solution)/shard_map/ppermute | solution.py:349
  119.0 3.0 %collective-permute-start.18 = (bf16[2,16,64,128]{3,2,1,0:T(8,128)(2,1)S(1)}, bf16[2,16,64,128]{3,2,1,0:T(8,128)(2,1)S(1)}, u32[]{:S(2)}, u32[]{:S(2)}) collective-permute-start(bf16[2,16,64,128]{3,2,1,0:T(8,128)(2,1)S(1)} %collective-permute-done.15.refs_11_), channel_id=1, source_target_pairs={{0,1},{1,0},{2,3},{3,2},{4,5},{5,4},{6,7},{7,6},{8,9},{9,8},{10,11... | collective-permute-start | bytes 1572872 | tf_op jit(solution)/shard_map/ppermute | solution.py:349
  (18 other events, 186.5 us)

commit v5 on v4

--- a/solution.py
+++ b/solution.py
@@ -95,8 +95,9 @@
 
     def product(kb, cls, p, fold):
         samples = pl.ds(pl.multiple_of(kb * BLOCK, BLOCK), BLOCK)
-        high, low = fold[p, cls, 0], fold[p, cls, 1]
-        left = jnp.concatenate([high, low, high], axis=1)
+        planes = range(2) if p is None else (p,)
+        left = [[fold[plane, cls, part] for part in (0, 1, 0)] for plane in planes]
+        left = jnp.concatenate([jnp.concatenate(parts, axis=1) for parts in left], axis=0)
         table_high, table_low = table[cls, 0, samples, :], table[cls, 1, samples, :]
         right = jnp.concatenate([table_high, table_high, table_low], axis=0)
         return jnp.dot(left, right, preferred_element_type=jnp.float32)
@@ -106,9 +107,10 @@
             if fold_out is not None:
                 fir(kb + 1, a, 0, fold_out)
                 fir(kb + 1, a, 1, fold_out)
+            both = product(kb, a, None, fold_in) if fold_in is not None and count < CHUNK else None
             for b in range(2):
                 if fold_in is not None:
-                    value = product(kb, a, b, fold_in)
+                    value = product(kb, a, b, fold_in) if both is None else both[b * rows : (b + 1) * rows]
                     if first:
                         total[a, b] = value
                     else:

time: 132 us -> 132 us (level)
  no operation moved by 1% of the time
where the time goes in v5:
time: 132 us; the launch traced here: 131 us
  Pallas kernels  57.1 us (43%)
  starting transfers between devices  37.7 us (29%)
  waiting for transfers between devices  20.7 us (16%)
  local copies, waits for them, and re-layouts  14.5 us (11%)
    pallas_call x3, Pallas kernels, spectra(): pl.pallas_call(functools.partial(spectra_kernel, first_frame, count, last...  39.7 us
    pallas_call x2, Pallas kernels, correlate(): pl.pallas_call(functools.partial(correlate_kernel, pairs, places), out_sh...  17.4 us
    ppermute x5, starting transfers between devices, to_core(): return lax.ppermute(array, 'core', [(0, 1), (1, 0)])  11.4 us
    unnamed x53, local copies, waits for them, and re-layouts  11.3 us
    all_to_all x2, starting transfers between devices, turn(): lax.all_to_all(chunk, ('y', 'x_lo'), split_axis=0, concat_axis=0, tiled=T...  10.5 us
    ppermute x10, starting transfers between devices, along_z(): lax.ppermute(block.value, 'z', [(z, z ^ bits) for z in range(4)])  8.08 us
    ppermute x10, waiting for transfers between devices, along_z(): lax.ppermute(block.value, 'z', [(z, z ^ bits) for z in range(4)])  8 us
    ppermute x4, starting transfers between devices, along_x(): return Block(lax.ppermute(block.value, 'x_hi', [(0, 1), (1, 0)]))  7.75 us
  transfers between devices with their start and end apart: 21, of which 12 were waited for; matrix products, arithmetic and copies ran while one was open for 10% of the time, Pallas kernels for 25%

profile of v5, /device:TPU:1, one launch (start us, length us, event | category | flops | bytes accessed | tf_op | source)
XLA Modules:
  0.0 131.1 jit_solution(17760111880721924870)
XLA Ops:
  0.0 16.4 %spectra.4 = bf16[8,2,16,8,128]{4,3,2,1,0:T(8,128)(2,1)} custom-call(bf16[2,131,8,4096]{3,2,1,0:T(8,128)(2,1)} %bitcast.44, f32[4,4096]{1,0:T(4,128)} %taps_ref.5, bf16[2,2,2048,256]{3,2,1,0:T(8,128)(2,1)} %constant.36.clone.table_hbm, s32[512]{0:T(512)} %flags_ref.5, f32[4,4096]{1,0:T(4,128)} %taps_ref.5), custom_call_target="tpu_custom_call" | custom-call | flops 6400000000 | bytes 12960000 | tf_op jit(solution)/shard_map/spectra/pallas_call | solution.py:185
  16.4 6.0 %all-to-all-start = ((bf16[8,2,16,8,128]{4,3,2,1,0:T(8,128)(2,1)}), bf16[8,2,16,8,128]{4,3,2,1,0:T(8,128)(2,1)S(1)}, u32[]{:S(2)}, u32[]{:S(2)}) async-start(bf16[8,2,16,8,128]{4,3,2,1,0:T(8,128)(2,1)} %spectra.4), calls=%async_computation | async-start | bytes 1048576 | tf_op jit(solution)/shard_map/all_to_all | solution.py:355
  22.4 11.1 %spectra.3.before_ref = f32[2,2,256,128]{3,2,1,0:T(8,128)} custom-call(bf16[2,131,8,4096]{3,2,1,0:T(8,128)(2,1)} %bitcast.45, f32[4,4096]{1,0:T(4,128)} %taps_ref.5, bf16[2,2,2048,256]{3,2,1,0:T(8,128)(2,1)} %constant.36.clone.table_hbm, s32[512]{0:T(512)} %flags_ref.5, f32[4,4096]{1,0:T(4,128)} %taps_ref.5), custom_call_target="tpu_custom_call" | custom-call | flops 3200000000 | bytes 8480000 | tf_op jit(solution)/shard_map/spectra/pallas_call | solution.py:185
  33.6 3.8 %collective-permute-start.2 = (bf16[2,16,64,128]{3,2,1,0:T(8,128)(2,1)S(1)}, bf16[2,16,64,128]{3,2,1,0:T(8,128)(2,1)S(1)}, u32[]{:S(2)}, u32[]{:S(2)}) collective-permute-start(bf16[2,16,64,128]{3,2,1,0:T(8,128)(2,1)S(1)} %copy_bitcast_fusion.refs_0_), channel_id=1, source_target_pairs={{0,6},{2,4},{4,2},{6,0},{1,7},{3,5},{5,3},{7,1},{8,14},{10,12},{12... | collective-permute-start | bytes 1572872 | tf_op jit(solution)/shard_map/ppermute | solution.py:346
  37.5 2.5 %collective-permute-start = (bf16[2,16,64,128]{3,2,1,0:T(8,128)(2,1)S(1)}, bf16[2,16,64,128]{3,2,1,0:T(8,128)(2,1)S(1)}, u32[]{:S(2)}, u32[]{:S(2)}) collective-permute-start(bf16[2,16,64,128]{3,2,1,0:T(8,128)(2,1)S(1)} %copy_bitcast_fusion.refs_0_), channel_id=1, source_target_pairs={{0,8},{8,0},{1,9},{9,1},{2,10},{10,2},{3,11},{11,3},{4,12},{12,4},... | collective-permute-start | bytes 1572872 | tf_op jit(solution)/shard_map/ppermute | solution.py:342
  40.7 12.2 %spectra.5 = bf16[8,2,16,8,128]{4,3,2,1,0:T(8,128)(2,1)} custom-call(bf16[2,131,8,4096]{3,2,1,0:T(8,128)(2,1)} %bitcast.46, f32[4,4096]{1,0:T(4,128)} %taps_ref.5, bf16[2,2,2048,256]{3,2,1,0:T(8,128)(2,1)} %constant.36.clone.table_hbm, s32[512]{0:T(512)} %flags_ref.5, f32[2,2,256,128]{3,2,1,0:T(8,128)} %spectra.3.before_ref), custom_call_target="tpu_custom_call" | custom-call | flops 3200000000 | bytes 8480000 | tf_op jit(solution)/shard_map/spectra/pallas_call | solution.py:185
  53.1 4.5 %all-to-all-start.1 = ((bf16[8,2,16,8,128]{4,3,2,1,0:T(8,128)(2,1)}), bf16[8,2,16,8,128]{4,3,2,1,0:T(8,128)(2,1)S(1)}, u32[]{:S(2)}, u32[]{:S(2)}) async-start(bf16[8,2,16,8,128]{4,3,2,1,0:T(8,128)(2,1)} %spectra.5), calls=%async_computation.1 | async-start | bytes 1048576 | tf_op jit(solution)/shard_map/all_to_all | solution.py:355
  57.6 1.5 %collective-permute-start.3 = (bf16[2,16,64,128]{3,2,1,0:T(8,128)(2,1)S(1)}, bf16[2,16,64,128]{3,2,1,0:T(8,128)(2,1)S(1)}, u32[]{:S(2)}, u32[]{:S(2)}) collective-permute-start(bf16[2,16,64,128]{3,2,1,0:T(8,128)(2,1)S(1)} %collective-permute-done.2.refs_6_), channel_id=1, source_target_pairs={{0,2},{2,0},{4,6},{6,4},{1,3},{3,1},{5,7},{7,5},{8,10},{10,8},{12,... | collective-permute-start | bytes 1572872 | tf_op jit(solution)/shard_map/ppermute | solution.py:346
  60.8 4.5 %all-to-all-done.1 = bf16[8,2,16,8,128]{4,3,2,1,0:T(8,128)(2,1)S(1)} async-done(((bf16[8,2,16,8,128]{4,3,2,1,0:T(8,128)(2,1)}), bf16[8,2,16,8,128]{4,3,2,1,0:T(8,128)(2,1)S(1)}, u32[]{:S(2)}, u32[]{:S(2)}) %all-to-all-start.1) | async-done | bytes 524320 | tf_op jit(solution)/shard_map/all_to_all | solution.py:355
  65.5 1.8 %collective-permute-start.6 = (bf16[2,16,64,128]{3,2,1,0:T(8,128)(2,1)S(1)}, bf16[2,16,64,128]{3,2,1,0:T(8,128)(2,1)S(1)}, u32[]{:S(2)}, u32[]{:S(2)}) collective-permute-start(bf16[2,16,64,128]{3,2,1,0:T(8,128)(2,1)S(1)} %copy_bitcast_fusion.1.refs_1_), channel_id=1, source_target_pairs={{0,8},{8,0},{1,9},{9,1},{2,10},{10,2},{3,11},{11,3},{4,12},{12,4},... | collective-permute-start | bytes 1572872 | tf_op jit(solution)/shard_map/ppermute | solution.py:342
  67.3 1.6 %collective-permute-done.3.refs_8_ = bf16[2,16,64,128]{3,2,1,0:T(8,128)(2,1)S(1)} collective-permute-done((bf16[2,16,64,128]{3,2,1,0:T(8,128)(2,1)S(1)}, bf16[2,16,64,128]{3,2,1,0:T(8,128)(2,1)S(1)}, u32[]{:S(2)}, u32[]{:S(2)}) %collective-permute-start.3) | collective-permute-done | bytes 524320 | tf_op jit(solution)/shard_map/ppermute | solution.py:346
  69.0 1.2 collective-permute-start.5
  74.1 3.1 %collective-permute-done.6.refs_11_ = bf16[2,16,64,128]{3,2,1,0:T(8,128)(2,1)S(1)} collective-permute-done((bf16[2,16,64,128]{3,2,1,0:T(8,128)(2,1)S(1)}, bf16[2,16,64,128]{3,2,1,0:T(8,128)(2,1)S(1)}, u32[]{:S(2)}, u32[]{:S(2)}) %collective-permute-start.6) | collective-permute-done | bytes 524320 | tf_op jit(solution)/shard_map/ppermute | solution.py:342
  77.2 2.2 %collective-permute-done.5.refs_5_ = bf16[2,16,64,128]{3,2,1,0:T(8,128)(2,1)S(1)} collective-permute-done((bf16[2,16,64,128]{3,2,1,0:T(8,128)(2,1)S(1)}, bf16[2,16,64,128]{3,2,1,0:T(8,128)(2,1)S(1)}, u32[]{:S(2)}, u32[]{:S(2)}) %collective-permute-start.5) | collective-permute-done | bytes 524320 | tf_op jit(solution)/shard_map/ppermute | solution.py:346
  79.4 1.7 %collective-permute-start.9 = (bf16[2,16,64,128]{3,2,1,0:T(8,128)(2,1)S(1)}, bf16[2,16,64,128]{3,2,1,0:T(8,128)(2,1)S(1)}, u32[]{:S(2)}, u32[]{:S(2)}) collective-permute-start(bf16[2,16,64,128]{3,2,1,0:T(8,128)(2,1)S(1)} %collective-permute-done.5.refs_5_), channel_id=1, source_target_pairs={{0,8},{8,0},{1,9},{9,1},{2,10},{10,2},{3,11},{11,3},{4,12},{12,4},... | collective-permute-start | bytes 1572872 | tf_op jit(solution)/shard_map/ppermute | solution.py:342
  81.1 1.1 collective-permute-done.8.refs_7_
  85.3 4.5 %collective-permute-start.7 = (bf16[7,2,16,64,128]{4,3,2,1,0:T(8,128)(2,1)}, bf16[7,2,16,64,128]{4,3,2,1,0:T(8,128)(2,1)}, u32[]{:S(2)}, u32[]{:S(2)}) collective-permute-start(bf16[7,2,16,64,128]{4,3,2,1,0:T(8,128)(2,1)} %bitcast_dynamic-update-slice_fusion.6), channel_id=1, source_target_pairs={{0,1},{1,0},{2,3},{3,2},{4,5},{5,4},{6,7},{7,6},{8,9},{9,8},{10,11... | collective-permute-start | bytes 11010056 | tf_op jit(solution)/shard_map/ppermute | solution.py:351
  90.4 2.2 %collective-permute-done.10.refs_9_ = bf16[2,16,64,128]{3,2,1,0:T(8,128)(2,1)S(1)} collective-permute-done((bf16[2,16,64,128]{3,2,1,0:T(8,128)(2,1)S(1)}, bf16[2,16,64,128]{3,2,1,0:T(8,128)(2,1)S(1)}, u32[]{:S(2)}, u32[]{:S(2)}) %collective-permute-start.10) | collective-permute-done | bytes 524320 | tf_op jit(solution)/shard_map/ppermute | solution.py:346
  96.1 5.4 %collective-permute-start.12 = (bf16[6,2,16,64,128]{4,3,2,1,0:T(8,128)(2,1)}, bf16[6,2,16,64,128]{4,3,2,1,0:T(8,128)(2,1)S(1)}, u32[]{:S(2)}, u32[]{:S(2)}) collective-permute-start(bf16[6,2,16,64,128]{4,3,2,1,0:T(8,128)(2,1)} %bitcast_dynamic-update-slice_fusion), channel_id=1, source_target_pairs={{0,1},{1,0},{2,3},{3,2},{4,5},{5,4},{6,7},{7,6},{8,9},{9,8},{10,11... | collective-permute-start | bytes 9437192 | tf_op jit(solution)/shard_map/ppermute | solution.py:351
  101.5 1.7 %collective-permute-start.13 = (bf16[2,16,64,128]{3,2,1,0:T(8,128)(2,1)}, bf16[2,16,64,128]{3,2,1,0:T(8,128)(2,1)S(1)}, u32[]{:S(2)}, u32[]{:S(2)}) collective-permute-start(bf16[2,16,64,128]{3,2,1,0:T(8,128)(2,1)} %copy-done.12), channel_id=1, source_target_pairs={{0,8},{8,0},{1,9},{9,1},{2,10},{10,2},{3,11},{11,3},{4,12},{12,4},... | collective-permute-start | bytes 1572872 | tf_op jit(solution)/shard_map/ppermute | solution.py:342
  105.0 1.9 %collective-permute-done.12.refs_3_.refs_5_ = bf16[6,2,16,64,128]{4,3,2,1,0:T(8,128)(2,1)S(1)} collective-permute-done((bf16[6,2,16,64,128]{4,3,2,1,0:T(8,128)(2,1)}, bf16[6,2,16,64,128]{4,3,2,1,0:T(8,128)(2,1)S(1)}, u32[]{:S(2)}, u32[]{:S(2)}) %collective-permute-start.12) | collective-permute-done | bytes 3145760 | tf_op jit(solution)/shard_map/ppermute | solution.py:351
  107.6 1.0 copy-done
  108.6 9.3 %correlate.2 = (bf16[32,2,64,1024]{3,2,1,0:T(8,128)(2,1)}, f32[8,128]{1,0:T(8,128)}) custom-call(s32[3]{0:T(128)} %pad_add_fusion.place_ref, f32[32]{0:T(128)} %dynamic_slice.3.scale_ref, bf16[2,16,64,128]{3,2,1,0:T(8,128)(2,1)} %copy-done.1, bf16[2,16,64,128]{3,2,1,0:T(8,128)(2,1)} %copy-done.2, ...), custom_call_target="tpu_custom_call" | custom-call | flops 2500000000 | bytes 16500000 | tf_op jit(solution)/shard_map/correlate/pallas_call | solution.py:310
  122.8 8.1 %correlate.3 = (bf16[32,2,64,1024]{3,2,1,0:T(8,128)(2,1)}, f32[8,128]{1,0:T(8,128)}) custom-call(s32[3]{0:T(128)} %pad_add_fusion.place_ref, f32[32]{0:T(128)} %dynamic_slice.3.scale_ref, bf16[2,16,64,128]{3,2,1,0:T(8,128)(2,1)} %copy-done.1, bf16[2,16,64,128]{3,2,1,0:T(8,128)(2,1)} %copy-done.2, ...), custom_call_target="tpu_custom_call", output_to_operand_aliasing={{0}: (16, {})} | custom-call | flops 1500000000 | bytes 9900000 | tf_op jit(solution)/shard_map/correlate/pallas_call | solution.py:310
  (84 shorter events, 21.3 us)
Async XLA Ops:
  16.4 17.1 %all-to-all-start = ((bf16[8,2,16,8,128]{4,3,2,1,0:T(8,128)(2,1)}), bf16[8,2,16,8,128]{4,3,2,1,0:T(8,128)(2,1)S(1)}, u32[]{:S(2)}, u32[]{:S(2)}) async-start(bf16[8,2,16,8,128]{4,3,2,1,0:T(8,128)(2,1)} %spectra.4), calls=%async_computation | async-start | bytes 1048576 | tf_op jit(solution)/shard_map/all_to_all | solution.py:355
  33.6 19.4 %collective-permute-start.2 = (bf16[2,16,64,128]{3,2,1,0:T(8,128)(2,1)S(1)}, bf16[2,16,64,128]{3,2,1,0:T(8,128)(2,1)S(1)}, u32[]{:S(2)}, u32[]{:S(2)}) collective-permute-start(bf16[2,16,64,128]{3,2,1,0:T(8,128)(2,1)S(1)} %copy_bitcast_fusion.refs_0_), channel_id=1, source_target_pairs={{0,6},{2,4},{4,2},{6,0},{1,7},{3,5},{5,3},{7,1},{8,14},{10,12},{12... | collective-permute-start | bytes 1572872 | tf_op jit(solution)/shard_map/ppermute | solution.py:346
  37.5 15.6 %collective-permute-start.1 = (bf16[2,16,64,128]{3,2,1,0:T(8,128)(2,1)S(1)}, bf16[2,16,64,128]{3,2,1,0:T(8,128)(2,1)S(1)}, u32[]{:S(2)}, u32[]{:S(2)}) collective-permute-start(bf16[2,16,64,128]{3,2,1,0:T(8,128)(2,1)S(1)} %copy_bitcast_fusion.refs_0_), channel_id=1, source_target_pairs={{0,2},{2,0},{4,6},{6,4},{1,3},{3,1},{5,7},{7,5},{8,10},{10,8},{12,... | collective-permute-start | bytes 1572872 | tf_op jit(solution)/shard_map/ppermute | solution.py:346
  37.5 15.6 %collective-permute-start = (bf16[2,16,64,128]{3,2,1,0:T(8,128)(2,1)S(1)}, bf16[2,16,64,128]{3,2,1,0:T(8,128)(2,1)S(1)}, u32[]{:S(2)}, u32[]{:S(2)}) collective-permute-start(bf16[2,16,64,128]{3,2,1,0:T(8,128)(2,1)S(1)} %copy_bitcast_fusion.refs_0_), channel_id=1, source_target_pairs={{0,8},{8,0},{1,9},{9,1},{2,10},{10,2},{3,11},{11,3},{4,12},{12,4},... | collective-permute-start | bytes 1572872 | tf_op jit(solution)/shard_map/ppermute | solution.py:342
  53.1 12.3 %all-to-all-start.1 = ((bf16[8,2,16,8,128]{4,3,2,1,0:T(8,128)(2,1)}), bf16[8,2,16,8,128]{4,3,2,1,0:T(8,128)(2,1)S(1)}, u32[]{:S(2)}, u32[]{:S(2)}) async-start(bf16[8,2,16,8,128]{4,3,2,1,0:T(8,128)(2,1)} %spectra.5), calls=%async_computation.1 | async-start | bytes 1048576 | tf_op jit(solution)/shard_map/all_to_all | solution.py:355
  57.6 11.3 %collective-permute-start.3 = (bf16[2,16,64,128]{3,2,1,0:T(8,128)(2,1)S(1)}, bf16[2,16,64,128]{3,2,1,0:T(8,128)(2,1)S(1)}, u32[]{:S(2)}, u32[]{:S(2)}) collective-permute-start(bf16[2,16,64,128]{3,2,1,0:T(8,128)(2,1)S(1)} %collective-permute-done.2.refs_6_), channel_id=1, source_target_pairs={{0,2},{2,0},{4,6},{6,4},{1,3},{3,1},{5,7},{7,5},{8,10},{10,8},{12,... | collective-permute-start | bytes 1572872 | tf_op jit(solution)/shard_map/ppermute | solution.py:346
  59.1 12.0 %collective-permute-start.4 = (bf16[2,16,64,128]{3,2,1,0:T(8,128)(2,1)S(1)}, bf16[2,16,64,128]{3,2,1,0:T(8,128)(2,1)S(1)}, u32[]{:S(2)}, u32[]{:S(2)}) collective-permute-start(bf16[2,16,64,128]{3,2,1,0:T(8,128)(2,1)S(1)} %collective-permute-done.refs_10_), channel_id=1, source_target_pairs={{0,6},{2,4},{4,2},{6,0},{1,7},{3,5},{5,3},{7,1},{8,14},{10,12},{12... | collective-permute-start | bytes 1572872 | tf_op jit(solution)/shard_map/ppermute | solution.py:346
  65.5 28.0 %copy-start.2 = (bf16[2,16,64,128]{3,2,1,0:T(8,128)(2,1)}, bf16[2,16,64,128]{3,2,1,0:T(8,128)(2,1)S(1)}, u32[]{:S(2)}) copy-start(bf16[2,16,64,128]{3,2,1,0:T(8,128)(2,1)S(1)} %copy_bitcast_fusion.1.refs_1_) | copy-start | bytes 1572868
  65.5 11.7 %collective-permute-start.6 = (bf16[2,16,64,128]{3,2,1,0:T(8,128)(2,1)S(1)}, bf16[2,16,64,128]{3,2,1,0:T(8,128)(2,1)S(1)}, u32[]{:S(2)}, u32[]{:S(2)}) collective-permute-start(bf16[2,16,64,128]{3,2,1,0:T(8,128)(2,1)S(1)} %copy_bitcast_fusion.1.refs_1_), channel_id=1, source_target_pairs={{0,8},{8,0},{1,9},{9,1},{2,10},{10,2},{3,11},{11,3},{4,12},{12,4},... | collective-permute-start | bytes 1572872 | tf_op jit(solution)/shard_map/ppermute | solution.py:342
  69.0 24.5 %copy-start.7 = (bf16[2,16,64,128]{3,2,1,0:T(8,128)(2,1)}, bf16[2,16,64,128]{3,2,1,0:T(8,128)(2,1)S(1)}, u32[]{:S(2)}) copy-start(bf16[2,16,64,128]{3,2,1,0:T(8,128)(2,1)S(1)} %collective-permute-done.3.refs_8_) | copy-start | bytes 1572868
  69.0 10.4 %collective-permute-start.5 = (bf16[2,16,64,128]{3,2,1,0:T(8,128)(2,1)S(1)}, bf16[2,16,64,128]{3,2,1,0:T(8,128)(2,1)S(1)}, u32[]{:S(2)}, u32[]{:S(2)}) collective-permute-start(bf16[2,16,64,128]{3,2,1,0:T(8,128)(2,1)S(1)} %copy_bitcast_fusion.1.refs_1_), channel_id=1, source_target_pairs={{0,2},{2,0},{4,6},{6,4},{1,3},{3,1},{5,7},{7,5},{8,10},{10,8},{12,... | collective-permute-start | bytes 1572872 | tf_op jit(solution)/shard_map/ppermute | solution.py:346
  71.1 11.1 %collective-permute-start.8 = (bf16[2,16,64,128]{3,2,1,0:T(8,128)(2,1)S(1)}, bf16[2,16,64,128]{3,2,1,0:T(8,128)(2,1)S(1)}, u32[]{:S(2)}, u32[]{:S(2)}) collective-permute-start(bf16[2,16,64,128]{3,2,1,0:T(8,128)(2,1)S(1)} %copy_bitcast_fusion.1.refs_1_), channel_id=1, source_target_pairs={{0,6},{2,4},{4,2},{6,0},{1,7},{3,5},{5,3},{7,1},{8,14},{10,12},{12... | collective-permute-start | bytes 1572872 | tf_op jit(solution)/shard_map/ppermute | solution.py:346
  74.0 29.7 %copy-start.20 = (s32[256]{0:T(256)S(1)}, s32[256]{0:T(256)}, u32[]{:S(2)}) copy-start(s32[256]{0:T(256)} %param.8) | copy-start | bytes 3076
  79.4 11.0 %collective-permute-start.9 = (bf16[2,16,64,128]{3,2,1,0:T(8,128)(2,1)S(1)}, bf16[2,16,64,128]{3,2,1,0:T(8,128)(2,1)S(1)}, u32[]{:S(2)}, u32[]{:S(2)}) collective-permute-start(bf16[2,16,64,128]{3,2,1,0:T(8,128)(2,1)S(1)} %collective-permute-done.5.refs_5_), channel_id=1, source_target_pairs={{0,8},{8,0},{1,9},{9,1},{2,10},{10,2},{3,11},{11,3},{4,12},{12,4},... | collective-permute-start | bytes 1572872 | tf_op jit(solution)/shard_map/ppermute | solution.py:342
  82.2 10.4 %collective-permute-start.10 = (bf16[2,16,64,128]{3,2,1,0:T(8,128)(2,1)S(1)}, bf16[2,16,64,128]{3,2,1,0:T(8,128)(2,1)S(1)}, u32[]{:S(2)}, u32[]{:S(2)}) collective-permute-start(bf16[2,16,64,128]{3,2,1,0:T(8,128)(2,1)S(1)} %collective-permute-done.5.refs_5_), channel_id=1, source_target_pairs={{0,6},{2,4},{4,2},{6,0},{1,7},{3,5},{5,3},{7,1},{8,14},{10,12},{12... | collective-permute-start | bytes 1572872 | tf_op jit(solution)/shard_map/ppermute | solution.py:346
  83.6 10.7 %collective-permute-start.11 = (bf16[2,16,64,128]{3,2,1,0:T(8,128)(2,1)S(1)}, bf16[2,16,64,128]{3,2,1,0:T(8,128)(2,1)S(1)}, u32[]{:S(2)}, u32[]{:S(2)}) collective-permute-start(bf16[2,16,64,128]{3,2,1,0:T(8,128)(2,1)S(1)} %collective-permute-done.4.refs_6_), channel_id=1, source_target_pairs={{0,2},{2,0},{4,6},{6,4},{1,3},{3,1},{5,7},{7,5},{8,10},{10,8},{12,... | collective-permute-start | bytes 1572872 | tf_op jit(solution)/shard_map/ppermute | solution.py:346
  85.3 21.7 %collective-permute-start.7 = (bf16[7,2,16,64,128]{4,3,2,1,0:T(8,128)(2,1)}, bf16[7,2,16,64,128]{4,3,2,1,0:T(8,128)(2,1)}, u32[]{:S(2)}, u32[]{:S(2)}) collective-permute-start(bf16[7,2,16,64,128]{4,3,2,1,0:T(8,128)(2,1)} %bitcast_dynamic-update-slice_fusion.6), channel_id=1, source_target_pairs={{0,1},{1,0},{2,3},{3,2},{4,5},{5,4},{6,7},{7,6},{8,9},{9,8},{10,11... | collective-permute-start | bytes 11010056 | tf_op jit(solution)/shard_map/ppermute | solution.py:351
  96.1 10.9 %collective-permute-start.12 = (bf16[6,2,16,64,128]{4,3,2,1,0:T(8,128)(2,1)}, bf16[6,2,16,64,128]{4,3,2,1,0:T(8,128)(2,1)S(1)}, u32[]{:S(2)}, u32[]{:S(2)}) collective-permute-start(bf16[6,2,16,64,128]{4,3,2,1,0:T(8,128)(2,1)} %bitcast_dynamic-update-slice_fusion), channel_id=1, source_target_pairs={{0,1},{1,0},{2,3},{3,2},{4,5},{5,4},{6,7},{7,6},{8,9},{9,8},{10,11... | collective-permute-start | bytes 9437192 | tf_op jit(solution)/shard_map/ppermute | solution.py:351
  101.5 16.5 %collective-permute-start.13 = (bf16[2,16,64,128]{3,2,1,0:T(8,128)(2,1)}, bf16[2,16,64,128]{3,2,1,0:T(8,128)(2,1)S(1)}, u32[]{:S(2)}, u32[]{:S(2)}) collective-permute-start(bf16[2,16,64,128]{3,2,1,0:T(8,128)(2,1)} %copy-done.12), channel_id=1, source_target_pairs={{0,8},{8,0},{1,9},{9,1},{2,10},{10,2},{3,11},{11,3},{4,12},{12,4},... | collective-permute-start | bytes 1572872 | tf_op jit(solution)/shard_map/ppermute | solution.py:342
  103.2 14.8 %collective-permute-start.15 = (bf16[2,16,64,128]{3,2,1,0:T(8,128)(2,1)}, bf16[2,16,64,128]{3,2,1,0:T(8,128)(2,1)S(1)}, u32[]{:S(2)}, u32[]{:S(2)}) collective-permute-start(bf16[2,16,64,128]{3,2,1,0:T(8,128)(2,1)} %copy-done.8), channel_id=1, source_target_pairs={{0,6},{2,4},{4,2},{6,0},{1,7},{3,5},{5,3},{7,1},{8,14},{10,12},{12... | collective-permute-start | bytes 1572872 | tf_op jit(solution)/shard_map/ppermute | solution.py:346
  103.7 14.2 %collective-permute-start.14 = (bf16[2,16,64,128]{3,2,1,0:T(8,128)(2,1)}, bf16[2,16,64,128]{3,2,1,0:T(8,128)(2,1)S(1)}, u32[]{:S(2)}, u32[]{:S(2)}) collective-permute-start(bf16[2,16,64,128]{3,2,1,0:T(8,128)(2,1)} %copy-done.5), channel_id=1, source_target_pairs={{0,2},{2,0},{4,6},{6,4},{1,3},{3,1},{5,7},{7,5},{8,10},{10,8},{12,... | collective-permute-start | bytes 1572872 | tf_op jit(solution)/shard_map/ppermute | solution.py:346
  118.0 2.5 %collective-permute-start.16 = (bf16[2,16,64,128]{3,2,1,0:T(8,128)(2,1)S(1)}, bf16[2,16,64,128]{3,2,1,0:T(8,128)(2,1)S(1)}, u32[]{:S(2)}, u32[]{:S(2)}) collective-permute-start(bf16[2,16,64,128]{3,2,1,0:T(8,128)(2,1)S(1)} %collective-permute-done.14.refs_2_), channel_id=1, source_target_pairs={{0,1},{1,0},{2,3},{3,2},{4,5},{5,4},{6,7},{7,6},{8,9},{9,8},{10,11... | collective-permute-start | bytes 1572872 | tf_op jit(solution)/shard_map/ppermute | solution.py:351
  119.0 2.3 %collective-permute-start.17 = (bf16[2,16,64,128]{3,2,1,0:T(8,128)(2,1)S(1)}, bf16[2,16,64,128]{3,2,1,0:T(8,128)(2,1)S(1)}, u32[]{:S(2)}, u32[]{:S(2)}) collective-permute-start(bf16[2,16,64,128]{3,2,1,0:T(8,128)(2,1)S(1)} %collective-permute-done.13.refs_8_), channel_id=1, source_target_pairs={{0,1},{1,0},{2,3},{3,2},{4,5},{5,4},{6,7},{7,6},{8,9},{9,8},{10,11... | collective-permute-start | bytes 1572872 | tf_op jit(solution)/shard_map/ppermute | solution.py:351
  119.0 3.0 %collective-permute-start.18 = (bf16[2,16,64,128]{3,2,1,0:T(8,128)(2,1)S(1)}, bf16[2,16,64,128]{3,2,1,0:T(8,128)(2,1)S(1)}, u32[]{:S(2)}, u32[]{:S(2)}) collective-permute-start(bf16[2,16,64,128]{3,2,1,0:T(8,128)(2,1)S(1)} %collective-permute-done.15.refs_11_), channel_id=1, source_target_pairs={{0,1},{1,0},{2,3},{3,2},{4,5},{5,4},{6,7},{7,6},{8,9},{9,8},{10,11... | collective-permute-start | bytes 1572872 | tf_op jit(solution)/shard_map/ppermute | solution.py:351
  (18 other events, 186.6 us)
